TPU v7x, 512 devices: a whole 4x4x16 slice. The times are simulated.
512 devices in a mesh: gx: 16 (over z), gy: 8 (over x, core), gz: 4 (over y).
Axes of the slice: x: 4, y: 4, z: 16, core: 2. Of those that a mesh axis runs over, the one named last changes fastest.
Arguments:
- residuals: float32 [8, 4, 64, 32, 512], P(None, None, 'gx', 'gy', 'gz'), may hold values from -8 to 8
- shear_rate: float32 [64, 32, 512], P('gx', 'gy', 'gz'), may hold values from 0.05 to 20
- coupling: float32 [4, 4, 64, 32, 512], P(None, None, 'gx', 'gy', 'gz'), may hold values from -0.5 to 4, as said below
Outputs:
- correction: float32 [8, 4, 64, 32, 512], P(None, None, 'gx', 'gy', 'gz')
- factor: float32 [40, 40], replicated
Inputs may be any that keep to these rules, and one draw needn't show every extreme that they name: `coupling`: diagonal entries of each block lie between 2 and 4; off-diagonal entries have magnitude at most 0.5.
All inputs are finite; a program needn't handle non-finite values.
Results may differ from a plain program's by a relative error of at most 0.0003.
Values sent between devices are 32-bit elements; how exact they have to be, the bound alone decides.
No kernel may reach another device: no remote copies, remote signals or barrier semaphores. Data moves between devices by JAX's collectives and lax.ppermute only.
A program may use at most 64 MiB of HBM per device.

v0:
```python
import jax
import jax.numpy as jnp
from jax import lax
from jax.sharding import PartitionSpec as P

POWERS = 4


VISCOSITY = 0.2
YIELD_STRESS = 1.0
REGULARIZE = 100.0
HIGHEST = lax.Precision.HIGHEST


def with_halo(block, sides, width):
    for axis, dim in sides:
        count = lax.axis_size(axis)
        forward = [(i, i + 1) for i in range(count - 1)]
        backward = [(target, source) for source, target in forward]
        low = lax.ppermute(
            lax.slice_in_dim(block, block.shape[dim] - width, None, axis=dim), axis, forward
        )
        high = lax.ppermute(lax.slice_in_dim(block, 0, width, axis=dim), axis, backward)
        block = jnp.concatenate([low, block, high], axis=dim)
    return block


def swapped(shard, axis, stride):
    return lax.ppermute(shard, axis, [(i, i ^ 1 << stride) for i in range(lax.axis_size(axis))])


def viscosity(shear_rate):
    return VISCOSITY + YIELD_STRESS * (1.0 - jnp.exp(-REGULARIZE * shear_rate)) / shear_rate


def coefficient_stack(shear_rate, coupling):
    cell_shape = shear_rate.shape
    entries = coupling.shape[0] * coupling.shape[1]
    return jnp.concatenate(
        [
            coupling.reshape((entries,) + cell_shape),
            viscosity(shear_rate)[None],
            jnp.ones((1,) + cell_shape, jnp.float32),
        ],
        axis=0,
    )


def inner_part(values_in, shift_x, shift_y, shift_z):
    size_x, size_y, size_z = values_in.shape[-3:]
    return values_in[
        ...,
        shift_x : shift_x + size_x - 2,
        shift_y : shift_y + size_y - 2,
        shift_z : shift_z + size_z - 2,
    ]


def advance(padded, coeffs):
    centre = inner_part(padded, 1, 1, 1)
    components = centre.shape[1]
    eta_all = coeffs[components * components]
    eta_mid = inner_part(eta_all, 1, 1, 1)
    inside_flag = inner_part(coeffs[components * components + 1], 1, 1, 1)
    beside = jnp.zeros_like(centre)
    kappa_sum = jnp.zeros_like(eta_mid)
    for offsets in ((0, 1, 1), (2, 1, 1), (1, 0, 1), (1, 2, 1), (1, 1, 0), (1, 1, 2)):
        face_kappa = 0.5 * (eta_mid + inner_part(eta_all, offsets[0], offsets[1], offsets[2]))
        kappa_sum = kappa_sum + face_kappa
        beside = beside + face_kappa[None, None] * inner_part(
            padded, offsets[0], offsets[1], offsets[2]
        )
    coupled = inner_part(coeffs[: components * components], 1, 1, 1)
    results = []
    for row_index in range(components):
        summed = -beside[:, row_index]
        for column_index in range(components):
            if column_index != row_index:
                summed = (
                    summed
                    + coupled[row_index * components + column_index][None] * centre[:, column_index]
                )
        denom = coupled[row_index * components + row_index] + kappa_sum + 1.0 - inside_flag
        results.append(inside_flag[None] * summed / denom[None])
    return jnp.stack(results, axis=1)


def cholesky_upper(gram_matrix):
    order = gram_matrix.shape[0]
    positions = jnp.arange(order, dtype=jnp.int32)

    def row_step(row, upper):
        column = lax.dynamic_slice_in_dim(upper, row, 1, 1)[:, 0]
        gram_row = lax.dynamic_slice_in_dim(gram_matrix, row, 1, 0)[0]
        remain = gram_row - jnp.dot(column, upper, precision=HIGHEST)
        pivot = jnp.sum(jnp.where(positions == row, remain, 0.0))
        root = jnp.sqrt(pivot)
        new_row = jnp.where(positions >= row, remain / root, 0.0)
        return lax.dynamic_update_slice_in_dim(upper, new_row[None, :], row, 0)

    return lax.fori_loop(0, order, row_step, jnp.zeros((order, order), jnp.float32))


def back_solve(upper, target):
    order = upper.shape[0]
    positions = jnp.arange(order, dtype=jnp.int32)

    def solve_step(count, solution):
        row = order - 1 - count
        upper_row = lax.dynamic_slice_in_dim(upper, row, 1, 0)[0]
        pivot = jnp.sum(jnp.where(positions == row, upper_row, 0.0))
        target_row = lax.dynamic_slice_in_dim(target, row, 1, 0)[0]
        value = (target_row - jnp.dot(upper_row, solution, precision=HIGHEST)) / pivot
        return lax.dynamic_update_slice_in_dim(solution, value[None, :], row, 0)

    return lax.fori_loop(0, order, solve_step, jnp.zeros(target.shape, jnp.float32))


def gram_schmidt(matrix):
    row_count, column_count = matrix.shape

    def column_step(column, state_pair):
        ortho_basis, upper_factor = state_pair
        vector = lax.dynamic_slice_in_dim(matrix, column, 1, 1)[:, 0]
        first_coef = jnp.dot(ortho_basis.T, vector, precision=HIGHEST)
        vector = vector - jnp.dot(ortho_basis, first_coef, precision=HIGHEST)
        second_coef = jnp.dot(ortho_basis.T, vector, precision=HIGHEST)
        vector = vector - jnp.dot(ortho_basis, second_coef, precision=HIGHEST)
        length = jnp.sqrt(jnp.sum(vector * vector))
        unit_pick = (jnp.arange(column_count) == column).astype(jnp.float32)
        ortho_basis = lax.dynamic_update_slice_in_dim(
            ortho_basis, (vector / length)[:, None], column, 1
        )
        upper_factor = lax.dynamic_update_slice_in_dim(
            upper_factor, (first_coef + second_coef + length * unit_pick)[:, None], column, 1
        )
        return (ortho_basis, upper_factor)

    initial = (
        jnp.zeros((row_count, column_count), jnp.float32),
        jnp.zeros((column_count, column_count), jnp.float32),
    )
    return lax.fori_loop(0, column_count, column_step, initial)


def small_solve(factor, rhs_count):
    target = factor[:, :rhs_count]
    hessenberg = factor[:, :-rhs_count] + factor[:, rhs_count:]
    ortho_basis, upper_factor = gram_schmidt(hessenberg)
    projected = jnp.dot(ortho_basis.T, target, precision=HIGHEST)
    return back_solve(upper_factor, projected)


def local(residuals, shear_rate, coupling):
    coeffs = coefficient_stack(shear_rate, coupling)
    krylov_basis = [residuals]
    face_coeffs = with_halo(coeffs, (("gx", 1), ("gy", 2), ("gz", 3)), 1)
    for power_step in range(POWERS):
        padded = with_halo(krylov_basis[-1], (("gx", 2), ("gy", 3), ("gz", 4)), 1)
        krylov_basis.append(advance(padded, face_coeffs))
    rhs_count = residuals.shape[0]
    stacked = jnp.stack(krylov_basis).reshape(len(krylov_basis) * rhs_count, -1)
    local_gram = jnp.dot(stacked, stacked.T, precision=HIGHEST)
    factor = cholesky_upper(local_gram)
    my_index = lax.axis_index(("gx", "gy", "gz"))
    for bit_pos in range(lax.axis_size(("gx", "gy", "gz")).bit_length() - 1):
        partner = swapped(factor, ("gx", "gy", "gz"), bit_pos)
        is_upper = my_index >> bit_pos & 1 == 1
        lower_one = jnp.where(is_upper, partner, factor)
        upper_one = jnp.where(is_upper, factor, partner)
        factor = gram_schmidt(jnp.concatenate([lower_one, upper_one], axis=0))[1]
    update = small_solve(factor, rhs_count)
    correction = jnp.dot(update.T, stacked[: rhs_count * POWERS], precision=HIGHEST)
    return (correction.reshape(residuals.shape), factor)


def solution(mesh):
    in_specs = (
        P(None, None, "gx", "gy", "gz"),
        P("gx", "gy", "gz"),
        P(None, None, "gx", "gy", "gz"),
    )
    out_specs = (P(None, None, "gx", "gy", "gz"), P())
    return jax.shard_map(local, mesh=mesh, in_specs=in_specs, out_specs=out_specs, check_vma=False)
```

profile of v0, /device:TPU:1, one launch (start us, length us, event | category | flops | bytes accessed | tf_op | source)
XLA Modules:
  0.0 1155.1 jit_solution(8906972495343865155)
XLA Ops:
  2.2 4.4 collective-permute-start
  9.0 4.2 collective-permute-start.6
  16.1 4.3 collective-permute-start.2
  20.5 3.0 collective-permute-start.3
  23.8 2.2 collective-permute-done.3
  26.3 3.2 collective-permute-start.4
  30.9 2.2 collective-permute-start.8
  33.0 2.2 collective-permute-start.9
  35.2 2.4 collective-permute-done.4
  37.6 4.1 collective-permute-done.5
  44.0 3.2 collective-permute-start.10
  50.4 3.4 collective-permute-done.11
  56.5 4.3 collective-permute-start.12
  62.1 4.9 collective-permute-done.13
  67.1 6.6 collective-permute-start.14
  73.6 1.9 collective-permute-start.15
  75.6 4.0 collective-permute-done.15
  80.7 2.9 collective-permute-start.16
  88.1 1.7 collective-permute-done.17
  89.8 1.8 copy.175
  94.0 4.9 collective-permute-start.18
  100.4 5.0 collective-permute-done.19
  105.4 4.8 collective-permute-start.20
  110.2 1.9 collective-permute-start.21
  112.1 4.0 collective-permute-done.21
  117.9 1.8 collective-permute-start.22
  122.0 1.7 pad_maximum_fusion.2
  125.9 1.8 copy.179
  129.7 4.9 collective-permute-start.24
  135.9 4.0 collective-permute-done.25
  139.9 5.1 collective-permute-start.26
  145.1 1.9 collective-permute-start.27
  147.0 1.7 pad_maximum_fusion.4
  148.7 2.3 collective-permute-done.27
  151.9 1.5 copy.180
  153.4 1.6 collective-permute-start.28
  158.4 2.8 collective-permute-done.29
  161.1 1.8 copy.183
  163.0 1.5 fusion.127
  166.1 69.0 %while.192 = (s32[]{:T(128)}, f32[40,40]{0,1:T(8,128)S(1)}, f32[40,40]{1,0:T(8,128)S(1)}, s32[]{:T(128)}, s32[]{:T(128)}) while((s32[]{:T(128)}, f32[40,40]{0,1:T(8,128)S(1)}, f32[40,40]{1,0:T(8,128)S(1)}, s32[]{:T(128)}, s32[]{:T(128)}) %tuple.404), condition=%wide.region_2.3_spmd.clone.clone, body=%wide.region_0.2_spmd.clone.clone.sunk | while | flops 19481 | bytes 24245 | solution.py:101
  235.1 1.9 collective-permute-start.30
  237.0 2.6 collective-permute-done.30
  239.7 83.7 %while.181 = (s32[]{:T(128)}, f32[80,40]{0,1:T(8,128)S(1)}, f32[40,40]{0,1:T(8,128)S(1)}, f32[80,40]{0,1:T(8,128)S(1)}, s32[]{:T(128)}, /*index=5*/s32[]{:T(128)}) while((s32[]{:T(128)}, f32[80,40]{0,1:T(8,128)S(1)}, f32[40,40]{0,1:T(8,128)S(1)}, f32[80,40]{0,1:T(8,128)S(1)}, s32[]{:T(128)}, /*index=5*/s32[]{:T(128)}) %tuple.407), condition=%wide.region_5.6_spmd, body=%wide.region_3.5_spmd.sunk | while | flops 154161 | bytes 63821 | solution.py:143
  323.4 2.8 collective-permute-start.31
  326.2 3.3 collective-permute-done.31
  329.6 83.7 %while.182 = (s32[]{:T(128)}, f32[80,40]{0,1:T(8,128)S(1)}, f32[40,40]{0,1:T(8,128)S(1)}, f32[80,40]{0,1:T(8,128)S(1)}, s32[]{:T(128)}, /*index=5*/s32[]{:T(128)}) while((s32[]{:T(128)}, f32[80,40]{0,1:T(8,128)S(1)}, f32[40,40]{0,1:T(8,128)S(1)}, f32[80,40]{0,1:T(8,128)S(1)}, s32[]{:T(128)}, /*index=5*/s32[]{:T(128)}) %tuple.410), condition=%wide.region_8.9_spmd, body=%wide.region_6.8_spmd.sunk | while | flops 154161 | bytes 63821 | solution.py:143
  413.3 2.9 collective-permute-start.32
  417.1 83.7 %while.183 = (s32[]{:T(128)}, f32[80,40]{0,1:T(8,128)S(1)}, f32[40,40]{0,1:T(8,128)S(1)}, f32[80,40]{0,1:T(8,128)S(1)}, s32[]{:T(128)}, /*index=5*/s32[]{:T(128)}) while((s32[]{:T(128)}, f32[80,40]{0,1:T(8,128)S(1)}, f32[40,40]{0,1:T(8,128)S(1)}, f32[80,40]{0,1:T(8,128)S(1)}, s32[]{:T(128)}, /*index=5*/s32[]{:T(128)}) %tuple.413), condition=%wide.region_11.12_spmd, body=%wide.region_9.11_spmd.sunk | while | flops 154161 | bytes 63821 | solution.py:143
  500.9 5.0 collective-permute-start.33
  507.2 83.7 %while.184 = (s32[]{:T(128)}, f32[80,40]{0,1:T(8,128)S(1)}, f32[40,40]{0,1:T(8,128)S(1)}, f32[80,40]{0,1:T(8,128)S(1)}, s32[]{:T(128)}, /*index=5*/s32[]{:T(128)}) while((s32[]{:T(128)}, f32[80,40]{0,1:T(8,128)S(1)}, f32[40,40]{0,1:T(8,128)S(1)}, f32[80,40]{0,1:T(8,128)S(1)}, s32[]{:T(128)}, /*index=5*/s32[]{:T(128)}) %tuple.416), condition=%wide.region_14.15_spmd, body=%wide.region_12.14_spmd.sunk | while | flops 154161 | bytes 63821 | solution.py:143
  590.9 3.7 collective-permute-start.34
  594.6 2.3 collective-permute-done.34
  597.0 83.7 %while.185 = (s32[]{:T(128)}, f32[80,40]{0,1:T(8,128)S(1)}, f32[40,40]{0,1:T(8,128)S(1)}, f32[80,40]{0,1:T(8,128)S(1)}, s32[]{:T(128)}, /*index=5*/s32[]{:T(128)}) while((s32[]{:T(128)}, f32[80,40]{0,1:T(8,128)S(1)}, f32[40,40]{0,1:T(8,128)S(1)}, f32[80,40]{0,1:T(8,128)S(1)}, s32[]{:T(128)}, /*index=5*/s32[]{:T(128)}) %tuple.419), condition=%wide.region_17.18_spmd, body=%wide.region_15.17_spmd.sunk | while | flops 154161 | bytes 63821 | solution.py:143
  680.8 3.6 collective-permute-start.35
  685.7 83.7 %while.186 = (s32[]{:T(128)}, f32[80,40]{0,1:T(8,128)S(1)}, f32[40,40]{0,1:T(8,128)S(1)}, f32[80,40]{0,1:T(8,128)S(1)}, s32[]{:T(128)}, /*index=5*/s32[]{:T(128)}) while((s32[]{:T(128)}, f32[80,40]{0,1:T(8,128)S(1)}, f32[40,40]{0,1:T(8,128)S(1)}, f32[80,40]{0,1:T(8,128)S(1)}, s32[]{:T(128)}, /*index=5*/s32[]{:T(128)}) %tuple.422), condition=%wide.region_20.21_spmd, body=%wide.region_18.20_spmd.sunk | while | flops 154161 | bytes 63821 | solution.py:143
  769.4 5.9 collective-permute-start.36
  776.6 83.7 %while.187 = (s32[]{:T(128)}, f32[80,40]{0,1:T(8,128)S(1)}, f32[40,40]{0,1:T(8,128)S(1)}, f32[80,40]{0,1:T(8,128)S(1)}, s32[]{:T(128)}, /*index=5*/s32[]{:T(128)}) while((s32[]{:T(128)}, f32[80,40]{0,1:T(8,128)S(1)}, f32[40,40]{0,1:T(8,128)S(1)}, f32[80,40]{0,1:T(8,128)S(1)}, s32[]{:T(128)}, /*index=5*/s32[]{:T(128)}) %tuple.425), condition=%wide.region_23.24_spmd, body=%wide.region_21.23_spmd.sunk | while | flops 154161 | bytes 63821 | solution.py:143
  860.3 7.2 collective-permute-start.37
  868.9 80.6 %while.188 = (s32[]{:T(128)}, f32[80,40]{0,1:T(8,128)S(1)}, f32[40,40]{0,1:T(8,128)S(1)}, f32[80,40]{0,1:T(8,128)S(1)}, s32[]{:T(128)}, /*index=5*/s32[]{:T(128)}) while((s32[]{:T(128)}, f32[80,40]{0,1:T(8,128)S(1)}, f32[40,40]{0,1:T(8,128)S(1)}, f32[80,40]{0,1:T(8,128)S(1)}, s32[]{:T(128)}, /*index=5*/s32[]{:T(128)}) %tuple.428), condition=%wide.region_26.27_spmd, body=%wide.region_24.26_spmd.sunk | while | flops 154161 | bytes 63821 | solution.py:143
  949.5 9.0 collective-permute-start.38
  959.3 3.4 collective-permute-done.38
  962.8 80.1 %while.189 = (s32[]{:T(128)}, f32[80,40]{0,1:T(8,128)S(1)}, f32[40,40]{0,1:T(8,128)S(1)}, f32[80,40]{0,1:T(8,128)S(1)}, s32[]{:T(128)}, /*index=5*/s32[]{:T(128)}) while((s32[]{:T(128)}, f32[80,40]{0,1:T(8,128)S(1)}, f32[40,40]{0,1:T(8,128)S(1)}, f32[80,40]{0,1:T(8,128)S(1)}, s32[]{:T(128)}, /*index=5*/s32[]{:T(128)}) %tuple.431), condition=%wide.region_29.30_spmd, body=%wide.region_27.29_spmd.sunk | while | flops 154161 | bytes 63821 | solution.py:143
  1043.6 63.5 %while.190 = (s32[]{:T(128)}, f32[40,32]{0,1:T(8,128)S(1)}, f32[32,32]{0,1:T(8,128)S(1)}, f32[40,32]{0,1:T(8,128)S(1)}, s32[]{:T(128)}, /*index=5*/s32[]{:T(128)}) while((s32[]{:T(128)}, f32[40,32]{0,1:T(8,128)S(1)}, f32[32,32]{0,1:T(8,128)S(1)}, f32[40,32]{0,1:T(8,128)S(1)}, s32[]{:T(128)}, /*index=5*/s32[]{:T(128)}) %tuple.434), condition=%wide.region_32.33_spmd, body=%wide.region_30.32_spmd.sunk | while | flops 61769 | bytes 34957 | solution.py:143
  1107.3 45.8 %while.191 = (s32[]{:T(128)}, f32[32,8]{1,0:T(8,128)S(1)}, f32[32,8]{1,0:T(8,128)S(1)}, f32[32,32]{1,0:T(8,128)S(1)}, s32[]{:T(128)}, /*index=5*/s32[]{:T(128)}, s32[]{:T(128)}, s32[]{:T(128)}) while((s32[]{:T(128)}, f32[32,8]{1,0:T(8,128)S(1)}, f32[32,8]{1,0:T(8,128)S(1)}, f32[32,32]{1,0:T(8,128)S(1)}, s32[]{:T(128)}, ...), condition=%wide.region_35.36_spmd.clone, body=%wide.region_33.35_spmd.clone.sunk | while | flops 3189 | bytes 18807 | solution.py:116
  (3675 shorter events, 657.1 us)
Async XLA Ops:
  0.6 15.4 %copy-start = (f32[4,4,4,4,128]{4,3,2,1,0:T(4,128)S(1)}, f32[4,4,4,4,128]{4,3,2,1,0:T(4,128)}, u32[]{:S(2)}) copy-start(f32[4,4,4,4,128]{4,3,2,1,0:T(4,128)} %param.29) | copy-start | bytes 393220
  0.6 22.9 %copy-start.1 = (f32[8,4,4,4,128]{4,3,2,1,0:T(4,128)S(1)}, f32[8,4,4,4,128]{4,3,2,1,0:T(4,128)}, u32[]{:S(2)}) copy-start(f32[8,4,4,4,128]{4,3,2,1,0:T(4,128)} %param.27) | copy-start | bytes 786436
  2.2 13.8 %collective-permute-start = (f32[18,1,4,128]{3,2,1,0:T(4,128)S(1)}, f32[18,1,4,128]{3,2,1,0:T(4,128)S(1)}, u32[]{:S(2)}, u32[]{:S(2)}) collective-permute-start(f32[18,1,4,128]{3,2,1,0:T(4,128)S(1)} %get-tuple-element.1261), channel_id=1, source_target_pairs={{0,32},{32,64},{64,96},{96,128},{128,160},{160,192},{192,224},{224... | collective-permute-start | bytes 110600 | tf_op jit(solution)/shard_map/ppermute | solution.py:20
  6.6 9.4 collective-permute-start.1
  9.0 14.5 %collective-permute-start.6 = (f32[8,4,1,4,128]{4,0,3,2,1:T(8,128)S(1)}, f32[8,4,1,4,128]{4,0,3,2,1:T(8,128)S(1)}, u32[]{:S(2)}, u32[]{:S(2)}) collective-permute-start(f32[8,4,1,4,128]{4,0,3,2,1:T(8,128)S(1)} %get-tuple-element.1249), channel_id=1, source_target_pairs={{0,32},{32,64},{64,96},{96,128},{128,160},{160,192},{192,224},{224... | collective-permute-start | bytes 196616 | tf_op jit(solution)/shard_map/ppermute | solution.py:20
  13.2 10.5 collective-permute-start.7
  16.1 7.6 collective-permute-start.2
  20.5 5.5 collective-permute-start.3
  26.3 11.3 collective-permute-start.4
  29.5 12.2 %collective-permute-start.5 = (f32[18,6,6,1]{3,2,1,0:T(8,128)S(1)}, f32[18,6,6,1]{3,2,1,0:T(8,128)S(1)}, u32[]{:S(2)}, u32[]{:S(2)}) collective-permute-start(f32[18,6,6,1]{3,2,1,0:T(8,128)S(1)} %get-tuple-element.1213), channel_id=1, source_target_pairs={{1,0},{2,1},{3,2},{5,4},{6,5},{7,6},{9,8},{10,9},{11,10},{13,12},{... | collective-permute-start | bytes 7784 | tf_op jit(solution)/shard_map/ppermute | solution.py:23
  30.9 11.9 %collective-permute-start.8 = (f32[8,4,6,1,128]{4,0,3,2,1:T(8,128)S(1)}, f32[8,4,6,1,128]{4,0,3,2,1:T(8,128)S(1)}, u32[]{:S(2)}, u32[]{:S(2)}) collective-permute-start(f32[8,4,6,1,128]{4,0,3,2,1:T(8,128)S(1)} %get-tuple-element.1232), channel_id=1, source_target_pairs={{0,4},{4,8},{8,12},{12,16},{16,20},{20,24},{24,28},{1,5},{5,9},{9,... | collective-permute-start | bytes 294920 | tf_op jit(solution)/shard_map/ppermute | solution.py:20
  33.0 9.8 collective-permute-start.9
  42.7 12.0 %copy-start.51 = (f32[4,4,128]{2,1,0:T(4,128)}, f32[4,4,128]{2,1,0:T(4,128)S(1)}, u32[]{:S(2)}) copy-start(f32[4,4,128]{2,1,0:T(4,128)S(1)} %get-tuple-element.1170) | copy-start | bytes 24580
  42.7 12.0 %copy-start.52 = (f32[4,4,128]{2,1,0:T(4,128)}, f32[4,4,128]{2,1,0:T(4,128)S(1)}, u32[]{:S(2)}) copy-start(f32[4,4,128]{2,1,0:T(4,128)S(1)} %get-tuple-element.1171) | copy-start | bytes 24580
  42.7 12.0 %copy-start.53 = (f32[4,4,128]{2,1,0:T(4,128)}, f32[4,4,128]{2,1,0:T(4,128)S(1)}, u32[]{:S(2)}) copy-start(f32[4,4,128]{2,1,0:T(4,128)S(1)} %get-tuple-element.1172) | copy-start | bytes 24580
  42.8 12.0 %copy-start.54 = (f32[4,4,128]{2,1,0:T(4,128)}, f32[4,4,128]{2,1,0:T(4,128)S(1)}, u32[]{:S(2)}) copy-start(f32[4,4,128]{2,1,0:T(4,128)S(1)} %get-tuple-element.1173) | copy-start | bytes 24580
  42.8 12.0 %copy-start.55 = (f32[4,4,128]{2,1,0:T(4,128)}, f32[4,4,128]{2,1,0:T(4,128)S(1)}, u32[]{:S(2)}) copy-start(f32[4,4,128]{2,1,0:T(4,128)S(1)} %get-tuple-element.1174) | copy-start | bytes 24580
  42.8 12.0 %copy-start.56 = (f32[4,4,128]{2,1,0:T(4,128)}, f32[4,4,128]{2,1,0:T(4,128)S(1)}, u32[]{:S(2)}) copy-start(f32[4,4,128]{2,1,0:T(4,128)S(1)} %get-tuple-element.1175) | copy-start | bytes 24580
  42.8 12.8 %copy-start.47 = (f32[4,4,128]{2,1,0:T(4,128)}, f32[4,4,128]{2,1,0:T(4,128)S(1)}, u32[]{:S(2)}) copy-start(f32[4,4,128]{2,1,0:T(4,128)S(1)} %get-tuple-element.1168) | copy-start | bytes 24580
  44.0 5.5 collective-permute-start.10
  48.1 5.7 collective-permute-start.11
  49.5 5.7 copy-start.61
  49.5 5.7 copy-start.65
  49.5 6.1 copy-start.57
  56.5 5.6 collective-permute-start.12
  60.8 6.2 collective-permute-start.13
  67.1 8.5 collective-permute-start.14
  73.6 5.9 collective-permute-start.15
  80.7 6.5 collective-permute-start.16
  84.6 5.2 collective-permute-start.17
  94.0 6.3 collective-permute-start.18
  98.9 6.5 collective-permute-start.19
  100.3 15.8 %copy-start.4 = (f32[8,4,1,4,128]{4,0,3,2,1:T(8,128)}, f32[8,4,1,4,128]{4,0,3,2,1:T(8,128)S(1)}, u32[]{:S(2)}) copy-start(f32[8,4,1,4,128]{4,0,3,2,1:T(8,128)S(1)} %collective-permute-done.18) | copy-start | bytes 196612
  105.4 10.7 copy-start.6
  105.4 6.7 collective-permute-start.20
  110.2 5.9 collective-permute-start.21
  117.9 5.7 collective-permute-start.22
  120.7 5.2 collective-permute-start.23
  123.7 4.0 copy-start.5
  123.7 4.0 copy-start.7
  129.7 6.2 collective-permute-start.24
  134.5 5.3 collective-permute-start.25
  139.9 8.8 collective-permute-start.26
  145.1 5.9 collective-permute-start.27
  153.4 4.0 collective-permute-start.28
  155.9 5.2 collective-permute-start.29
  163.0 1.7 copy-start.12
  163.0 1.7 copy-start.15
  163.0 1.7 copy-start.18
  163.0 1.7 copy-start.21
  163.0 1.7 copy-start.24
  163.0 1.7 copy-start.50
  163.0 1.7 copy-start.60
  235.1 4.5 collective-permute-start.30
  323.4 6.0 collective-permute-start.31
  413.3 3.7 collective-permute-start.32
  500.9 6.2 collective-permute-start.33
  590.9 6.0 collective-permute-start.34
  680.8 4.8 collective-permute-start.35
  685.7 272.8 %copy-start.2 = (f32[1,8,4,4,4,128]{5,1,4,3,2,0:T(8,128)S(1)}, f32[1,8,4,4,4,128]{5,1,4,3,2,0:T(8,128)}, u32[]{:S(2)}) copy-start(f32[1,8,4,4,4,128]{5,1,4,3,2,0:T(8,128)} %get-tuple-element.1240) | copy-start | bytes 786436
  685.7 272.8 %copy-start.3 = (f32[1,8,4,4,4,128]{5,1,4,3,2,0:T(8,128)S(1)}, f32[1,8,4,4,4,128]{5,1,4,3,2,0:T(8,128)}, u32[]{:S(2)}) copy-start(f32[1,8,4,4,4,128]{5,1,4,3,2,0:T(8,128)} %get-tuple-element.1242) | copy-start | bytes 786436
  769.4 7.1 collective-permute-start.36
  860.3 8.4 collective-permute-start.37
  949.5 13.2 %collective-permute-start.38 = (f32[40,40]{0,1:T(8,128)S(1)}, f32[40,40]{0,1:T(8,128)S(1)}, u32[]{:S(2)}, u32[]{:S(2)}) collective-permute-start(f32[40,40]{0,1:T(8,128)S(1)} %get-tuple-element.1015), channel_id=1, source_target_pairs={{0,256},{1,257},{2,258},{3,259},{4,260},{5,261},{6,262},{7,263},{8... | collective-permute-start | bytes 19208 | tf_op jit(solution)/shard_map/ppermute | solution.py:29
  (44 other events, 59.7 us)
where the time goes:
time: 1170 us; the launch traced here: 1160 us
  matrix products  543 us (46%)
  loops' own time  320 us (27%)
  starting transfers between devices  124 us (11%)
  local copies, waits for them, and re-layouts  66.4 us (6%)
  waiting for transfers between devices  59.3 us (5%)
  other arithmetic  39.1 us (3%)
    dot_general x392, matrix products, column_step(): vector = vector - jnp.dot(ortho_basis, second_coef, precision=HIGHEST)  318 us
    another operation x10, loops' own time, gram_schmidt(): return lax.fori_loop(0, column_count, column_step, initial)  291 us
    ppermute x15, starting transfers between devices, with_halo(): lax.ppermute(lax.slice_in_dim(block, block.shape[dim] - width, None, axis...  58.2 us
    dot_general x392, matrix products, column_step(): second_coef = jnp.dot(ortho_basis.T, vector, precision=HIGHEST)  58.1 us
    dot_general x392, matrix products, column_step(): vector = vector - jnp.dot(ortho_basis, first_coef, precision=HIGHEST)  57.6 us
    dot_general x392, matrix products, column_step(): first_coef = jnp.dot(ortho_basis.T, vector, precision=HIGHEST)  52.1 us
    ppermute x9, starting transfers between devices, swapped(): lax.ppermute(shard, axis, [(i, i ^ 1 << stride) for i in range(lax.axis_s...  42 us
    ppermute x15, waiting for transfers between devices, with_halo(): lax.ppermute(lax.slice_in_dim(block, 0, width, axis=dim), axis, backward)  39.7 us
  transfers between devices with their start and end apart: 39, of which 22 were waited for; matrix products, arithmetic and copies ran while one was open for 1% of the time, Pallas kernels for 0%

commit v1 on v0

v1 whole, which is shorter than its diff:
```python
import jax
import jax.numpy as jnp
from jax import lax
from jax.experimental import pallas as pl
from jax.experimental.pallas import tpu as pltpu
from jax.sharding import PartitionSpec as P

POWERS = 4
RHS = 8
COMP = 4
BX = 4
BY = 4
LANES = 128
COLS = BX * BY
GRID = BX + 2 * POWERS
HIGHEST = lax.Precision.HIGHEST
VMEM = pl.BlockSpec(memory_space=pltpu.VMEM)

FIELD_ROWS = COMP * COLS * RHS
COUPLE_AT = FIELD_ROWS
ETA_AT = COUPLE_AT + COMP * COMP * COLS
MAIN_ROWS = ETA_AT + COLS
GHOST_ROWS = COMP * RHS + 24
BLOCK_ROWS = MAIN_ROWS + GHOST_ROWS

NEAR = [(1, 1), (1, 2), (2, 1)]
FAR = [(1, 3), (2, 2), (3, 1)]
CORNER = [(side, a, b) for a, b in NEAR + FAR for side in (0, 1)]
NEAR_COUNT = 2 * len(NEAR)
C_COUPLE_AT = len(CORNER) * COMP * RHS
C_ETA_AT = C_COUPLE_AT + NEAR_COUNT * 16
C_GHOST_AT = C_ETA_AT + 16
CORNER_ROWS = C_GHOST_AT + 2 * GHOST_ROWS


def lane_index():
    return lax.broadcasted_iota(jnp.int32, (RHS, LANES), 1)


def pack_kernel(res_ref, shear_ref, couple_ref, main_ref, low_ref, high_ref):
    lane = lane_index()
    shear = shear_ref[...]
    eta = 0.2 + (1.0 - jnp.exp(-100.0 * shear)) / shear
    main_ref[ETA_AT:MAIN_ROWS, :] = eta
    main_ref[COUPLE_AT:ETA_AT, :] = couple_ref[...]

    def pack(group, load):
        low = jnp.zeros((RHS, LANES), jnp.float32)
        high = jnp.zeros((RHS, LANES), jnp.float32)
        for col in range(COLS):
            turned = pltpu.roll(load(col), (8 * col + 4) % LANES, 1)
            here = lane // 4
            high = jnp.where(here == 2 * col, turned, high)
            low = jnp.where(here == 2 * col + 1, turned, low)
        low_ref[group * 8 : group * 8 + 8, :] = low
        high_ref[group * 8 : group * 8 + 8, :] = high

    for comp in range(COMP):

        def load_field(col):
            place = comp * COLS + col
            value = res_ref[pl.ds(place, RHS, stride=COMP * COLS), :]
            main_ref[place * RHS : place * RHS + RHS, :] = value
            return value

        pack(comp, load_field)
    for half in range(2):
        pack(
            COMP + half,
            lambda col: couple_ref[pl.ds(half * 8 * COLS + col, 8, stride=COLS), :],
        )
    pack(
        COMP + 2,
        lambda col: jnp.broadcast_to(eta[col : col + 1, :], (RHS, LANES)),
    )


def pack(residuals, shear_rate, coupling):
    return pl.pallas_call(
        pack_kernel,
        out_shape=(
            jax.ShapeDtypeStruct((MAIN_ROWS, LANES), jnp.float32),
            jax.ShapeDtypeStruct((GHOST_ROWS, LANES), jnp.float32),
            jax.ShapeDtypeStruct((GHOST_ROWS, LANES), jnp.float32),
        ),
        in_specs=[VMEM] * 3,
        out_specs=(VMEM,) * 3,
        compiler_params=pltpu.CompilerParams(vmem_limit_bytes=4 * 2**20),
    )(
        residuals.reshape(RHS * COMP * COLS, LANES),
        shear_rate.reshape(COLS, LANES),
        coupling.reshape(COMP * COMP * COLS, LANES),
    )


def corner_kernel(left_ref, right_ref, down_ref, up_ref):
    for out_ref, top in ((down_ref, False), (up_ref, True)):
        for place, (side, a, b) in enumerate(CORNER):
            src = right_ref if side else left_ref
            x = a - 1 if side else BX - a
            y = BY - b if top else b - 1
            col = x * BY + y
            for comp in range(COMP):
                start = (comp * COLS + col) * RHS
                row = (place * COMP + comp) * RHS
                out_ref[row : row + RHS, :] = src[start : start + RHS, :]
            if place < NEAR_COUNT:
                for half in range(2):
                    row = C_COUPLE_AT + place * 16 + half * 8
                    out_ref[row : row + 8, :] = src[
                        pl.ds(COUPLE_AT + half * 8 * COLS + col, 8, stride=COLS), :
                    ]
            out_ref[C_ETA_AT + place : C_ETA_AT + place + 1, :] = src[
                ETA_AT + col : ETA_AT + col + 1, :
            ]
        out_ref[C_ETA_AT + len(CORNER) : C_GHOST_AT, :] = jnp.zeros(
            (16 - len(CORNER), LANES), jnp.float32
        )
        out_ref[C_GHOST_AT : C_GHOST_AT + GHOST_ROWS, :] = left_ref[MAIN_ROWS:BLOCK_ROWS, :]
        out_ref[C_GHOST_AT + GHOST_ROWS : CORNER_ROWS, :] = right_ref[MAIN_ROWS:BLOCK_ROWS, :]


def corners(left, right):
    return pl.pallas_call(
        corner_kernel,
        out_shape=(jax.ShapeDtypeStruct((CORNER_ROWS, LANES), jnp.float32),) * 2,
        in_specs=[VMEM] * 2,
        out_specs=(VMEM,) * 2,
        compiler_params=pltpu.CompilerParams(vmem_limit_bytes=4 * 2**20),
    )(left, right)


def distance(place):
    return max(POWERS - place, 0, place - (POWERS + BX - 1))


def powers_kernel(
    own_ref, left_ref, right_ref, front_ref, back_ref, low_ref, high_ref,
    basis_ref, gram_ref,
    main, ghost, coef, coef_ghost, face, face_ghost, square,
):
    lane = lane_index()
    first, last = lane == 0, lane == LANES - 1

    def slot(x, y):
        return x * GRID + y

    def place_column(src, x, y, field_at, couple_at, couple_stride, eta_at, ghost_at, col):
        reach = distance(x) + distance(y)
        at = slot(x, y)
        for comp in range(COMP):
            main[0, at * COMP + comp] = src[field_at[comp] : field_at[comp] + RHS, :]
        coef[at, 16:24, :] = jnp.broadcast_to(src[eta_at : eta_at + 1, :], (8, LANES))
        if reach >= POWERS:
            return
        for half in range(2):
            start = couple_at + half * 8 * couple_stride
            coef[at, half * 8 : half * 8 + 8, :] = (
                src[pl.ds(start, 8, stride=couple_stride), :]
                if couple_stride > 1
                else src[start : start + 8, :]
            )
        shift = (-8 * col - 4) % LANES
        for comp in range(COMP):
            row = ghost_at + comp * RHS
            ghost[0, at * COMP + comp] = pltpu.roll(src[row : row + RHS, :], shift, 1)
        for part in range(3):
            row = ghost_at + COMP * RHS + part * 8
            coef_ghost[at, part * 8 : part * 8 + 8, :] = pltpu.roll(
                src[row : row + 8, :], shift, 1
            )

    for src, off_x, off_y in (
        (own_ref, 0, 0), (left_ref, -1, 0), (right_ref, 1, 0), (front_ref, 0, -1), (back_ref, 0, 1)
    ):
        for x in range(BX):
            for y in range(BY):
                col = x * BY + y
                place_column(
                    src, POWERS + off_x * BX + x, POWERS + off_y * BY + y,
                    [(comp * COLS + col) * RHS for comp in range(COMP)],
                    COUPLE_AT + col, COLS, ETA_AT + col, MAIN_ROWS, col,
                )
    for src, top in ((low_ref, True), (high_ref, False)):
        for place, (side, a, b) in enumerate(CORNER):
            x = POWERS + BX - 1 + a if side else POWERS - a
            y = POWERS - b if top else POWERS + BY - 1 + b
            col = (a - 1 if side else BX - a) * BY + (BY - b if top else b - 1)
            at = slot(x, y)
            for comp in range(COMP):
                row = (place * COMP + comp) * RHS
                main[0, at * COMP + comp] = src[row : row + RHS, :]
            coef[at, 16:24, :] = jnp.broadcast_to(
                src[C_ETA_AT + place : C_ETA_AT + place + 1, :], (8, LANES)
            )
            if place < NEAR_COUNT:
                for half in range(2):
                    row = C_COUPLE_AT + place * 16 + half * 8
                    coef[at, half * 8 : half * 8 + 8, :] = src[row : row + 8, :]
                shift = (-8 * col - 4) % LANES
                base = C_GHOST_AT + side * GHOST_ROWS
                for comp in range(COMP):
                    row = base + comp * RHS
                    ghost[0, at * COMP + comp] = pltpu.roll(src[row : row + RHS, :], shift, 1)
                for part in range(3):
                    row = base + COMP * RHS + part * 8
                    coef_ghost[at, part * 8 : part * 8 + 8, :] = pltpu.roll(
                        src[row : row + 8, :], shift, 1
                    )

    def over_columns(reach, body):
        for off in range(reach + 1):
            ys = range(POWERS - (reach - off), POWERS + BY + reach - off)
            if off == 0:
                xs, count = (lambda i: POWERS + i), BX
            else:
                xs, count = (lambda i, off=off: POWERS - off + i * (BX - 1 + 2 * off)), 2

            def step(i, carry, ys=ys, xs=xs, off=off):
                x = xs(i)
                for y in ys:
                    body(x, y, off + distance(y))
                return carry

            lax.fori_loop(0, count, step, 0)

    def shifted(value, other):
        up, down = pltpu.roll(value, LANES - 1, 1), pltpu.roll(value, 1, 1)
        other_up, other_down = pltpu.roll(other, LANES - 1, 1), pltpu.roll(other, 1, 1)
        return (
            jnp.where(last, other_up, up), jnp.where(first, other_down, down),
            jnp.where(last, up, other_up), jnp.where(first, down, other_down),
        )

    def faces(table, out, x, y, at, eta, up, down):
        around = [
            table[slot(x - 1, y), 16:24, :], table[slot(x + 1, y), 16:24, :],
            table[slot(x, y - 1), 16:24, :], table[slot(x, y + 1), 16:24, :],
            down, up,
        ]
        total = jnp.zeros_like(eta)
        for index, beside in enumerate(around):
            kappa = 0.5 * (eta + beside)
            total = total + kappa
            out[at * 10 + index] = -kappa
        for comp in range(COMP):
            diagonal = jnp.broadcast_to(
                table[at, 5 * comp : 5 * comp + 1, :], (RHS, LANES)
            )
            out[at * 10 + 6 + comp] = jnp.where(eta > 0.0, 1.0 / (diagonal + total), 0.0)

    def prepare(x, y, reach):
        at = slot(x, y)
        eta, eta_ghost = coef[at, 16:24, :], coef_ghost[at, 16:24, :]
        up, down, ghost_up, ghost_down = shifted(eta, eta_ghost)
        faces(coef, face, x, y, at, eta, up, down)
        if reach < POWERS - 1:
            faces(coef_ghost, face_ghost, x, y, at, eta_ghost, ghost_up, ghost_down)

    over_columns(POWERS - 1, prepare)

    def apply(field, table, faces_of, at, x, y, source, centre, up, down):
        kappa = [faces_of[at * 10 + index] for index in range(6)]
        entry = {}
        for row in range(COMP):
            for col in range(COMP):
                if row != col:
                    e = row * COMP + col
                    entry[row, col] = jnp.broadcast_to(table[at, e : e + 1, :], (RHS, LANES))
        results = []
        for comp in range(COMP):
            beside = [
                field[source, slot(x - 1, y) * COMP + comp],
                field[source, slot(x + 1, y) * COMP + comp],
                field[source, slot(x, y - 1) * COMP + comp],
                field[source, slot(x, y + 1) * COMP + comp],
                down[comp],
                up[comp],
            ]
            terms = [k * v for k, v in zip(kappa, beside)]
            terms += [entry[comp, d] * centre[d] for d in range(COMP) if d != comp]
            while len(terms) > 1:
                terms = [
                    terms[i] + terms[i + 1] if i + 1 < len(terms) else terms[i]
                    for i in range(0, len(terms), 2)
                ]
            results.append(terms[0] * faces_of[at * 10 + 6 + comp])
        return results

    for power in range(1, POWERS + 1):
        limit = POWERS - power
        source, target = (power - 1) % 2, power % 2

        def advance(x, y, reach, limit=limit, source=source, target=target, power=power):
            at = slot(x, y)
            centre = [main[source, at * COMP + comp] for comp in range(COMP)]
            outer = [ghost[source, at * COMP + comp] for comp in range(COMP)]
            moved = [shifted(c, o) for c, o in zip(centre, outer)]
            results = apply(
                main, coef, face, at, x, y, source, centre,
                [m[0] for m in moved], [m[1] for m in moved],
            )
            for comp in range(COMP):
                main[target, at * COMP + comp] = results[comp]
            if reach == 0:
                results_at = (x - POWERS) * BY + (y - POWERS)
            if reach < limit:
                outside = apply(
                    ghost, coef_ghost, face_ghost, at, x, y, source, outer,
                    [m[2] for m in moved], [m[3] for m in moved],
                )
                for comp in range(COMP):
                    ghost[target, at * COMP + comp] = outside[comp]

        over_columns(limit, advance)
        for comp in range(COMP):
            for x in range(BX):
                for y in range(BY):
                    tile = comp * COLS + x * BY + y
                    at = slot(POWERS + x, POWERS + y)
                    if power == 1:
                        basis_ref[tile, 0:RHS, :] = main[0, at * COMP + comp]
                    basis_ref[tile, power * RHS : power * RHS + RHS, :] = main[
                        target, at * COMP + comp
                    ]

    order = (POWERS + 1) * RHS
    total = jnp.zeros((order, order), jnp.float32)
    for tile in range(0, COMP * COLS, 2):
        both = jnp.concatenate([basis_ref[tile], basis_ref[tile + 1]], axis=1)
        total = total + lax.dot_general(
            both, both, (((1,), (1,)), ((), ())),
            precision=HIGHEST, preferred_element_type=jnp.float32,
        )
    square[...] = jnp.zeros_like(square)
    square[:, 0:order] = total
    packed = jnp.zeros((RHS, LANES), jnp.float32)
    start = 0
    for block in range(POWERS + 1):
        width = order - block * RHS
        value = pltpu.roll(
            square[block * RHS : block * RHS + RHS, :], (start - block * RHS) % LANES, 1
        )
        packed = jnp.where((lane >= start) & (lane < start + width), value, packed)
        start += width
    gram_ref[...] = packed


def powers(own, left, right, front, back, low, high):
    count = GRID * GRID
    return pl.pallas_call(
        powers_kernel,
        out_shape=(
            jax.ShapeDtypeStruct((COMP * COLS, (POWERS + 1) * RHS, LANES), jnp.float32),
            jax.ShapeDtypeStruct((RHS, LANES), jnp.float32),
        ),
        in_specs=[VMEM] * 7,
        out_specs=(VMEM,) * 2,
        scratch_shapes=[
            pltpu.VMEM((2, count * COMP, RHS, LANES), jnp.float32),
            pltpu.VMEM((2, count * COMP, RHS, LANES), jnp.float32),
            pltpu.VMEM((count, 24, LANES), jnp.float32),
            pltpu.VMEM((count, 24, LANES), jnp.float32),
            pltpu.VMEM((count * 10, RHS, LANES), jnp.float32),
            pltpu.VMEM((count * 10, RHS, LANES), jnp.float32),
            pltpu.VMEM(((POWERS + 1) * RHS, LANES), jnp.float32),
        ],
        compiler_params=pltpu.CompilerParams(vmem_limit_bytes=48 * 2**20),
    )(own, left, right, front, back, low, high)


def finish_kernel(gram_ref, basis_ref, out_ref, factor_ref, square, upper):
    lane = lane_index()
    order = (POWERS + 1) * RHS
    parts = [gram_ref[i] for i in range(gram_ref.shape[0])]
    while len(parts) > 1:
        parts = [
            parts[i] + parts[i + 1] if i + 1 < len(parts) else parts[i]
            for i in range(0, len(parts), 2)
        ]
    packed = parts[0]
    square[...] = jnp.zeros_like(square)
    start = 0
    for block in range(POWERS + 1):
        width = order - block * RHS
        value = pltpu.roll(packed, (block * RHS - start) % LANES, 1)
        keep = (lane >= block * RHS) & (lane < order)
        square[block * RHS : block * RHS + RHS, :] = jnp.where(keep, value, 0.0)
        start += width
    half = square[...]
    other = half.T
    gram = []
    for block in range(POWERS + 1):
        rows = slice(block * RHS, block * RHS + RHS)
        gram.append(jnp.where(lane < block * RHS, other[rows, :], half[rows, :]))
    summed = [tile + pltpu.roll(tile, LANES - RHS, 1) for tile in gram]
    normal = [summed[i] + summed[i + 1] for i in range(POWERS)] + [summed[0]]

    upper[...] = jnp.zeros_like(upper)
    for step in range(order):
        tile, row = step // RHS, step % RHS
        pick = gram[tile][row : row + 1, :]
        pivot = pick[:, step : step + 1]
        inverse = 1.0 / pivot
        upper[step : step + 1, :] = jnp.where(
            lane[0:1, :] >= step, pick * lax.rsqrt(pivot), 0.0
        )
        scaled = pick * inverse
        for i in range(tile, POWERS + 1):
            gram[i] = gram[i] - gram[i][:, step : step + 1] * scaled
        if step < POWERS * RHS:
            pick = normal[tile][row : row + 1, :]
            inverse = 1.0 / pick[:, step : step + 1]
            scaled = jnp.where(lane[0:1, :] == step, -inverse, pick * inverse)
            for i in range(tile, POWERS + 1):
                kept = jnp.where(lane == step, 0.0, normal[i])
                normal[i] = kept - normal[i][:, step : step + 1] * scaled
    factor_ref[...] = upper[0:order, 0:order]
    answer = normal[POWERS]
    weights = [
        jnp.broadcast_to(answer[:, i : i + 1], (RHS, LANES)) for i in range(POWERS * RHS)
    ]

    def combine(tile, carry):
        sums = [None] * 4
        for i in range(POWERS * RHS):
            term = weights[i] * jnp.broadcast_to(basis_ref[tile, i : i + 1, :], (RHS, LANES))
            sums[i % 4] = term if sums[i % 4] is None else sums[i % 4] + term
        out_ref[pl.ds(tile, RHS, stride=COMP * COLS), :] = (sums[0] + sums[1]) + (
            sums[2] + sums[3]
        )
        return carry

    lax.fori_loop(0, COMP * COLS, combine, 0)


def finish(gram, basis):
    order = (POWERS + 1) * RHS
    return pl.pallas_call(
        finish_kernel,
        out_shape=(
            jax.ShapeDtypeStruct((RHS * COMP * COLS, LANES), jnp.float32),
            jax.ShapeDtypeStruct((order, order), jnp.float32),
        ),
        in_specs=[VMEM] * 2,
        out_specs=(VMEM,) * 2,
        scratch_shapes=[
            pltpu.VMEM((LANES, LANES), jnp.float32),
            pltpu.VMEM((order, LANES), jnp.float32),
        ],
        compiler_params=pltpu.CompilerParams(vmem_limit_bytes=6 * 2**20),
    )(gram, basis)


def moved(block, axis, step):
    count = lax.axis_size(axis)
    pairs = [(i, i + step) for i in range(count) if 0 <= i + step < count]
    return lax.ppermute(block, axis, pairs)


def gathered(tile, axes):
    count = lax.axis_size(axes)
    return lax.all_to_all(jnp.broadcast_to(tile[None], (count,) + tile.shape), axes, 0, 0)


def local(residuals, shear_rate, coupling):
    block, low, high = pack(residuals, shear_rate, coupling)
    ghosts = moved(high, "gz", 1) + moved(low, "gz", -1)
    own = jnp.concatenate([block, ghosts], axis=0)
    left, right = moved(own, "gx", 1), moved(own, "gx", -1)
    front, back = moved(own, "gy", 1), moved(own, "gy", -1)
    down, up = corners(left, right)
    low_corner, high_corner = moved(up, "gy", 1), moved(down, "gy", -1)
    basis, gram = powers(own, left, right, front, back, low_corner, high_corner)
    gram = jnp.sum(gathered(gram, ("gy", "gz")), axis=0)
    correction, factor = finish(gathered(gram, "gx"), basis)
    return correction.reshape(residuals.shape), factor


def solution(mesh):
    in_specs = (
        P(None, None, "gx", "gy", "gz"),
        P("gx", "gy", "gz"),
        P(None, None, "gx", "gy", "gz"),
    )
    out_specs = (P(None, None, "gx", "gy", "gz"), P())
    return jax.shard_map(local, mesh=mesh, in_specs=in_specs, out_specs=out_specs, check_vma=False)
```

time: 1170 us -> 95.2 us (0.08); the launches traced: 1160 us -> 94.8 us
  matrix products: 543 us -> 0 us
  loops' own time: 320 us -> 0 us
  starting transfers between devices: 124 us -> 25.8 us
  local copies, waits for them, and re-layouts: 66.4 us -> 2.57 us
  waiting for transfers between devices: 59.3 us -> 9.59 us
  blocking collectives: 0 us -> 42.1 us
  other arithmetic: 39.1 us -> 0.07 us
  Pallas kernels: 0 us -> 14 us
    dot_general x1643 -> x0, matrix products: 543 us -> none  [the longest x392 318 us: column_step(): vector = vector - jnp.dot(ortho_basis, second_coef, precision=HIGHEST)]
    another operation x12 -> x0, loops' own time: 320 us -> none  [the longest x10 291 us: gram_schmidt(): return lax.fori_loop(0, column_count, column_step, initial)]
    ppermute x39 -> x8, starting transfers between devices: 124 us -> 25.8 us  [moved(): return lax.ppermute(block, axis, pairs)]
    ppermute x39 -> x8, waiting for transfers between devices: 59.3 us -> 9.59 us  [moved(): return lax.ppermute(block, axis, pairs)]
    all_to_all x0 -> x2, blocking collectives: none -> 42.1 us  [gathered(): lax.all_to_all(jnp.broadcast_to(tile[None], (count,) + tile.shape), axes,...]
    dynamic_update_slice x856 -> x0, local copies, waits for them, and re-layouts: 36.7 us -> none  [the longest x392 14.9 us: column_step(): lax.dynamic_update_slice_in_dim(upper_factor, (first_coef + second_coef +...]
    reduce_sum x32 -> x1, other arithmetic: 19.4 us -> 0.04 us  [local(): gram = jnp.sum(gathered(gram, ('gy', 'gz')), axis=0)]
    pallas_call x0 -> x4, Pallas kernels: none -> 14 us  [the longest x1 8.46 us: powers(): pl.pallas_call(powers_kernel, out_shape=(jax.ShapeDtypeStruct((COMP * COL...]
  transfers between devices with their start and end apart: 39 -> 8, of which waited for: 22 -> 3; matrix products, arithmetic and copies ran while one was open for 1% -> 0% of each run, Pallas kernels for 0% -> 0%
where the time goes in v1:
time: 95.2 us; the launch traced here: 94.8 us
  blocking collectives  42.1 us (44%)
  starting transfers between devices  25.8 us (27%)
  Pallas kernels  14 us (15%)
  waiting for transfers between devices  9.59 us (10%)
  local copies, waits for them, and re-layouts  2.57 us (3%)
    all_to_all x2, blocking collectives, gathered(): lax.all_to_all(jnp.broadcast_to(tile[None], (count,) + tile.shape), axes,...  42.1 us
    ppermute x8, starting transfers between devices, moved(): return lax.ppermute(block, axis, pairs)  25.8 us
    ppermute x8, waiting for transfers between devices, moved(): return lax.ppermute(block, axis, pairs)  9.59 us
    pallas_call x1, Pallas kernels, powers(): pl.pallas_call(powers_kernel, out_shape=(jax.ShapeDtypeStruct((COMP * COL...  8.46 us
    pallas_call x1, Pallas kernels, finish(): pl.pallas_call(finish_kernel, out_shape=(jax.ShapeDtypeStruct((RHS * COMP...  5.15 us
    unnamed x6, local copies, waits for them, and re-layouts  2.54 us
  transfers between devices with their start and end apart: 8, of which 3 were waited for; matrix products, arithmetic and copies ran while one was open for 0% of the time, Pallas kernels for 0%

profile of v1, /device:TPU:1, one launch (start us, length us, event | category | flops | bytes accessed | tf_op | source)
XLA Modules:
  0.0 94.8 jit_solution(10155154233146151719)
XLA Ops:
  0.6 0.0 copy-start
  0.6 0.9 copy-done
  1.6 0.0 copy-start.1
  1.6 0.9 copy-done.1
  2.5 0.0 copy-start.2
  2.5 0.7 copy-done.2
  3.2 0.3 shard_map.50
  3.5 4.0 %collective-permute-start = (f32[56,128]{1,0:T(8,128)S(1)}, f32[56,128]{1,0:T(8,128)S(1)}, u32[]{:S(2)}, u32[]{:S(2)}) collective-permute-start(f32[56,128]{1,0:T(8,128)S(1)} %get-tuple-element.12), channel_id=1, source_target_pairs={{0,1},{1,2},{2,3},{4,5},{5,6},{6,7},{8,9},{9,10},{10,11},{12,13},{... | collective-permute-start | bytes 86024 | tf_op jit(solution)/shard_map/ppermute | solution.py:458
  7.5 1.3 %collective-permute-start.1 = (f32[56,128]{1,0:T(8,128)S(1)}, f32[56,128]{1,0:T(8,128)S(1)}, u32[]{:S(2)}, u32[]{:S(2)}) collective-permute-start(f32[56,128]{1,0:T(8,128)S(1)} %get-tuple-element.13), channel_id=1, source_target_pairs={{1,0},{2,1},{3,2},{5,4},{6,5},{7,6},{9,8},{10,9},{11,10},{13,12},{... | collective-permute-start | bytes 86024 | tf_op jit(solution)/shard_map/ppermute | solution.py:458
  8.8 0.0 collective-permute-done
  8.8 3.3 %collective-permute-done.1 = f32[56,128]{1,0:T(8,128)S(1)} collective-permute-done((f32[56,128]{1,0:T(8,128)S(1)}, f32[56,128]{1,0:T(8,128)S(1)}, u32[]{:S(2)}, u32[]{:S(2)}) %collective-permute-start.1) | collective-permute-done | bytes 28704 | tf_op jit(solution)/shard_map/ppermute | solution.py:458
  12.2 1.3 %collective-permute-start.3 = (f32[840,128]{1,0:T(8,128)S(1)}, f32[840,128]{1,0:T(8,128)S(1)}, u32[]{:S(2)}, u32[]{:S(2)}) collective-permute-start(f32[840,128]{1,0:T(8,128)S(1)} %pad_maximum_fusion.own_ref), channel_id=1, source_target_pairs={{32,0},{64,32},{96,64},{128,96},{160,128},{192,160},{224,192},{256... | collective-permute-start | bytes 1290248 | tf_op jit(solution)/shard_map/ppermute | solution.py:458
  13.5 4.2 %collective-permute-start.2 = (f32[840,128]{1,0:T(8,128)S(1)}, f32[840,128]{1,0:T(8,128)S(1)}, u32[]{:S(2)}, u32[]{:S(2)}) collective-permute-start(f32[840,128]{1,0:T(8,128)S(1)} %pad_maximum_fusion.own_ref), channel_id=1, source_target_pairs={{0,32},{32,64},{64,96},{96,128},{128,160},{160,192},{192,224},{224... | collective-permute-start | bytes 1290248 | tf_op jit(solution)/shard_map/ppermute | solution.py:458
  17.7 7.6 %collective-permute-start.5 = (f32[840,128]{1,0:T(8,128)S(1)}, f32[840,128]{1,0:T(8,128)S(1)}, u32[]{:S(2)}, u32[]{:S(2)}) collective-permute-start(f32[840,128]{1,0:T(8,128)S(1)} %pad_maximum_fusion.own_ref), channel_id=1, source_target_pairs={{4,0},{8,4},{12,8},{16,12},{20,16},{24,20},{28,24},{5,1},{9,5},{13... | collective-permute-start | bytes 1290248 | tf_op jit(solution)/shard_map/ppermute | solution.py:458
  25.2 1.9 %collective-permute-start.4 = (f32[840,128]{1,0:T(8,128)S(1)}, f32[840,128]{1,0:T(8,128)S(1)}, u32[]{:S(2)}, u32[]{:S(2)}) collective-permute-start(f32[840,128]{1,0:T(8,128)S(1)} %pad_maximum_fusion.own_ref), channel_id=1, source_target_pairs={{0,4},{4,8},{8,12},{12,16},{16,20},{20,24},{24,28},{1,5},{5,9},{9,... | collective-permute-start | bytes 1290248 | tf_op jit(solution)/shard_map/ppermute | solution.py:458
  27.2 0.0 collective-permute-done.3.right_ref
  27.2 0.0 collective-permute-done.2.left_ref
  27.2 0.1 shard_map.51
  27.3 3.5 %collective-permute-start.6 = (f32[608,128]{1,0:T(8,128)S(1)}, f32[608,128]{1,0:T(8,128)S(1)}, u32[]{:S(2)}, u32[]{:S(2)}) collective-permute-start(f32[608,128]{1,0:T(8,128)S(1)} %get-tuple-element.14), channel_id=1, source_target_pairs={{0,4},{4,8},{8,12},{12,16},{16,20},{20,24},{24,28},{1,5},{5,9},{9,... | collective-permute-start | bytes 933896 | tf_op jit(solution)/shard_map/ppermute | solution.py:458
  30.8 1.9 %collective-permute-start.7 = (f32[608,128]{1,0:T(8,128)S(1)}, f32[608,128]{1,0:T(8,128)S(1)}, u32[]{:S(2)}, u32[]{:S(2)}) collective-permute-start(f32[608,128]{1,0:T(8,128)S(1)} %get-tuple-element.15), channel_id=1, source_target_pairs={{4,0},{8,4},{12,8},{16,12},{20,16},{24,20},{28,24},{5,1},{9,5},{13... | collective-permute-start | bytes 933896 | tf_op jit(solution)/shard_map/ppermute | solution.py:458
  32.8 0.0 collective-permute-done.5.back_ref
  32.8 0.0 collective-permute-done.4.front_ref
  32.8 2.8 %collective-permute-done.6.low_ref = f32[608,128]{1,0:T(8,128)S(1)} collective-permute-done((f32[608,128]{1,0:T(8,128)S(1)}, f32[608,128]{1,0:T(8,128)S(1)}, u32[]{:S(2)}, u32[]{:S(2)}) %collective-permute-start.6) | collective-permute-done | bytes 311328 | tf_op jit(solution)/shard_map/ppermute | solution.py:458
  35.6 3.4 %collective-permute-done.7.high_ref = f32[608,128]{1,0:T(8,128)S(1)} collective-permute-done((f32[608,128]{1,0:T(8,128)S(1)}, f32[608,128]{1,0:T(8,128)S(1)}, u32[]{:S(2)}, u32[]{:S(2)}) %collective-permute-start.7) | collective-permute-done | bytes 311328 | tf_op jit(solution)/shard_map/ppermute | solution.py:458
  39.0 8.5 %shard_map.52 = (f32[64,40,128]{2,1,0:T(8,128)S(1)}, f32[8,128]{1,0:T(8,128)S(1)}) custom-call(f32[840,128]{1,0:T(8,128)S(1)} %pad_maximum_fusion.own_ref, f32[840,128]{1,0:T(8,128)S(1)} %collective-permute-done.2.left_ref, f32[840,128]{1,0:T(8,128)S(1)} %collective-permute-done.3.right_ref, f32[840,128]{1,0:T(8,128)S(1)} %collective-permute-done.4.front_ref, ...), custom_call_target="tpu_custom_call" | custom-call | tf_op jit(solution)/shard_map/pallas_call | solution.py:351
  47.5 14.0 %all_to_all.10 = f32[32,8,128]{2,1,0:T(8,128)S(1)} all-to-all(f32[32,8,128]{2,1,0:T(8,128)S(1)} %broadcast_in_dim.4), channel_id=1, replica_groups=mesh['gx'=16,'gy'=8,'gz'=4] {'gy','gz'}, dimensions={0} | all-to-all | bytes 262144 | tf_op jit(solution)/shard_map/all_to_all | solution.py:463
  61.6 28.1 %all_to_all.11.gram_ref = f32[16,8,128]{2,1,0:T(8,128)S(1)} all-to-all(f32[16,8,128]{2,1,0:T(8,128)S(1)} %broadcast_in_dim.5), channel_id=1, replica_groups=mesh['gx'=16,'gy'=8,'gz'=4] {'gx'}, dimensions={0} | all-to-all | bytes 131072 | tf_op jit(solution)/shard_map/all_to_all | solution.py:463
  89.6 5.2 %shard_map.53 = (f32[512,128]{1,0:T(8,128)}, f32[40,40]{1,0:T(8,128)}) custom-call(f32[16,8,128]{2,1,0:T(8,128)S(1)} %all_to_all.11.gram_ref, f32[64,40,128]{2,1,0:T(8,128)S(1)} %get-tuple-element.17.basis_ref), custom_call_target="tpu_custom_call" | custom-call | tf_op jit(solution)/shard_map/pallas_call | solution.py:439
  (5 shorter events, 0.1 us)
Async XLA Ops:
  0.6 1.0 %copy-start = (f32[8,4,4,4,128]{4,3,2,1,0:T(4,128)S(1)}, f32[8,4,4,4,128]{4,3,2,1,0:T(4,128)}, u32[]{:S(2)}) copy-start(f32[8,4,4,4,128]{4,3,2,1,0:T(4,128)} %param.3) | copy-start | bytes 786436
  1.6 0.9 copy-start.1
  2.5 0.7 copy-start.2
  3.5 5.3 %collective-permute-start = (f32[56,128]{1,0:T(8,128)S(1)}, f32[56,128]{1,0:T(8,128)S(1)}, u32[]{:S(2)}, u32[]{:S(2)}) collective-permute-start(f32[56,128]{1,0:T(8,128)S(1)} %get-tuple-element.12), channel_id=1, source_target_pairs={{0,1},{1,2},{2,3},{4,5},{5,6},{6,7},{8,9},{9,10},{10,11},{12,13},{... | collective-permute-start | bytes 86024 | tf_op jit(solution)/shard_map/ppermute | solution.py:458
  7.5 4.6 %collective-permute-start.1 = (f32[56,128]{1,0:T(8,128)S(1)}, f32[56,128]{1,0:T(8,128)S(1)}, u32[]{:S(2)}, u32[]{:S(2)}) collective-permute-start(f32[56,128]{1,0:T(8,128)S(1)} %get-tuple-element.13), channel_id=1, source_target_pairs={{1,0},{2,1},{3,2},{5,4},{6,5},{7,6},{9,8},{10,9},{11,10},{13,12},{... | collective-permute-start | bytes 86024 | tf_op jit(solution)/shard_map/ppermute | solution.py:458
  12.2 15.0 %collective-permute-start.3 = (f32[840,128]{1,0:T(8,128)S(1)}, f32[840,128]{1,0:T(8,128)S(1)}, u32[]{:S(2)}, u32[]{:S(2)}) collective-permute-start(f32[840,128]{1,0:T(8,128)S(1)} %pad_maximum_fusion.own_ref), channel_id=1, source_target_pairs={{32,0},{64,32},{96,64},{128,96},{160,128},{192,160},{224,192},{256... | collective-permute-start | bytes 1290248 | tf_op jit(solution)/shard_map/ppermute | solution.py:458
  13.5 13.7 %collective-permute-start.2 = (f32[840,128]{1,0:T(8,128)S(1)}, f32[840,128]{1,0:T(8,128)S(1)}, u32[]{:S(2)}, u32[]{:S(2)}) collective-permute-start(f32[840,128]{1,0:T(8,128)S(1)} %pad_maximum_fusion.own_ref), channel_id=1, source_target_pairs={{0,32},{32,64},{64,96},{96,128},{128,160},{160,192},{192,224},{224... | collective-permute-start | bytes 1290248 | tf_op jit(solution)/shard_map/ppermute | solution.py:458
  17.7 15.1 %collective-permute-start.5 = (f32[840,128]{1,0:T(8,128)S(1)}, f32[840,128]{1,0:T(8,128)S(1)}, u32[]{:S(2)}, u32[]{:S(2)}) collective-permute-start(f32[840,128]{1,0:T(8,128)S(1)} %pad_maximum_fusion.own_ref), channel_id=1, source_target_pairs={{4,0},{8,4},{12,8},{16,12},{20,16},{24,20},{28,24},{5,1},{9,5},{13... | collective-permute-start | bytes 1290248 | tf_op jit(solution)/shard_map/ppermute | solution.py:458
  25.2 7.5 %collective-permute-start.4 = (f32[840,128]{1,0:T(8,128)S(1)}, f32[840,128]{1,0:T(8,128)S(1)}, u32[]{:S(2)}, u32[]{:S(2)}) collective-permute-start(f32[840,128]{1,0:T(8,128)S(1)} %pad_maximum_fusion.own_ref), channel_id=1, source_target_pairs={{0,4},{4,8},{8,12},{12,16},{16,20},{20,24},{24,28},{1,5},{5,9},{9,... | collective-permute-start | bytes 1290248 | tf_op jit(solution)/shard_map/ppermute | solution.py:458
  27.3 8.3 %collective-permute-start.6 = (f32[608,128]{1,0:T(8,128)S(1)}, f32[608,128]{1,0:T(8,128)S(1)}, u32[]{:S(2)}, u32[]{:S(2)}) collective-permute-start(f32[608,128]{1,0:T(8,128)S(1)} %get-tuple-element.14), channel_id=1, source_target_pairs={{0,4},{4,8},{8,12},{12,16},{16,20},{20,24},{24,28},{1,5},{5,9},{9,... | collective-permute-start | bytes 933896 | tf_op jit(solution)/shard_map/ppermute | solution.py:458
  30.8 8.2 %collective-permute-start.7 = (f32[608,128]{1,0:T(8,128)S(1)}, f32[608,128]{1,0:T(8,128)S(1)}, u32[]{:S(2)}, u32[]{:S(2)}) collective-permute-start(f32[608,128]{1,0:T(8,128)S(1)} %get-tuple-element.15), channel_id=1, source_target_pairs={{4,0},{8,4},{12,8},{16,12},{20,16},{24,20},{28,24},{5,1},{9,5},{13... | collective-permute-start | bytes 933896 | tf_op jit(solution)/shard_map/ppermute | solution.py:458

commit v2 on v1

v2 whole, which is shorter than its diff:
```python
import jax
import jax.numpy as jnp
from jax import lax
from jax.experimental import pallas as pl
from jax.experimental.pallas import tpu as pltpu
from jax.sharding import PartitionSpec as P

POWERS = 4
RHS = 8
COMP = 4
BX = 4
BY = 4
LANES = 128
COLS = BX * BY
GRID = BX + 2 * POWERS
HIGHEST = lax.Precision.HIGHEST
VMEM = pl.BlockSpec(memory_space=pltpu.VMEM)

FIELD_ROWS = COMP * COLS * RHS
COUPLE_AT = FIELD_ROWS
ETA_AT = COUPLE_AT + COMP * COMP * COLS
MAIN_ROWS = ETA_AT + COLS
GHOST_ROWS = COMP * RHS + 24
BLOCK_ROWS = MAIN_ROWS + GHOST_ROWS

NEAR = [(1, 1), (1, 2), (2, 1)]
FAR = [(1, 3), (2, 2), (3, 1)]
CORNER = NEAR + FAR
C_COUPLE_AT = len(CORNER) * COMP * RHS
C_ETA_AT = C_COUPLE_AT + len(NEAR) * 16
C_GHOST_AT = C_ETA_AT + 8
CORNER_ROWS = C_GHOST_AT + GHOST_ROWS
SIDES = [(1, 1), (1, -1), (-1, 1), (-1, -1)]


def lane_index():
    return lax.broadcasted_iota(jnp.int32, (RHS, LANES), 1)


def pack_kernel(raw_ref, main_ref, low_ref, high_ref):
    lane = lane_index()
    shear = raw_ref[ETA_AT:MAIN_ROWS, :]
    eta = -0.5 * (0.2 + (1.0 - jnp.exp(-100.0 * shear)) / shear)
    main_ref[ETA_AT:MAIN_ROWS, :] = eta
    main_ref[COUPLE_AT:ETA_AT, :] = raw_ref[COUPLE_AT:ETA_AT, :]

    def pack(group, load):
        low = jnp.zeros((RHS, LANES), jnp.float32)
        high = jnp.zeros((RHS, LANES), jnp.float32)
        for col in range(COLS):
            turned = pltpu.roll(load(col), (8 * col + 4) % LANES, 1)
            here = lane // 4
            high = jnp.where(here == 2 * col, turned, high)
            low = jnp.where(here == 2 * col + 1, turned, low)
        low_ref[group * 8 : group * 8 + 8, :] = low
        high_ref[group * 8 : group * 8 + 8, :] = high

    for comp in range(COMP):

        def load_field(col):
            place = comp * COLS + col
            value = raw_ref[pl.ds(place, RHS, stride=COMP * COLS), :]
            main_ref[place * RHS : place * RHS + RHS, :] = value
            return value

        pack(comp, load_field)
    for half in range(2):
        pack(
            COMP + half,
            lambda col: raw_ref[pl.ds(COUPLE_AT + half * 8 * COLS + col, 8, stride=COLS), :],
        )
    pack(
        COMP + 2,
        lambda col: jnp.broadcast_to(eta[col : col + 1, :], (RHS, LANES)),
    )


def pack(residuals, shear_rate, coupling):
    raw = jnp.concatenate(
        [part.reshape(-1, LANES) for part in (residuals, coupling, shear_rate)], axis=0
    )
    return pl.pallas_call(
        pack_kernel,
        out_shape=(
            jax.ShapeDtypeStruct((MAIN_ROWS, LANES), jnp.float32),
            jax.ShapeDtypeStruct((GHOST_ROWS, LANES), jnp.float32),
            jax.ShapeDtypeStruct((GHOST_ROWS, LANES), jnp.float32),
        ),
        in_specs=[VMEM],
        out_specs=(VMEM,) * 3,
        compiler_params=pltpu.CompilerParams(vmem_limit_bytes=4 * 2**20),
    )(raw)


def corner_kernel(main_ref, ghosts_ref, own_ref, *outs):
    own_ref[0:MAIN_ROWS, :] = main_ref[...]
    ghosts = ghosts_ref[0]
    for i in range(1, ghosts_ref.shape[0]):
        ghosts = ghosts + ghosts_ref[i]
    own_ref[MAIN_ROWS:BLOCK_ROWS, :] = ghosts
    for (side_x, side_y), out_ref in zip(SIDES, outs):
        for place, (a, b) in enumerate(CORNER):
            x = BX - a if side_x > 0 else a - 1
            y = BY - b if side_y > 0 else b - 1
            col = x * BY + y
            for comp in range(COMP):
                start = (comp * COLS + col) * RHS
                row = (place * COMP + comp) * RHS
                out_ref[row : row + RHS, :] = main_ref[start : start + RHS, :]
            if place < len(NEAR):
                for half in range(2):
                    row = C_COUPLE_AT + place * 16 + half * 8
                    out_ref[row : row + 8, :] = main_ref[
                        pl.ds(COUPLE_AT + half * 8 * COLS + col, 8, stride=COLS), :
                    ]
            out_ref[C_ETA_AT + place : C_ETA_AT + place + 1, :] = main_ref[
                ETA_AT + col : ETA_AT + col + 1, :
            ]
        out_ref[C_ETA_AT + len(CORNER) : C_GHOST_AT, :] = jnp.zeros(
            (8 - len(CORNER), LANES), jnp.float32
        )
        out_ref[C_GHOST_AT:CORNER_ROWS, :] = ghosts


def corners(main, ghosts):
    return pl.pallas_call(
        corner_kernel,
        out_shape=(jax.ShapeDtypeStruct((BLOCK_ROWS, LANES), jnp.float32),)
        + (jax.ShapeDtypeStruct((CORNER_ROWS, LANES), jnp.float32),) * 4,
        in_specs=[VMEM] * 2,
        out_specs=(VMEM,) * 5,
        compiler_params=pltpu.CompilerParams(vmem_limit_bytes=4 * 2**20),
    )(main, ghosts)


def distance(place):
    return max(POWERS - place, 0, place - (POWERS + BX - 1))


def powers_kernel(
    own_ref, left_ref, right_ref, front_ref, back_ref, corner_0, corner_1, corner_2, corner_3,
    basis_ref, gram_ref,
    main, ghost, coef, coef_ghost, face, face_ghost, scale, scale_ghost, square,
):
    lane = lane_index()
    first, last = lane == 0, lane == LANES - 1

    def slot(x, y):
        return x * GRID + y

    def place_column(src, x, y, field_at, couple_at, couple_stride, eta_at, ghost_at, col):
        reach = distance(x) + distance(y)
        at = slot(x, y)
        for comp in range(COMP):
            main[0, at * COMP + comp] = src[field_at[comp] : field_at[comp] + RHS, :]
        coef[at, 16:24, :] = jnp.broadcast_to(src[eta_at : eta_at + 1, :], (8, LANES))
        if reach >= POWERS:
            return
        for half in range(2):
            start = couple_at + half * 8 * couple_stride
            coef[at, half * 8 : half * 8 + 8, :] = (
                src[pl.ds(start, 8, stride=couple_stride), :]
                if couple_stride > 1
                else src[start : start + 8, :]
            )
        shift = (-8 * col - 4) % LANES
        for comp in range(COMP):
            row = ghost_at + comp * RHS
            ghost[0, at * COMP + comp] = pltpu.roll(src[row : row + RHS, :], shift, 1)
        for part in range(3):
            row = ghost_at + COMP * RHS + part * 8
            coef_ghost[at, part * 8 : part * 8 + 8, :] = pltpu.roll(
                src[row : row + 8, :], shift, 1
            )

    for src, off_x, off_y in (
        (own_ref, 0, 0), (left_ref, -1, 0), (right_ref, 1, 0), (front_ref, 0, -1), (back_ref, 0, 1)
    ):
        for x in range(BX):
            for y in range(BY):
                col = x * BY + y
                place_column(
                    src, POWERS + off_x * BX + x, POWERS + off_y * BY + y,
                    [(comp * COLS + col) * RHS for comp in range(COMP)],
                    COUPLE_AT + col, COLS, ETA_AT + col, MAIN_ROWS, col,
                )
    for (side_x, side_y), src in zip(SIDES, (corner_0, corner_1, corner_2, corner_3)):
        for place, (a, b) in enumerate(CORNER):
            x = POWERS - a if side_x > 0 else POWERS + BX - 1 + a
            y = POWERS - b if side_y > 0 else POWERS + BY - 1 + b
            col = (BX - a if side_x > 0 else a - 1) * BY + (BY - b if side_y > 0 else b - 1)
            place_column(
                src, x, y, [(place * COMP + comp) * RHS for comp in range(COMP)],
                C_COUPLE_AT + place * 16, 1, C_ETA_AT + place, C_GHOST_AT, col,
            )

    def rows_of(reach):
        for x in range(POWERS - reach, POWERS + BX + reach):
            rest = reach - distance(x)
            yield x, range(POWERS - rest, POWERS + BY + rest)

    def shifted(value, other):
        up, down = pltpu.roll(value, LANES - 1, 1), pltpu.roll(value, 1, 1)
        other_up, other_down = pltpu.roll(other, LANES - 1, 1), pltpu.roll(other, 1, 1)
        return (
            jnp.where(last, other_up, up), jnp.where(first, other_down, down),
            jnp.where(last, up, other_up), jnp.where(first, down, other_down),
        )

    def faces(table, out, inverse, x, y, at, eta, up, down):
        around = [
            table[slot(x - 1, y), 16:24, :], table[slot(x + 1, y), 16:24, :],
            table[slot(x, y - 1), 16:24, :], table[slot(x, y + 1), 16:24, :],
            down, up,
        ]
        kappas = [eta + beside for beside in around]
        for index, kappa in enumerate(kappas):
            out[at * 6 + index] = kappa
        total = (kappas[0] + kappas[1]) + (kappas[2] + kappas[3]) + (kappas[4] + kappas[5])
        diagonal = table[at, pl.ds(0, COMP, stride=COMP + 1), :]
        inverse[at, 0:COMP, :] = jnp.where(
            eta[0:COMP, :] < 0.0, 1.0 / (diagonal - total[0:COMP, :]), 0.0
        )

    for x, ys in rows_of(POWERS - 1):
        for y in ys:
            at = slot(x, y)
            eta, eta_ghost = coef[at, 16:24, :], coef_ghost[at, 16:24, :]
            up, down, ghost_up, ghost_down = shifted(eta, eta_ghost)
            faces(coef, face, scale, x, y, at, eta, up, down)
            if distance(x) + distance(y) < POWERS - 1:
                faces(coef_ghost, face_ghost, scale_ghost, x, y, at, eta_ghost, ghost_up, ghost_down)

    def spread(table, at, row):
        return jnp.broadcast_to(table[at, row : row + 1, :], (RHS, LANES))

    def apply(load, table, faces_of, inverse, x, y, before, centre, after, up, down):
        at = slot(x, y)
        kappa = [faces_of[at * 6 + index] for index in range(6)]
        results = []
        for comp in range(COMP):
            beside = [
                load(x - 1, y, comp), load(x + 1, y, comp), before[comp], after[comp],
                down[comp], up[comp],
            ]
            terms = [k * v for k, v in zip(kappa, beside)]
            terms += [
                spread(table, at, comp * COMP + d) * centre[d] for d in range(COMP) if d != comp
            ]
            while len(terms) > 1:
                terms = [
                    terms[i] + terms[i + 1] if i + 1 < len(terms) else terms[i]
                    for i in range(0, len(terms), 2)
                ]
            results.append(terms[0] * spread(inverse, at, comp))
        return results

    for power in range(1, POWERS + 1):
        limit = POWERS - power
        source, target = (power - 1) % 2, power % 2

        def load_main(x, y, comp, source=source):
            return main[source, slot(x, y) * COMP + comp]

        def load_ghost(x, y, comp, source=source):
            return ghost[source, slot(x, y) * COMP + comp]

        for x, ys in rows_of(limit):
            rows = {}

            def at_row(load, y, x=x, rows=rows):
                if (load, y) not in rows:
                    rows[load, y] = [load(x, y, comp) for comp in range(COMP)]
                return rows[load, y]

            for y in ys:
                at = slot(x, y)
                centre, outer = at_row(load_main, y), at_row(load_ghost, y)
                moved = [shifted(c, o) for c, o in zip(centre, outer)]
                results = apply(
                    load_main, coef, face, scale, x, y,
                    at_row(load_main, y - 1), centre, at_row(load_main, y + 1),
                    [m[0] for m in moved], [m[1] for m in moved],
                )
                for comp in range(COMP):
                    if limit:
                        main[target, at * COMP + comp] = results[comp]
                if distance(x) + distance(y) == 0:
                    for comp in range(COMP):
                        tile = comp * COLS + (x - POWERS) * BY + (y - POWERS)
                        if power == 1:
                            basis_ref[tile, 0:RHS, :] = centre[comp]
                        basis_ref[tile, power * RHS : power * RHS + RHS, :] = results[comp]
                if distance(x) + distance(y) < limit:
                    outside = apply(
                        load_ghost, coef_ghost, face_ghost, scale_ghost, x, y,
                        at_row(load_ghost, y - 1), outer, at_row(load_ghost, y + 1),
                        [m[2] for m in moved], [m[3] for m in moved],
                    )
                    for comp in range(COMP):
                        ghost[target, at * COMP + comp] = outside[comp]

    order = (POWERS + 1) * RHS
    total = jnp.zeros((order, order), jnp.float32)
    for tile in range(0, COMP * COLS, 2):
        both = jnp.concatenate([basis_ref[tile], basis_ref[tile + 1]], axis=1)
        total = total + lax.dot_general(
            both, both, (((1,), (1,)), ((), ())),
            precision=HIGHEST, preferred_element_type=jnp.float32,
        )
    square[...] = jnp.zeros_like(square)
    square[:, 0:order] = total
    packed = jnp.zeros((RHS, LANES), jnp.float32)
    start = 0
    for block in range(POWERS + 1):
        width = order - block * RHS
        value = pltpu.roll(
            square[block * RHS : block * RHS + RHS, :], (start - block * RHS) % LANES, 1
        )
        packed = jnp.where((lane >= start) & (lane < start + width), value, packed)
        start += width
    gram_ref[...] = packed


def powers(own, left, right, front, back, *corner):
    count = GRID * GRID
    return pl.pallas_call(
        powers_kernel,
        out_shape=(
            jax.ShapeDtypeStruct((COMP * COLS, (POWERS + 1) * RHS, LANES), jnp.float32),
            jax.ShapeDtypeStruct((RHS, LANES), jnp.float32),
        ),
        in_specs=[VMEM] * 9,
        out_specs=(VMEM,) * 2,
        scratch_shapes=[
            pltpu.VMEM((2, count * COMP, RHS, LANES), jnp.float32),
            pltpu.VMEM((2, count * COMP, RHS, LANES), jnp.float32),
            pltpu.VMEM((count, 24, LANES), jnp.float32),
            pltpu.VMEM((count, 24, LANES), jnp.float32),
            pltpu.VMEM((count * 6, RHS, LANES), jnp.float32),
            pltpu.VMEM((count * 6, RHS, LANES), jnp.float32),
            pltpu.VMEM((count, RHS, LANES), jnp.float32),
            pltpu.VMEM((count, RHS, LANES), jnp.float32),
            pltpu.VMEM(((POWERS + 1) * RHS, LANES), jnp.float32),
        ],
        compiler_params=pltpu.CompilerParams(vmem_limit_bytes=48 * 2**20),
    )(own, left, right, front, back, *corner)


def finish_kernel(gram_ref, basis_ref, out_ref, factor_ref, square, upper):
    lane = lane_index()
    order = (POWERS + 1) * RHS
    parts = [gram_ref[i] for i in range(gram_ref.shape[0])]
    while len(parts) > 1:
        parts = [
            parts[i] + parts[i + 1] if i + 1 < len(parts) else parts[i]
            for i in range(0, len(parts), 2)
        ]
    packed = parts[0]
    square[...] = jnp.zeros_like(square)
    start = 0
    for block in range(POWERS + 1):
        width = order - block * RHS
        value = pltpu.roll(packed, (block * RHS - start) % LANES, 1)
        keep = (lane >= block * RHS) & (lane < order)
        square[block * RHS : block * RHS + RHS, :] = jnp.where(keep, value, 0.0)
        start += width
    half = square[...]
    other = half.T
    gram = []
    for block in range(POWERS + 1):
        rows = slice(block * RHS, block * RHS + RHS)
        gram.append(jnp.where(lane < block * RHS, other[rows, :], half[rows, :]))
    summed = [tile + pltpu.roll(tile, LANES - RHS, 1) for tile in gram]
    normal = [summed[i] + summed[i + 1] for i in range(POWERS)] + [summed[0]]

    upper[...] = jnp.zeros_like(upper)
    number = lane[0:1, :]

    def pair(matrix, step):
        tile, row = step // RHS, step % RHS
        p, q = matrix[tile][row : row + 1, :], matrix[tile][row + 1 : row + 2, :]
        one = p[:, step : step + 1]
        cross = p[:, step + 1 : step + 2]
        inverse = 1.0 / one
        ratio = cross * inverse
        other = q[:, step + 1 : step + 2] - cross * ratio
        rest = q - ratio * p
        inverse_other = 1.0 / other
        second = rest * inverse_other
        first = p * inverse - ratio * second
        return p, rest, one, other, first, second, inverse, inverse_other, ratio

    for step in range(0, order, 2):
        tile = step // RHS
        p, rest, one, other, first, second, _, _, _ = pair(gram, step)
        upper[step : step + 1, :] = jnp.where(number >= step, p * lax.rsqrt(one), 0.0)
        upper[step + 1 : step + 2, :] = jnp.where(
            number > step, rest * lax.rsqrt(other), 0.0
        )
        low = tile if step % RHS < RHS - 2 else tile + 1
        for i in range(low, POWERS + 1):
            gram[i] = (
                gram[i]
                - gram[i][:, step : step + 1] * first
                - gram[i][:, step + 1 : step + 2] * second
            )
        if step < POWERS * RHS:
            _, _, _, _, first, second, inverse, inverse_other, ratio = pair(normal, step)
            mixed = ratio * inverse_other
            at_one, at_other = number == step, number == step + 1
            first = jnp.where(
                at_one, -(inverse + ratio * mixed), jnp.where(at_other, mixed, first)
            )
            second = jnp.where(at_one, mixed, jnp.where(at_other, -inverse_other, second))
            cleared = (lane == step) | (lane == step + 1)
            for i in range(low, POWERS + 1):
                normal[i] = (
                    jnp.where(cleared, 0.0, normal[i])
                    - normal[i][:, step : step + 1] * first
                    - normal[i][:, step + 1 : step + 2] * second
                )
    factor_ref[...] = upper[0:order, 0:order]
    answer = normal[POWERS]
    weights = [
        jnp.broadcast_to(answer[:, i : i + 1], (RHS, LANES)) for i in range(POWERS * RHS)
    ]

    def combine(tile, carry):
        sums = [None] * 4
        for i in range(POWERS * RHS):
            term = weights[i] * jnp.broadcast_to(basis_ref[tile, i : i + 1, :], (RHS, LANES))
            sums[i % 4] = term if sums[i % 4] is None else sums[i % 4] + term
        out_ref[pl.ds(tile, RHS, stride=COMP * COLS), :] = (sums[0] + sums[1]) + (
            sums[2] + sums[3]
        )
        return carry

    lax.fori_loop(0, COMP * COLS, combine, 0, unroll=4)


def finish(gram, basis):
    order = (POWERS + 1) * RHS
    return pl.pallas_call(
        finish_kernel,
        out_shape=(
            jax.ShapeDtypeStruct((RHS * COMP * COLS, LANES), jnp.float32),
            jax.ShapeDtypeStruct((order, order), jnp.float32),
        ),
        in_specs=[VMEM] * 2,
        out_specs=(VMEM,) * 2,
        scratch_shapes=[
            pltpu.VMEM((LANES, LANES), jnp.float32),
            pltpu.VMEM((order, LANES), jnp.float32),
        ],
        compiler_params=pltpu.CompilerParams(vmem_limit_bytes=6 * 2**20),
    )(gram, basis)


def moved(block, step_x, step_y):
    across, along = lax.axis_size("gx"), lax.axis_size("gy")
    pairs = [
        (x * along + y, (x + step_x) * along + y + step_y)
        for x in range(across)
        for y in range(along)
        if 0 <= x + step_x < across and 0 <= y + step_y < along
    ]
    return lax.ppermute(block, ("gx", "gy"), pairs)


def vertical(low, high):
    count, place = lax.axis_size("gz"), lax.axis_index("gz")
    index = jnp.arange(count)[:, None, None]
    sent = jnp.where(index == place + 1, high[None], jnp.where(index == place - 1, low[None], 0.0))
    return lax.all_to_all(sent, "gz", 0, 0)


def gathered(tile, axes):
    count = lax.axis_size(axes)
    return lax.all_to_all(jnp.broadcast_to(tile[None], (count,) + tile.shape), axes, 0, 0)


def local(residuals, shear_rate, coupling):
    block, low, high = pack(residuals, shear_rate, coupling)
    own, *parts = corners(block, vertical(low, high))
    left, right = moved(own, 1, 0), moved(own, -1, 0)
    corner = [moved(part, *side) for part, side in zip(parts, SIDES)]
    front, back = moved(own, 0, 1), moved(own, 0, -1)
    basis, gram = powers(own, left, right, front, back, *corner)
    gram = jnp.sum(gathered(gram, ("gy", "gz")), axis=0)
    correction, factor = finish(gathered(gram, "gx"), basis)
    return correction.reshape(residuals.shape), factor


def solution(mesh):
    in_specs = (
        P(None, None, "gx", "gy", "gz"),
        P("gx", "gy", "gz"),
        P(None, None, "gx", "gy", "gz"),
    )
    out_specs = (P(None, None, "gx", "gy", "gz"), P())
    return jax.shard_map(local, mesh=mesh, in_specs=in_specs, out_specs=out_specs, check_vma=False)
```

time: 95.2 us -> 103 us (1.082)
  blocking collectives: 42.1 us -> 51.4 us
  waiting for transfers between devices: 9.59 us -> 14.6 us
  Pallas kernels: 14 us -> 11.4 us
  local copies, waits for them, and re-layouts: 2.57 us -> 0.02 us
  starting transfers between devices: 25.8 us -> 23.4 us
  other arithmetic: 0.07 us -> 1.19 us
    all_to_all x0 -> x1, blocking collectives: none -> 9.55 us  [vertical(): return lax.all_to_all(sent, 'gz', 0, 0)]
    ppermute x8, waiting for transfers between devices: 9.59 us -> 14.6 us  [moved(): return lax.ppermute(block, ('gx', 'gy'), pairs)]
    pallas_call x1, Pallas kernels: 8.46 us -> 5.44 us  [powers(): pl.pallas_call(powers_kernel, out_shape=(jax.ShapeDtypeStruct((COMP * COL...]
    unnamed x6 -> x0, local copies, waits for them, and re-layouts: 2.54 us -> none
    ppermute x8, starting transfers between devices: 25.8 us -> 23.4 us  [moved(): return lax.ppermute(block, ('gx', 'gy'), pairs)]
    concatenate x1, other arithmetic: 0.03 us -> 1.06 us  [pack(): jnp.concatenate([part.reshape(-1, LANES) for part in (residuals, coupling...]
  transfers between devices with their start and end apart: 8 -> 8, of which waited for: 3 -> 2; matrix products, arithmetic and copies ran while one was open for 0% -> 0% of each run, Pallas kernels for 0% -> 0%
where the time goes in v2:
time: 103 us
  blocking collectives  51.4 us (50%)
  starting transfers between devices  23.4 us (23%)
  waiting for transfers between devices  14.6 us (14%)
  Pallas kernels  11.4 us (11%)
  other arithmetic  1.19 us (1%)
    all_to_all x2, blocking collectives, gathered(): lax.all_to_all(jnp.broadcast_to(tile[None], (count,) + tile.shape), axes,...  41.9 us
    ppermute x8, starting transfers between devices, moved(): return lax.ppermute(block, ('gx', 'gy'), pairs)  23.4 us
    ppermute x8, waiting for transfers between devices, moved(): return lax.ppermute(block, ('gx', 'gy'), pairs)  14.6 us
    all_to_all x1, blocking collectives, vertical(): return lax.all_to_all(sent, 'gz', 0, 0)  9.55 us
    pallas_call x1, Pallas kernels, finish(): pl.pallas_call(finish_kernel, out_shape=(jax.ShapeDtypeStruct((RHS * COMP...  5.55 us
    pallas_call x1, Pallas kernels, powers(): pl.pallas_call(powers_kernel, out_shape=(jax.ShapeDtypeStruct((COMP * COL...  5.44 us
  transfers between devices with their start and end apart: 8, of which 2 were waited for; matrix products, arithmetic and copies ran while one was open for 0% of the time, Pallas kernels for 0%

profile of v2, /device:TPU:1, one launch (start us, length us, event | category | flops | bytes accessed | tf_op | source)
XLA Modules:
  0.0 102.7 jit_solution(4406880013257837037)
XLA Ops:
  0.6 1.1 %pad_maximum_fusion.raw_ref = f32[784,128]{1,0:T(8,128)S(1)} fusion(f32[16,128]{1,0:T(8,128)} %bitcast.6, f32[256,128]{1,0:T(8,128)} %bitcast.5, f32[512,128]{1,0:T(8,128)} %bitcast.4), kind=kLoop, calls=%fused_computation | loop fusion | flops 200704 | bytes 802816 | tf_op jit(solution)/shard_map/concatenate | solution.py:79
  1.7 0.3 shard_map.50
  2.0 0.1 select_select_fusion
  2.1 9.6 %all_to_all.15.ghosts_ref = f32[4,56,128]{2,1,0:T(8,128)S(1)} all-to-all(f32[4,56,128]{2,1,0:T(8,128)S(1)} %select_select_fusion), channel_id=1, replica_groups=mesh['gx'=16,'gy'=8,'gz'=4] {'gz'}, dimensions={0} | all-to-all | bytes 229376 | tf_op jit(solution)/shard_map/all_to_all | solution.py:475
  11.6 0.1 shard_map.51
  11.7 6.5 %collective-permute-start.4 = (f32[304,128]{1,0:T(8,128)S(1)}, f32[304,128]{1,0:T(8,128)S(1)}, u32[]{:S(2)}, u32[]{:S(2)}) collective-permute-start(f32[304,128]{1,0:T(8,128)S(1)} %get-tuple-element.18), channel_id=1, source_target_pairs={{0,36},{4,40},{8,44},{12,48},{16,52},{20,56},{24,60},{32,68},{36,7... | collective-permute-start | bytes 466952 | tf_op jit(solution)/shard_map/ppermute | solution.py:468
  18.2 1.3 %collective-permute-start.5 = (f32[304,128]{1,0:T(8,128)S(1)}, f32[304,128]{1,0:T(8,128)S(1)}, u32[]{:S(2)}, u32[]{:S(2)}) collective-permute-start(f32[304,128]{1,0:T(8,128)S(1)} %get-tuple-element.19), channel_id=1, source_target_pairs={{4,32},{8,36},{12,40},{16,44},{20,48},{24,52},{28,56},{36,64},{40,... | collective-permute-start | bytes 466952 | tf_op jit(solution)/shard_map/ppermute | solution.py:468
  19.5 1.9 %collective-permute-start.3 = (f32[840,128]{1,0:T(8,128)S(1)}, f32[840,128]{1,0:T(8,128)S(1)}, u32[]{:S(2)}, u32[]{:S(2)}) collective-permute-start(f32[840,128]{1,0:T(8,128)S(1)} %get-tuple-element.17.own_ref), channel_id=1, source_target_pairs={{4,0},{8,4},{12,8},{16,12},{20,16},{24,20},{28,24},{36,32},{40,36}... | collective-permute-start | bytes 1290248 | tf_op jit(solution)/shard_map/ppermute | solution.py:468
  21.4 5.6 %collective-permute-start.2 = (f32[840,128]{1,0:T(8,128)S(1)}, f32[840,128]{1,0:T(8,128)S(1)}, u32[]{:S(2)}, u32[]{:S(2)}) collective-permute-start(f32[840,128]{1,0:T(8,128)S(1)} %get-tuple-element.17.own_ref), channel_id=1, source_target_pairs={{0,4},{4,8},{8,12},{12,16},{16,20},{20,24},{24,28},{32,36},{36,40}... | collective-permute-start | bytes 1290248 | tf_op jit(solution)/shard_map/ppermute | solution.py:468
  27.1 1.3 %collective-permute-start.1 = (f32[840,128]{1,0:T(8,128)S(1)}, f32[840,128]{1,0:T(8,128)S(1)}, u32[]{:S(2)}, u32[]{:S(2)}) collective-permute-start(f32[840,128]{1,0:T(8,128)S(1)} %get-tuple-element.17.own_ref), channel_id=1, source_target_pairs={{32,0},{36,4},{40,8},{44,12},{48,16},{52,20},{56,24},{60,28},{64,3... | collective-permute-start | bytes 1290248 | tf_op jit(solution)/shard_map/ppermute | solution.py:468
  28.4 0.0 collective-permute-done.4.corner_0
  28.4 4.2 %collective-permute-start = (f32[840,128]{1,0:T(8,128)S(1)}, f32[840,128]{1,0:T(8,128)S(1)}, u32[]{:S(2)}, u32[]{:S(2)}) collective-permute-start(f32[840,128]{1,0:T(8,128)S(1)} %get-tuple-element.17.own_ref), channel_id=1, source_target_pairs={{0,32},{4,36},{8,40},{12,44},{16,48},{20,52},{24,56},{28,60},{32,6... | collective-permute-start | bytes 1290248 | tf_op jit(solution)/shard_map/ppermute | solution.py:468
  32.6 0.0 collective-permute-done.5.corner_1
  32.6 1.3 %collective-permute-start.6 = (f32[304,128]{1,0:T(8,128)S(1)}, f32[304,128]{1,0:T(8,128)S(1)}, u32[]{:S(2)}, u32[]{:S(2)}) collective-permute-start(f32[304,128]{1,0:T(8,128)S(1)} %get-tuple-element.20), channel_id=1, source_target_pairs={{32,4},{36,8},{40,12},{44,16},{48,20},{52,24},{56,28},{64,36},{68,... | collective-permute-start | bytes 466952 | tf_op jit(solution)/shard_map/ppermute | solution.py:468
  33.9 7.0 %collective-permute-done.6.corner_2 = f32[304,128]{1,0:T(8,128)S(1)} collective-permute-done((f32[304,128]{1,0:T(8,128)S(1)}, f32[304,128]{1,0:T(8,128)S(1)}, u32[]{:S(2)}, u32[]{:S(2)}) %collective-permute-start.6) | collective-permute-done | bytes 155680 | tf_op jit(solution)/shard_map/ppermute | solution.py:468
  40.9 1.3 %collective-permute-start.7 = (f32[304,128]{1,0:T(8,128)S(1)}, f32[304,128]{1,0:T(8,128)S(1)}, u32[]{:S(2)}, u32[]{:S(2)}) collective-permute-start(f32[304,128]{1,0:T(8,128)S(1)} %get-tuple-element.21), channel_id=1, source_target_pairs={{36,0},{40,4},{44,8},{48,12},{52,16},{56,20},{60,24},{68,32},{72,3... | collective-permute-start | bytes 466952 | tf_op jit(solution)/shard_map/ppermute | solution.py:468
  42.2 7.6 %collective-permute-done.7.corner_3 = f32[304,128]{1,0:T(8,128)S(1)} collective-permute-done((f32[304,128]{1,0:T(8,128)S(1)}, f32[304,128]{1,0:T(8,128)S(1)}, u32[]{:S(2)}, u32[]{:S(2)}) %collective-permute-start.7) | collective-permute-done | bytes 155680 | tf_op jit(solution)/shard_map/ppermute | solution.py:468
  49.7 0.0 collective-permute-done.3.back_ref
  49.7 0.0 collective-permute-done.2.front_ref
  49.7 0.0 collective-permute-done.1.right_ref
  49.7 0.0 collective-permute-done.left_ref
  49.8 5.4 %shard_map.52 = (f32[64,40,128]{2,1,0:T(8,128)S(1)}, f32[8,128]{1,0:T(8,128)S(1)}) custom-call(f32[840,128]{1,0:T(8,128)S(1)} %get-tuple-element.17.own_ref, f32[840,128]{1,0:T(8,128)S(1)} %collective-permute-done.left_ref, f32[840,128]{1,0:T(8,128)S(1)} %collective-permute-done.1.right_ref, f32[840,128]{1,0:T(8,128)S(1)} %collective-permute-done.2.front_ref, ...), custom_call_target="tpu_custom_call" | custom-call | tf_op jit(solution)/shard_map/pallas_call | solution.py:327
  55.2 15.7 %all_to_all.16 = f32[32,8,128]{2,1,0:T(8,128)S(1)} all-to-all(f32[32,8,128]{2,1,0:T(8,128)S(1)} %broadcast_in_dim.56), channel_id=1, replica_groups=mesh['gx'=16,'gy'=8,'gz'=4] {'gy','gz'}, dimensions={0} | all-to-all | bytes 262144 | tf_op jit(solution)/shard_map/all_to_all | solution.py:480
  71.0 26.1 %all_to_all.17.gram_ref = f32[16,8,128]{2,1,0:T(8,128)S(1)} all-to-all(f32[16,8,128]{2,1,0:T(8,128)S(1)} %broadcast_in_dim.57), channel_id=1, replica_groups=mesh['gx'=16,'gy'=8,'gz'=4] {'gx'}, dimensions={0} | all-to-all | bytes 131072 | tf_op jit(solution)/shard_map/all_to_all | solution.py:480
  97.1 5.6 %shard_map.53 = (f32[512,128]{1,0:T(8,128)}, f32[40,40]{1,0:T(8,128)}) custom-call(f32[16,8,128]{2,1,0:T(8,128)S(1)} %all_to_all.17.gram_ref, f32[64,40,128]{2,1,0:T(8,128)S(1)} %get-tuple-element.23.basis_ref), custom_call_target="tpu_custom_call" | custom-call | tf_op jit(solution)/shard_map/pallas_call | solution.py:444
  (4 shorter events, 0.1 us)
Async XLA Ops:
  11.7 16.6 %collective-permute-start.4 = (f32[304,128]{1,0:T(8,128)S(1)}, f32[304,128]{1,0:T(8,128)S(1)}, u32[]{:S(2)}, u32[]{:S(2)}) collective-permute-start(f32[304,128]{1,0:T(8,128)S(1)} %get-tuple-element.18), channel_id=1, source_target_pairs={{0,36},{4,40},{8,44},{12,48},{16,52},{20,56},{24,60},{32,68},{36,7... | collective-permute-start | bytes 466952 | tf_op jit(solution)/shard_map/ppermute | solution.py:468
  18.2 14.4 %collective-permute-start.5 = (f32[304,128]{1,0:T(8,128)S(1)}, f32[304,128]{1,0:T(8,128)S(1)}, u32[]{:S(2)}, u32[]{:S(2)}) collective-permute-start(f32[304,128]{1,0:T(8,128)S(1)} %get-tuple-element.19), channel_id=1, source_target_pairs={{4,32},{8,36},{12,40},{16,44},{20,48},{24,52},{28,56},{36,64},{40,... | collective-permute-start | bytes 466952 | tf_op jit(solution)/shard_map/ppermute | solution.py:468
  19.5 30.2 %collective-permute-start.3 = (f32[840,128]{1,0:T(8,128)S(1)}, f32[840,128]{1,0:T(8,128)S(1)}, u32[]{:S(2)}, u32[]{:S(2)}) collective-permute-start(f32[840,128]{1,0:T(8,128)S(1)} %get-tuple-element.17.own_ref), channel_id=1, source_target_pairs={{4,0},{8,4},{12,8},{16,12},{20,16},{24,20},{28,24},{36,32},{40,36}... | collective-permute-start | bytes 1290248 | tf_op jit(solution)/shard_map/ppermute | solution.py:468
  21.4 28.3 %collective-permute-start.2 = (f32[840,128]{1,0:T(8,128)S(1)}, f32[840,128]{1,0:T(8,128)S(1)}, u32[]{:S(2)}, u32[]{:S(2)}) collective-permute-start(f32[840,128]{1,0:T(8,128)S(1)} %get-tuple-element.17.own_ref), channel_id=1, source_target_pairs={{0,4},{4,8},{8,12},{12,16},{16,20},{20,24},{24,28},{32,36},{36,40}... | collective-permute-start | bytes 1290248 | tf_op jit(solution)/shard_map/ppermute | solution.py:468
  27.1 22.7 %collective-permute-start.1 = (f32[840,128]{1,0:T(8,128)S(1)}, f32[840,128]{1,0:T(8,128)S(1)}, u32[]{:S(2)}, u32[]{:S(2)}) collective-permute-start(f32[840,128]{1,0:T(8,128)S(1)} %get-tuple-element.17.own_ref), channel_id=1, source_target_pairs={{32,0},{36,4},{40,8},{44,12},{48,16},{52,20},{56,24},{60,28},{64,3... | collective-permute-start | bytes 1290248 | tf_op jit(solution)/shard_map/ppermute | solution.py:468
  28.4 21.4 %collective-permute-start = (f32[840,128]{1,0:T(8,128)S(1)}, f32[840,128]{1,0:T(8,128)S(1)}, u32[]{:S(2)}, u32[]{:S(2)}) collective-permute-start(f32[840,128]{1,0:T(8,128)S(1)} %get-tuple-element.17.own_ref), channel_id=1, source_target_pairs={{0,32},{4,36},{8,40},{12,44},{16,48},{20,52},{24,56},{28,60},{32,6... | collective-permute-start | bytes 1290248 | tf_op jit(solution)/shard_map/ppermute | solution.py:468
  32.6 8.3 %collective-permute-start.6 = (f32[304,128]{1,0:T(8,128)S(1)}, f32[304,128]{1,0:T(8,128)S(1)}, u32[]{:S(2)}, u32[]{:S(2)}) collective-permute-start(f32[304,128]{1,0:T(8,128)S(1)} %get-tuple-element.20), channel_id=1, source_target_pairs={{32,4},{36,8},{40,12},{44,16},{48,20},{52,24},{56,28},{64,36},{68,... | collective-permute-start | bytes 466952 | tf_op jit(solution)/shard_map/ppermute | solution.py:468
  40.9 8.9 %collective-permute-start.7 = (f32[304,128]{1,0:T(8,128)S(1)}, f32[304,128]{1,0:T(8,128)S(1)}, u32[]{:S(2)}, u32[]{:S(2)}) collective-permute-start(f32[304,128]{1,0:T(8,128)S(1)} %get-tuple-element.21), channel_id=1, source_target_pairs={{36,0},{40,4},{44,8},{48,12},{52,16},{56,20},{60,24},{68,32},{72,3... | collective-permute-start | bytes 466952 | tf_op jit(solution)/shard_map/ppermute | solution.py:468

commit v3 on v2

--- a/solution.py
+++ b/solution.py
@@ -17,20 +17,27 @@
 VMEM = pl.BlockSpec(memory_space=pltpu.VMEM)
 
 FIELD_ROWS = COMP * COLS * RHS
-COUPLE_AT = FIELD_ROWS
-ETA_AT = COUPLE_AT + COMP * COMP * COLS
-MAIN_ROWS = ETA_AT + COLS
+LAYER = COMP * COMP * BY
 GHOST_ROWS = COMP * RHS + 24
-BLOCK_ROWS = MAIN_ROWS + GHOST_ROWS
+GHOST_AT = LAYER
+FIELD_AT = GHOST_AT + GHOST_ROWS
+ETA_AT = FIELD_AT + FIELD_ROWS
+TAIL_AT = ETA_AT + COLS
+BLOCK_ROWS = TAIL_AT + (BX - 1) * LAYER
+SIDE_ROWS = BLOCK_ROWS - LAYER
 
 NEAR = [(1, 1), (1, 2), (2, 1)]
 FAR = [(1, 3), (2, 2), (3, 1)]
-CORNER = NEAR + FAR
+CORNER = [(side, a, b) for a, b in NEAR + FAR for side in (0, 1)]
+NEAR_COUNT = 2 * len(NEAR)
 C_COUPLE_AT = len(CORNER) * COMP * RHS
-C_ETA_AT = C_COUPLE_AT + len(NEAR) * 16
-C_GHOST_AT = C_ETA_AT + 8
+C_ETA_AT = C_COUPLE_AT + NEAR_COUNT * 16
+C_GHOST_AT = C_ETA_AT + 16
 CORNER_ROWS = C_GHOST_AT + GHOST_ROWS
-SIDES = [(1, 1), (1, -1), (-1, 1), (-1, -1)]
+
+
+def couple_at(x):
+    return TAIL_AT + (x - 1) * LAYER if x else 0
 
 
 def lane_index():
@@ -39,10 +46,17 @@
 
 def pack_kernel(raw_ref, main_ref, low_ref, high_ref):
     lane = lane_index()
-    shear = raw_ref[ETA_AT:MAIN_ROWS, :]
+    raw_couple = FIELD_ROWS
+    raw_shear = FIELD_ROWS + BX * LAYER
+    shear = raw_ref[raw_shear : raw_shear + COLS, :]
     eta = -0.5 * (0.2 + (1.0 - jnp.exp(-100.0 * shear)) / shear)
-    main_ref[ETA_AT:MAIN_ROWS, :] = eta
-    main_ref[COUPLE_AT:ETA_AT, :] = raw_ref[COUPLE_AT:ETA_AT, :]
+    main_ref[ETA_AT:TAIL_AT, :] = eta
+    main_ref[GHOST_AT:FIELD_AT, :] = jnp.zeros((GHOST_ROWS, LANES), jnp.float32)
+    for entry in range(COMP * COMP):
+        for x in range(BX):
+            start = raw_couple + entry * COLS + x * BY
+            row = couple_at(x) + entry * BY
+            main_ref[row : row + BY, :] = raw_ref[start : start + BY, :]
 
     def pack(group, load):
         low = jnp.zeros((RHS, LANES), jnp.float32)
@@ -60,14 +74,15 @@
         def load_field(col):
             place = comp * COLS + col
             value = raw_ref[pl.ds(place, RHS, stride=COMP * COLS), :]
-            main_ref[place * RHS : place * RHS + RHS, :] = value
+            row = FIELD_AT + place * RHS
+            main_ref[row : row + RHS, :] = value
             return value
 
         pack(comp, load_field)
     for half in range(2):
         pack(
             COMP + half,
-            lambda col: raw_ref[pl.ds(COUPLE_AT + half * 8 * COLS + col, 8, stride=COLS), :],
+            lambda col: raw_ref[pl.ds(raw_couple + half * 8 * COLS + col, 8, stride=COLS), :],
         )
     pack(
         COMP + 2,
@@ -82,7 +97,7 @@
     return pl.pallas_call(
         pack_kernel,
         out_shape=(
-            jax.ShapeDtypeStruct((MAIN_ROWS, LANES), jnp.float32),
+            jax.ShapeDtypeStruct((BLOCK_ROWS, LANES), jnp.float32),
             jax.ShapeDtypeStruct((GHOST_ROWS, LANES), jnp.float32),
             jax.ShapeDtypeStruct((GHOST_ROWS, LANES), jnp.float32),
         ),
@@ -92,45 +107,45 @@
     )(raw)
 
 
-def corner_kernel(main_ref, ghosts_ref, own_ref, *outs):
-    own_ref[0:MAIN_ROWS, :] = main_ref[...]
-    ghosts = ghosts_ref[0]
-    for i in range(1, ghosts_ref.shape[0]):
-        ghosts = ghosts + ghosts_ref[i]
-    own_ref[MAIN_ROWS:BLOCK_ROWS, :] = ghosts
-    for (side_x, side_y), out_ref in zip(SIDES, outs):
-        for place, (a, b) in enumerate(CORNER):
-            x = BX - a if side_x > 0 else a - 1
-            y = BY - b if side_y > 0 else b - 1
+def corner_kernel(left_ref, right_ref, down_ref, up_ref):
+    lane = lane_index()
+    for out_ref, top in ((down_ref, False), (up_ref, True)):
+        for place, (side, a, b) in enumerate(CORNER):
+            src = right_ref if side else left_ref
+            base = 0 if side else -LAYER
+            x = a - 1 if side else BX - a
+            y = BY - b if top else b - 1
             col = x * BY + y
             for comp in range(COMP):
-                start = (comp * COLS + col) * RHS
+                start = base + FIELD_AT + (comp * COLS + col) * RHS
                 row = (place * COMP + comp) * RHS
-                out_ref[row : row + RHS, :] = main_ref[start : start + RHS, :]
-            if place < len(NEAR):
+                out_ref[row : row + RHS, :] = src[start : start + RHS, :]
+            if place < NEAR_COUNT:
                 for half in range(2):
                     row = C_COUPLE_AT + place * 16 + half * 8
-                    out_ref[row : row + 8, :] = main_ref[
-                        pl.ds(COUPLE_AT + half * 8 * COLS + col, 8, stride=COLS), :
-                    ]
-            out_ref[C_ETA_AT + place : C_ETA_AT + place + 1, :] = main_ref[
-                ETA_AT + col : ETA_AT + col + 1, :
-            ]
+                    start = base + couple_at(x) + half * 8 * BY + y
+                    out_ref[row : row + 8, :] = src[pl.ds(start, 8, stride=BY), :]
+            start = base + ETA_AT + col
+            out_ref[C_ETA_AT + place : C_ETA_AT + place + 1, :] = src[start : start + 1, :]
         out_ref[C_ETA_AT + len(CORNER) : C_GHOST_AT, :] = jnp.zeros(
-            (8 - len(CORNER), LANES), jnp.float32
-        )
-        out_ref[C_GHOST_AT:CORNER_ROWS, :] = ghosts
-
-
-def corners(main, ghosts):
+            (16 - len(CORNER), LANES), jnp.float32
+        )
+        for row in range(0, GHOST_ROWS, 8):
+            right = right_ref[GHOST_AT + row : GHOST_AT + row + 8, :]
+            left = left_ref[GHOST_AT - LAYER + row : GHOST_AT - LAYER + row + 8, :]
+            out_ref[C_GHOST_AT + row : C_GHOST_AT + row + 8, :] = jnp.where(
+                lane < LANES // 2, right, left
+            )
+
+
+def corners(left, right):
     return pl.pallas_call(
         corner_kernel,
-        out_shape=(jax.ShapeDtypeStruct((BLOCK_ROWS, LANES), jnp.float32),)
-        + (jax.ShapeDtypeStruct((CORNER_ROWS, LANES), jnp.float32),) * 4,
+        out_shape=(jax.ShapeDtypeStruct((CORNER_ROWS, LANES), jnp.float32),) * 2,
         in_specs=[VMEM] * 2,
-        out_specs=(VMEM,) * 5,
+        out_specs=(VMEM,) * 2,
         compiler_params=pltpu.CompilerParams(vmem_limit_bytes=4 * 2**20),
-    )(main, ghosts)
+    )(left, right)
 
 
 def distance(place):
@@ -138,7 +153,7 @@
 
 
 def powers_kernel(
-    own_ref, left_ref, right_ref, front_ref, back_ref, corner_0, corner_1, corner_2, corner_3,
+    own_ref, left_ref, right_ref, front_ref, back_ref, low_ref, high_ref,
     basis_ref, gram_ref,
     main, ghost, coef, coef_ghost, face, face_ghost, scale, scale_ghost, square,
 ):
@@ -148,7 +163,7 @@
     def slot(x, y):
         return x * GRID + y
 
-    def place_column(src, x, y, field_at, couple_at, couple_stride, eta_at, ghost_at, col):
+    def place_column(src, x, y, field_at, entry_at, couple_stride, eta_at, ghost_at, col):
         reach = distance(x) + distance(y)
         at = slot(x, y)
         for comp in range(COMP):
@@ -157,7 +172,7 @@
         if reach >= POWERS:
             return
         for half in range(2):
-            start = couple_at + half * 8 * couple_stride
+            start = entry_at + half * 8 * couple_stride
             coef[at, half * 8 : half * 8 + 8, :] = (
                 src[pl.ds(start, 8, stride=couple_stride), :]
                 if couple_stride > 1
@@ -173,22 +188,23 @@
                 src[row : row + 8, :], shift, 1
             )
 
-    for src, off_x, off_y in (
-        (own_ref, 0, 0), (left_ref, -1, 0), (right_ref, 1, 0), (front_ref, 0, -1), (back_ref, 0, 1)
+    for src, base, off_x, off_y in (
+        (own_ref, 0, 0, 0), (left_ref, -LAYER, -1, 0), (right_ref, 0, 1, 0),
+        (front_ref, 0, 0, -1), (back_ref, 0, 0, 1),
     ):
         for x in range(BX):
             for y in range(BY):
                 col = x * BY + y
                 place_column(
                     src, POWERS + off_x * BX + x, POWERS + off_y * BY + y,
-                    [(comp * COLS + col) * RHS for comp in range(COMP)],
-                    COUPLE_AT + col, COLS, ETA_AT + col, MAIN_ROWS, col,
+                    [base + FIELD_AT + (comp * COLS + col) * RHS for comp in range(COMP)],
+                    base + couple_at(x) + y, BY, base + ETA_AT + col, base + GHOST_AT, col,
                 )
-    for (side_x, side_y), src in zip(SIDES, (corner_0, corner_1, corner_2, corner_3)):
-        for place, (a, b) in enumerate(CORNER):
-            x = POWERS - a if side_x > 0 else POWERS + BX - 1 + a
-            y = POWERS - b if side_y > 0 else POWERS + BY - 1 + b
-            col = (BX - a if side_x > 0 else a - 1) * BY + (BY - b if side_y > 0 else b - 1)
+    for src, top in ((low_ref, True), (high_ref, False)):
+        for place, (side, a, b) in enumerate(CORNER):
+            x = POWERS + BX - 1 + a if side else POWERS - a
+            y = POWERS - b if top else POWERS + BY - 1 + b
+            col = (a - 1 if side else BX - a) * BY + (BY - b if top else b - 1)
             place_column(
                 src, x, y, [(place * COMP + comp) * RHS for comp in range(COMP)],
                 C_COUPLE_AT + place * 16, 1, C_ETA_AT + place, C_GHOST_AT, col,
@@ -322,7 +338,7 @@
     gram_ref[...] = packed
 
 
-def powers(own, left, right, front, back, *corner):
+def powers(*parts):
     count = GRID * GRID
     return pl.pallas_call(
         powers_kernel,
@@ -330,7 +346,7 @@
             jax.ShapeDtypeStruct((COMP * COLS, (POWERS + 1) * RHS, LANES), jnp.float32),
             jax.ShapeDtypeStruct((RHS, LANES), jnp.float32),
         ),
-        in_specs=[VMEM] * 9,
+        in_specs=[VMEM] * 7,
         out_specs=(VMEM,) * 2,
         scratch_shapes=[
             pltpu.VMEM((2, count * COMP, RHS, LANES), jnp.float32),
@@ -344,7 +360,7 @@
             pltpu.VMEM(((POWERS + 1) * RHS, LANES), jnp.float32),
         ],
         compiler_params=pltpu.CompilerParams(vmem_limit_bytes=48 * 2**20),
-    )(own, left, right, front, back, *corner)
+    )(*parts)
 
 
 def finish_kernel(gram_ref, basis_ref, out_ref, factor_ref, square, upper):
@@ -377,14 +393,16 @@
     upper[...] = jnp.zeros_like(upper)
     number = lane[0:1, :]
 
+    def wide(value, column):
+        return jnp.broadcast_to(value[:, column : column + 1], value.shape)
+
     def pair(matrix, step):
         tile, row = step // RHS, step % RHS
         p, q = matrix[tile][row : row + 1, :], matrix[tile][row + 1 : row + 2, :]
-        one = p[:, step : step + 1]
-        cross = p[:, step + 1 : step + 2]
+        one, cross, far = wide(p, step), wide(p, step + 1), wide(q, step + 1)
         inverse = 1.0 / one
         ratio = cross * inverse
-        other = q[:, step + 1 : step + 2] - cross * ratio
+        other = far - cross * ratio
         rest = q - ratio * p
         inverse_other = 1.0 / other
         second = rest * inverse_other
@@ -393,32 +411,28 @@
 
     for step in range(0, order, 2):
         tile = step // RHS
+        low = tile if step % RHS < RHS - 2 else tile + 1
         p, rest, one, other, first, second, _, _, _ = pair(gram, step)
-        upper[step : step + 1, :] = jnp.where(number >= step, p * lax.rsqrt(one), 0.0)
-        upper[step + 1 : step + 2, :] = jnp.where(
-            number > step, rest * lax.rsqrt(other), 0.0
-        )
-        low = tile if step % RHS < RHS - 2 else tile + 1
+        top = jnp.where(number >= step, p * lax.rsqrt(one), 0.0)
+        bottom = jnp.where(number > step, rest * lax.rsqrt(other), 0.0)
+        upper[step : step + 1, :] = top[0:1, :]
+        upper[step + 1 : step + 2, :] = bottom[0:1, :]
         for i in range(low, POWERS + 1):
-            gram[i] = (
-                gram[i]
-                - gram[i][:, step : step + 1] * first
-                - gram[i][:, step + 1 : step + 2] * second
-            )
+            gram[i] = gram[i] - wide(gram[i], step) * first - wide(gram[i], step + 1) * second
         if step < POWERS * RHS:
             _, _, _, _, first, second, inverse, inverse_other, ratio = pair(normal, step)
             mixed = ratio * inverse_other
             at_one, at_other = number == step, number == step + 1
+            cleared = (lane == step) | (lane == step + 1)
             first = jnp.where(
                 at_one, -(inverse + ratio * mixed), jnp.where(at_other, mixed, first)
             )
             second = jnp.where(at_one, mixed, jnp.where(at_other, -inverse_other, second))
-            cleared = (lane == step) | (lane == step + 1)
             for i in range(low, POWERS + 1):
                 normal[i] = (
                     jnp.where(cleared, 0.0, normal[i])
-                    - normal[i][:, step : step + 1] * first
-                    - normal[i][:, step + 1 : step + 2] * second
+                    - wide(normal[i], step) * first
+                    - wide(normal[i], step + 1) * second
                 )
     factor_ref[...] = upper[0:order, 0:order]
     answer = normal[POWERS]
@@ -457,15 +471,10 @@
     )(gram, basis)
 
 
-def moved(block, step_x, step_y):
-    across, along = lax.axis_size("gx"), lax.axis_size("gy")
-    pairs = [
-        (x * along + y, (x + step_x) * along + y + step_y)
-        for x in range(across)
-        for y in range(along)
-        if 0 <= x + step_x < across and 0 <= y + step_y < along
-    ]
-    return lax.ppermute(block, ("gx", "gy"), pairs)
+def moved(block, axis, step):
+    count = lax.axis_size(axis)
+    pairs = [(i, i + step) for i in range(count) if 0 <= i + step < count]
+    return lax.ppermute(block, axis, pairs)
 
 
 def vertical(low, high):
@@ -482,11 +491,13 @@
 
 def local(residuals, shear_rate, coupling):
     block, low, high = pack(residuals, shear_rate, coupling)
-    own, *parts = corners(block, vertical(low, high))
-    left, right = moved(own, 1, 0), moved(own, -1, 0)
-    corner = [moved(part, *side) for part, side in zip(parts, SIDES)]
-    front, back = moved(own, 0, 1), moved(own, 0, -1)
-    basis, gram = powers(own, left, right, front, back, *corner)
+    ghosts = jnp.sum(vertical(low, high), axis=0)
+    own = lax.dynamic_update_slice(block, ghosts, (GHOST_AT, 0))
+    left, right = moved(own[LAYER:], "gx", 1), moved(own[:SIDE_ROWS], "gx", -1)
+    front, back = moved(own, "gy", 1), moved(own, "gy", -1)
+    down, up = corners(left, right)
+    low_corner, high_corner = moved(up, "gy", 1), moved(down, "gy", -1)
+    basis, gram = powers(own, left, right, front, back, low_corner, high_corner)
     gram = jnp.sum(gathered(gram, ("gy", "gz")), axis=0)
     correction, factor = finish(gathered(gram, "gx"), basis)
     return correction.reshape(residuals.shape), factor

time: 103 us -> 87.6 us (0.85)
  waiting for transfers between devices: 14.6 us -> 5.79 us
  starting transfers between devices: 23.4 us -> 19.9 us
  Pallas kernels: 11.4 us -> 9.55 us
  blocking collectives: 51.4 us -> 49.9 us
    ppermute x8 -> x6, waiting for transfers between devices: 14.6 us -> 5.79 us  [moved(): return lax.ppermute(block, axis, pairs)]
    ppermute x8 -> x6, starting transfers between devices: 23.4 us -> 19.9 us  [moved(): return lax.ppermute(block, axis, pairs)]
    pallas_call x1, Pallas kernels: 5.55 us -> 3.62 us  [finish(): pl.pallas_call(finish_kernel, out_shape=(jax.ShapeDtypeStruct((RHS * COMP...]
    all_to_all x2, blocking collectives: 41.9 us -> 40.3 us  [gathered(): lax.all_to_all(jnp.broadcast_to(tile[None], (count,) + tile.shape), axes,...]
  transfers between devices with their start and end apart: 8 -> 6, of which waited for: 2 -> 3; matrix products, arithmetic and copies ran while one was open for 0% -> 0% of each run, Pallas kernels for 0% -> 0%
where the time goes in v3:
time: 87.6 us; the launch traced here: 87.2 us
  blocking collectives  49.9 us (57%)
  starting transfers between devices  19.9 us (23%)
  Pallas kernels  9.55 us (11%)
  waiting for transfers between devices  5.79 us (7%)
  other arithmetic  1.2 us (1%)
    all_to_all x2, blocking collectives, gathered(): lax.all_to_all(jnp.broadcast_to(tile[None], (count,) + tile.shape), axes,...  40.3 us
    ppermute x6, starting transfers between devices, moved(): return lax.ppermute(block, axis, pairs)  19.9 us
    all_to_all x1, blocking collectives, vertical(): return lax.all_to_all(sent, 'gz', 0, 0)  9.55 us
    ppermute x6, waiting for transfers between devices, moved(): return lax.ppermute(block, axis, pairs)  5.79 us
    pallas_call x1, Pallas kernels, powers(): pl.pallas_call(powers_kernel, out_shape=(jax.ShapeDtypeStruct((COMP * COL...  5.6 us
    pallas_call x1, Pallas kernels, finish(): pl.pallas_call(finish_kernel, out_shape=(jax.ShapeDtypeStruct((RHS * COMP...  3.62 us
  transfers between devices with their start and end apart: 6, of which 3 were waited for; matrix products, arithmetic and copies ran while one was open for 0% of the time, Pallas kernels for 0%

profile of v3, /device:TPU:1, one launch (start us, length us, event | category | flops | bytes accessed | tf_op | source)
XLA Modules:
  0.0 87.2 jit_solution(7222233482811402701)
XLA Ops:
  0.6 1.1 %pad_maximum_fusion.raw_ref = f32[784,128]{1,0:T(8,128)S(1)} fusion(f32[16,128]{1,0:T(8,128)} %bitcast.6, f32[256,128]{1,0:T(8,128)} %bitcast.5, f32[512,128]{1,0:T(8,128)} %bitcast.4), kind=kLoop, calls=%fused_computation | loop fusion | flops 200704 | bytes 802816 | tf_op jit(solution)/shard_map/concatenate | solution.py:94
  1.7 0.3 shard_map.50
  2.0 0.1 select_select_fusion
  2.1 9.6 %all_to_all.15 = f32[4,56,128]{2,1,0:T(8,128)S(1)} all-to-all(f32[4,56,128]{2,1,0:T(8,128)S(1)} %select_select_fusion), channel_id=1, replica_groups=mesh['gx'=16,'gy'=8,'gz'=4] {'gz'}, dimensions={0} | all-to-all | bytes 229376 | tf_op jit(solution)/shard_map/all_to_all | solution.py:484
  11.7 0.1 fusion
  11.7 1.3 %collective-permute-start.1 = (f32[776,128]{1,0:T(8,128)S(1)}, f32[776,128]{1,0:T(8,128)S(1)}, u32[]{:S(2)}, u32[]{:S(2)}) collective-permute-start(f32[776,128]{1,0:T(8,128)S(1)} %get-tuple-element.20), channel_id=1, source_target_pairs={{32,0},{64,32},{96,64},{128,96},{160,128},{192,160},{224,192},{256... | collective-permute-start | bytes 1191944 | tf_op jit(solution)/shard_map/ppermute | solution.py:477
  13.0 4.2 %collective-permute-start = (f32[776,128]{1,0:T(8,128)S(1)}, f32[776,128]{1,0:T(8,128)S(1)}, u32[]{:S(2)}, u32[]{:S(2)}) collective-permute-start(f32[776,128]{1,0:T(8,128)S(1)} %get-tuple-element.21), channel_id=1, source_target_pairs={{0,32},{32,64},{64,96},{96,128},{128,160},{160,192},{192,224},{224... | collective-permute-start | bytes 1191944 | tf_op jit(solution)/shard_map/ppermute | solution.py:477
  17.2 7.9 %collective-permute-start.3 = (f32[840,128]{1,0:T(8,128)S(1)}, f32[840,128]{1,0:T(8,128)S(1)}, u32[]{:S(2)}, u32[]{:S(2)}) collective-permute-start(f32[840,128]{1,0:T(8,128)S(1)} %constant_dynamic-update-slice_fusion.own_ref), channel_id=1, source_target_pairs={{4,0},{8,4},{12,8},{16,12},{20,16},{24,20},{28,24},{5,1},{9,5},{13... | collective-permute-start | bytes 1290248 | tf_op jit(solution)/shard_map/ppermute | solution.py:477
  25.1 1.9 %collective-permute-start.2 = (f32[840,128]{1,0:T(8,128)S(1)}, f32[840,128]{1,0:T(8,128)S(1)}, u32[]{:S(2)}, u32[]{:S(2)}) collective-permute-start(f32[840,128]{1,0:T(8,128)S(1)} %constant_dynamic-update-slice_fusion.own_ref), channel_id=1, source_target_pairs={{0,4},{4,8},{8,12},{12,16},{16,20},{20,24},{24,28},{1,5},{5,9},{9,... | collective-permute-start | bytes 1290248 | tf_op jit(solution)/shard_map/ppermute | solution.py:477
  27.0 0.0 collective-permute-done.1.right_ref
  27.1 0.0 collective-permute-done.left_ref
  27.1 2.5 %collective-permute-start.4 = (f32[552,128]{1,0:T(8,128)S(1)}, f32[552,128]{1,0:T(8,128)S(1)}, u32[]{:S(2)}, u32[]{:S(2)}) collective-permute-start(f32[552,128]{1,0:T(8,128)S(1)} %get-tuple-element.14), channel_id=1, source_target_pairs={{0,4},{4,8},{8,12},{12,16},{16,20},{20,24},{24,28},{1,5},{5,9},{9,... | collective-permute-start | bytes 847880 | tf_op jit(solution)/shard_map/ppermute | solution.py:477
  29.7 2.1 %collective-permute-start.5 = (f32[552,128]{1,0:T(8,128)S(1)}, f32[552,128]{1,0:T(8,128)S(1)}, u32[]{:S(2)}, u32[]{:S(2)}) collective-permute-start(f32[552,128]{1,0:T(8,128)S(1)} %get-tuple-element.15), channel_id=1, source_target_pairs={{4,0},{8,4},{12,8},{16,12},{20,16},{24,20},{28,24},{5,1},{9,5},{13... | collective-permute-start | bytes 847880 | tf_op jit(solution)/shard_map/ppermute | solution.py:477
  31.8 0.0 collective-permute-done.3.back_ref
  31.8 0.4 collective-permute-done.2.front_ref
  32.1 3.0 %collective-permute-done.4.low_ref = f32[552,128]{1,0:T(8,128)S(1)} collective-permute-done((f32[552,128]{1,0:T(8,128)S(1)}, f32[552,128]{1,0:T(8,128)S(1)}, u32[]{:S(2)}, u32[]{:S(2)}) %collective-permute-start.4) | collective-permute-done | bytes 282656 | tf_op jit(solution)/shard_map/ppermute | solution.py:477
  35.2 2.4 %collective-permute-done.5.high_ref = f32[552,128]{1,0:T(8,128)S(1)} collective-permute-done((f32[552,128]{1,0:T(8,128)S(1)}, f32[552,128]{1,0:T(8,128)S(1)}, u32[]{:S(2)}, u32[]{:S(2)}) %collective-permute-start.5) | collective-permute-done | bytes 282656 | tf_op jit(solution)/shard_map/ppermute | solution.py:477
  37.6 5.6 %shard_map.52 = (f32[64,40,128]{2,1,0:T(8,128)S(1)}, f32[8,128]{1,0:T(8,128)S(1)}) custom-call(f32[840,128]{1,0:T(8,128)S(1)} %constant_dynamic-update-slice_fusion.own_ref, f32[776,128]{1,0:T(8,128)S(1)} %collective-permute-done.left_ref, f32[776,128]{1,0:T(8,128)S(1)} %collective-permute-done.1.right_ref, f32[840,128]{1,0:T(8,128)S(1)} %collective-permute-done.2.front_ref, ...), custom_call_target="tpu_custom_call" | custom-call | tf_op jit(solution)/shard_map/pallas_call | solution.py:343
  43.2 12.3 %all_to_all.16 = f32[32,8,128]{2,1,0:T(8,128)S(1)} all-to-all(f32[32,8,128]{2,1,0:T(8,128)S(1)} %broadcast_in_dim.56), channel_id=1, replica_groups=mesh['gx'=16,'gy'=8,'gz'=4] {'gy','gz'}, dimensions={0} | all-to-all | bytes 262144 | tf_op jit(solution)/shard_map/all_to_all | solution.py:489
  55.5 28.1 %all_to_all.17.gram_ref = f32[16,8,128]{2,1,0:T(8,128)S(1)} all-to-all(f32[16,8,128]{2,1,0:T(8,128)S(1)} %broadcast_in_dim.57), channel_id=1, replica_groups=mesh['gx'=16,'gy'=8,'gz'=4] {'gx'}, dimensions={0} | all-to-all | bytes 131072 | tf_op jit(solution)/shard_map/all_to_all | solution.py:489
  83.6 3.6 %shard_map.53 = (f32[512,128]{1,0:T(8,128)}, f32[40,40]{1,0:T(8,128)}) custom-call(f32[16,8,128]{2,1,0:T(8,128)S(1)} %all_to_all.17.gram_ref, f32[64,40,128]{2,1,0:T(8,128)S(1)} %get-tuple-element.17.basis_ref), custom_call_target="tpu_custom_call" | custom-call | tf_op jit(solution)/shard_map/pallas_call | solution.py:458
  (7 shorter events, 0.1 us)
Async XLA Ops:
  11.7 15.3 %collective-permute-start.1 = (f32[776,128]{1,0:T(8,128)S(1)}, f32[776,128]{1,0:T(8,128)S(1)}, u32[]{:S(2)}, u32[]{:S(2)}) collective-permute-start(f32[776,128]{1,0:T(8,128)S(1)} %get-tuple-element.20), channel_id=1, source_target_pairs={{32,0},{64,32},{96,64},{128,96},{160,128},{192,160},{224,192},{256... | collective-permute-start | bytes 1191944 | tf_op jit(solution)/shard_map/ppermute | solution.py:477
  13.0 14.0 %collective-permute-start = (f32[776,128]{1,0:T(8,128)S(1)}, f32[776,128]{1,0:T(8,128)S(1)}, u32[]{:S(2)}, u32[]{:S(2)}) collective-permute-start(f32[776,128]{1,0:T(8,128)S(1)} %get-tuple-element.21), channel_id=1, source_target_pairs={{0,32},{32,64},{64,96},{96,128},{128,160},{160,192},{192,224},{224... | collective-permute-start | bytes 1191944 | tf_op jit(solution)/shard_map/ppermute | solution.py:477
  17.2 14.6 %collective-permute-start.3 = (f32[840,128]{1,0:T(8,128)S(1)}, f32[840,128]{1,0:T(8,128)S(1)}, u32[]{:S(2)}, u32[]{:S(2)}) collective-permute-start(f32[840,128]{1,0:T(8,128)S(1)} %constant_dynamic-update-slice_fusion.own_ref), channel_id=1, source_target_pairs={{4,0},{8,4},{12,8},{16,12},{20,16},{24,20},{28,24},{5,1},{9,5},{13... | collective-permute-start | bytes 1290248 | tf_op jit(solution)/shard_map/ppermute | solution.py:477
  25.1 7.0 %collective-permute-start.2 = (f32[840,128]{1,0:T(8,128)S(1)}, f32[840,128]{1,0:T(8,128)S(1)}, u32[]{:S(2)}, u32[]{:S(2)}) collective-permute-start(f32[840,128]{1,0:T(8,128)S(1)} %constant_dynamic-update-slice_fusion.own_ref), channel_id=1, source_target_pairs={{0,4},{4,8},{8,12},{12,16},{16,20},{20,24},{24,28},{1,5},{5,9},{9,... | collective-permute-start | bytes 1290248 | tf_op jit(solution)/shard_map/ppermute | solution.py:477
  27.1 8.0 %collective-permute-start.4 = (f32[552,128]{1,0:T(8,128)S(1)}, f32[552,128]{1,0:T(8,128)S(1)}, u32[]{:S(2)}, u32[]{:S(2)}) collective-permute-start(f32[552,128]{1,0:T(8,128)S(1)} %get-tuple-element.14), channel_id=1, source_target_pairs={{0,4},{4,8},{8,12},{12,16},{16,20},{20,24},{24,28},{1,5},{5,9},{9,... | collective-permute-start | bytes 847880 | tf_op jit(solution)/shard_map/ppermute | solution.py:477
  29.7 7.9 %collective-permute-start.5 = (f32[552,128]{1,0:T(8,128)S(1)}, f32[552,128]{1,0:T(8,128)S(1)}, u32[]{:S(2)}, u32[]{:S(2)}) collective-permute-start(f32[552,128]{1,0:T(8,128)S(1)} %get-tuple-element.15), channel_id=1, source_target_pairs={{4,0},{8,4},{12,8},{16,12},{20,16},{24,20},{28,24},{5,1},{9,5},{13... | collective-permute-start | bytes 847880 | tf_op jit(solution)/shard_map/ppermute | solution.py:477

commit v4 on v3

--- a/solution.py
+++ b/solution.py
@@ -152,68 +152,91 @@
     return max(POWERS - place, 0, place - (POWERS + BX - 1))
 
 
-def powers_kernel(
-    own_ref, left_ref, right_ref, front_ref, back_ref, low_ref, high_ref,
-    basis_ref, gram_ref,
-    main, ghost, coef, coef_ghost, face, face_ghost, scale, scale_ghost, square,
-):
+def corner(x, y):
+    return distance(x) > 0 and distance(y) > 0
+
+
+def rows_of(reach):
+    for x in range(POWERS - reach, POWERS + BX + reach):
+        rest = reach - distance(x)
+        yield x, range(POWERS - rest, POWERS + BY + rest)
+
+
+PLACES = [(x, y) for x, ys in rows_of(POWERS) for y in ys]
+SLOT = {place: i for i, place in enumerate(sorted(PLACES, key=lambda place: corner(*place)))}
+EARLY = sum(not corner(*place) for place in PLACES)
+
+
+def ready(x, y, power):
+    if power == 0:
+        return not corner(x, y)
+    around = ((x, y), (x - 1, y), (x + 1, y), (x, y - 1), (x, y + 1))
+    return all(ready(i, j, power - 1) for i, j in around)
+
+
+def state_shapes(count):
+    field = (count * COMP, RHS, LANES)
+    return (
+        [field] * 4 + [(count, 24, LANES)] * 2 + [(count * 6, RHS, LANES)] * 2
+        + [(count, RHS, LANES)] * 2
+    )
+
+
+def powers_part(early, blocks, first_state, mine, basis_ref):
     lane = lane_index()
     first, last = lane == 0, lane == LANES - 1
-
-    def slot(x, y):
-        return x * GRID + y
-
-    def place_column(src, x, y, field_at, entry_at, couple_stride, eta_at, ghost_at, col):
-        reach = distance(x) + distance(y)
-        at = slot(x, y)
+    MAIN, GHOST, COEF, FACE, SCALE = 0, 2, 4, 6, 8
+
+    def held(kind, x, y, power):
+        return first_state[kind] if early or ready(x, y, power) else mine[kind]
+
+    def place_column(src, x, y, field_at, entry_at, stride, eta_at, ghost_at, col):
+        at = SLOT[x, y]
         for comp in range(COMP):
-            main[0, at * COMP + comp] = src[field_at[comp] : field_at[comp] + RHS, :]
-        coef[at, 16:24, :] = jnp.broadcast_to(src[eta_at : eta_at + 1, :], (8, LANES))
-        if reach >= POWERS:
+            mine[MAIN][at * COMP + comp] = src[field_at[comp] : field_at[comp] + RHS, :]
+        mine[COEF][at, 16:24, :] = jnp.broadcast_to(src[eta_at : eta_at + 1, :], (8, LANES))
+        if distance(x) + distance(y) >= POWERS:
             return
         for half in range(2):
-            start = entry_at + half * 8 * couple_stride
-            coef[at, half * 8 : half * 8 + 8, :] = (
-                src[pl.ds(start, 8, stride=couple_stride), :]
-                if couple_stride > 1
-                else src[start : start + 8, :]
+            start = entry_at + half * 8 * stride
+            mine[COEF][at, half * 8 : half * 8 + 8, :] = (
+                src[pl.ds(start, 8, stride=stride), :] if stride > 1 else src[start : start + 8, :]
             )
         shift = (-8 * col - 4) % LANES
         for comp in range(COMP):
             row = ghost_at + comp * RHS
-            ghost[0, at * COMP + comp] = pltpu.roll(src[row : row + RHS, :], shift, 1)
+            mine[GHOST][at * COMP + comp] = pltpu.roll(src[row : row + RHS, :], shift, 1)
         for part in range(3):
             row = ghost_at + COMP * RHS + part * 8
-            coef_ghost[at, part * 8 : part * 8 + 8, :] = pltpu.roll(
+            mine[COEF + 1][at, part * 8 : part * 8 + 8, :] = pltpu.roll(
                 src[row : row + 8, :], shift, 1
             )
 
-    for src, base, off_x, off_y in (
-        (own_ref, 0, 0, 0), (left_ref, -LAYER, -1, 0), (right_ref, 0, 1, 0),
-        (front_ref, 0, 0, -1), (back_ref, 0, 0, 1),
-    ):
-        for x in range(BX):
-            for y in range(BY):
-                col = x * BY + y
+    if early:
+        own_ref, left_ref, right_ref, front_ref, back_ref = blocks
+        for src, base, off_x, off_y in (
+            (own_ref, 0, 0, 0), (left_ref, -LAYER, -1, 0), (right_ref, 0, 1, 0),
+            (front_ref, 0, 0, -1), (back_ref, 0, 0, 1),
+        ):
+            for x in range(BX):
+                for y in range(BY):
+                    col = x * BY + y
+                    place_column(
+                        src, POWERS + off_x * BX + x, POWERS + off_y * BY + y,
+                        [base + FIELD_AT + (comp * COLS + col) * RHS for comp in range(COMP)],
+                        base + couple_at(x) + y, BY, base + ETA_AT + col, base + GHOST_AT, col,
+                    )
+    else:
+        low_ref, high_ref = blocks
+        for src, top in ((low_ref, True), (high_ref, False)):
+            for place, (side, a, b) in enumerate(CORNER):
+                x = POWERS + BX - 1 + a if side else POWERS - a
+                y = POWERS - b if top else POWERS + BY - 1 + b
+                col = (a - 1 if side else BX - a) * BY + (BY - b if top else b - 1)
                 place_column(
-                    src, POWERS + off_x * BX + x, POWERS + off_y * BY + y,
-                    [base + FIELD_AT + (comp * COLS + col) * RHS for comp in range(COMP)],
-                    base + couple_at(x) + y, BY, base + ETA_AT + col, base + GHOST_AT, col,
+                    src, x, y, [(place * COMP + comp) * RHS for comp in range(COMP)],
+                    C_COUPLE_AT + place * 16, 1, C_ETA_AT + place, C_GHOST_AT, col,
                 )
-    for src, top in ((low_ref, True), (high_ref, False)):
-        for place, (side, a, b) in enumerate(CORNER):
-            x = POWERS + BX - 1 + a if side else POWERS - a
-            y = POWERS - b if top else POWERS + BY - 1 + b
-            col = (a - 1 if side else BX - a) * BY + (BY - b if top else b - 1)
-            place_column(
-                src, x, y, [(place * COMP + comp) * RHS for comp in range(COMP)],
-                C_COUPLE_AT + place * 16, 1, C_ETA_AT + place, C_GHOST_AT, col,
-            )
-
-    def rows_of(reach):
-        for x in range(POWERS - reach, POWERS + BX + reach):
-            rest = reach - distance(x)
-            yield x, range(POWERS - rest, POWERS + BY + rest)
 
     def shifted(value, other):
         up, down = pltpu.roll(value, LANES - 1, 1), pltpu.roll(value, 1, 1)
@@ -223,41 +246,47 @@
             jnp.where(last, up, other_up), jnp.where(first, down, other_down),
         )
 
-    def faces(table, out, inverse, x, y, at, eta, up, down):
+    def eta_at(kind, x, y):
+        return held(kind, x, y, 0)[SLOT[x, y], 16:24, :]
+
+    def faces(outer, x, y, eta, up, down):
+        kind, at = COEF + outer, SLOT[x, y]
         around = [
-            table[slot(x - 1, y), 16:24, :], table[slot(x + 1, y), 16:24, :],
-            table[slot(x, y - 1), 16:24, :], table[slot(x, y + 1), 16:24, :],
-            down, up,
+            eta_at(kind, x - 1, y), eta_at(kind, x + 1, y),
+            eta_at(kind, x, y - 1), eta_at(kind, x, y + 1), down, up,
         ]
         kappas = [eta + beside for beside in around]
         for index, kappa in enumerate(kappas):
-            out[at * 6 + index] = kappa
+            mine[FACE + outer][at * 6 + index] = kappa
         total = (kappas[0] + kappas[1]) + (kappas[2] + kappas[3]) + (kappas[4] + kappas[5])
-        diagonal = table[at, pl.ds(0, COMP, stride=COMP + 1), :]
-        inverse[at, 0:COMP, :] = jnp.where(
+        diagonal = held(kind, x, y, 0)[at, pl.ds(0, COMP, stride=COMP + 1), :]
+        mine[SCALE + outer][at, 0:COMP, :] = jnp.where(
             eta[0:COMP, :] < 0.0, 1.0 / (diagonal - total[0:COMP, :]), 0.0
         )
 
     for x, ys in rows_of(POWERS - 1):
         for y in ys:
-            at = slot(x, y)
-            eta, eta_ghost = coef[at, 16:24, :], coef_ghost[at, 16:24, :]
+            if ready(x, y, 1) != early:
+                continue
+            eta, eta_ghost = eta_at(COEF, x, y), eta_at(COEF + 1, x, y)
             up, down, ghost_up, ghost_down = shifted(eta, eta_ghost)
-            faces(coef, face, scale, x, y, at, eta, up, down)
+            faces(0, x, y, eta, up, down)
             if distance(x) + distance(y) < POWERS - 1:
-                faces(coef_ghost, face_ghost, scale_ghost, x, y, at, eta_ghost, ghost_up, ghost_down)
-
-    def spread(table, at, row):
-        return jnp.broadcast_to(table[at, row : row + 1, :], (RHS, LANES))
-
-    def apply(load, table, faces_of, inverse, x, y, before, centre, after, up, down):
-        at = slot(x, y)
+                faces(1, x, y, eta_ghost, ghost_up, ghost_down)
+
+    def spread(ref, at, row):
+        return jnp.broadcast_to(ref[at, row : row + 1, :], (RHS, LANES))
+
+    def apply(outer, power, x, y, before, centre, after, up, down):
+        at = SLOT[x, y]
+        table = held(COEF + outer, x, y, 0)
+        faces_of, inverse = held(FACE + outer, x, y, 1), held(SCALE + outer, x, y, 1)
         kappa = [faces_of[at * 6 + index] for index in range(6)]
         results = []
         for comp in range(COMP):
             beside = [
-                load(x - 1, y, comp), load(x + 1, y, comp), before[comp], after[comp],
-                down[comp], up[comp],
+                load(outer, power, x - 1, y, comp), load(outer, power, x + 1, y, comp),
+                before[comp], after[comp], down[comp], up[comp],
             ]
             terms = [k * v for k, v in zip(kappa, beside)]
             terms += [
@@ -271,51 +300,67 @@
             results.append(terms[0] * spread(inverse, at, comp))
         return results
 
+    def load(outer, power, x, y, comp):
+        kind = (GHOST if outer else MAIN) + power % 2
+        return held(kind, x, y, power)[SLOT[x, y] * COMP + comp]
+
     for power in range(1, POWERS + 1):
         limit = POWERS - power
-        source, target = (power - 1) % 2, power % 2
-
-        def load_main(x, y, comp, source=source):
-            return main[source, slot(x, y) * COMP + comp]
-
-        def load_ghost(x, y, comp, source=source):
-            return ghost[source, slot(x, y) * COMP + comp]
-
         for x, ys in rows_of(limit):
             rows = {}
 
-            def at_row(load, y, x=x, rows=rows):
-                if (load, y) not in rows:
-                    rows[load, y] = [load(x, y, comp) for comp in range(COMP)]
-                return rows[load, y]
+            def at_row(outer, y, x=x, rows=rows, power=power):
+                if (outer, y) not in rows:
+                    rows[outer, y] = [load(outer, power - 1, x, y, comp) for comp in range(COMP)]
+                return rows[outer, y]
 
             for y in ys:
-                at = slot(x, y)
-                centre, outer = at_row(load_main, y), at_row(load_ghost, y)
-                moved = [shifted(c, o) for c, o in zip(centre, outer)]
+                if ready(x, y, power) != early:
+                    continue
+                at = SLOT[x, y]
+                reach = distance(x) + distance(y)
+                centre, outer = at_row(0, y), at_row(1, y)
+                moves = [shifted(c, o) for c, o in zip(centre, outer)]
                 results = apply(
-                    load_main, coef, face, scale, x, y,
-                    at_row(load_main, y - 1), centre, at_row(load_main, y + 1),
-                    [m[0] for m in moved], [m[1] for m in moved],
+                    0, power - 1, x, y, at_row(0, y - 1), centre, at_row(0, y + 1),
+                    [m[0] for m in moves], [m[1] for m in moves],
                 )
                 for comp in range(COMP):
                     if limit:
-                        main[target, at * COMP + comp] = results[comp]
-                if distance(x) + distance(y) == 0:
+                        mine[MAIN + power % 2][at * COMP + comp] = results[comp]
+                if reach == 0:
                     for comp in range(COMP):
                         tile = comp * COLS + (x - POWERS) * BY + (y - POWERS)
                         if power == 1:
                             basis_ref[tile, 0:RHS, :] = centre[comp]
                         basis_ref[tile, power * RHS : power * RHS + RHS, :] = results[comp]
-                if distance(x) + distance(y) < limit:
+                if reach < limit:
                     outside = apply(
-                        load_ghost, coef_ghost, face_ghost, scale_ghost, x, y,
-                        at_row(load_ghost, y - 1), outer, at_row(load_ghost, y + 1),
-                        [m[2] for m in moved], [m[3] for m in moved],
+                        1, power - 1, x, y, at_row(1, y - 1), outer, at_row(1, y + 1),
+                        [m[2] for m in moves], [m[3] for m in moves],
                     )
                     for comp in range(COMP):
-                        ghost[target, at * COMP + comp] = outside[comp]
-
+                        mine[GHOST + power % 2][at * COMP + comp] = outside[comp]
+
+
+def early_kernel(*refs):
+    powers_part(True, refs[:5], refs[5:15], refs[5:15], refs[15])
+
+
+def late_kernel(*refs):
+    blocks, first_state, early_basis = refs[:2], refs[2:12], refs[12]
+    basis_ref, gram_ref, mine, square = refs[13], refs[14], refs[15:25], refs[25]
+    for x in range(BX):
+        for y in range(BY):
+            for power in range(1, POWERS + 1):
+                if ready(POWERS + x, POWERS + y, power):
+                    start = 0 if power == 1 else power * RHS
+                    stop = power * RHS + RHS
+                    for comp in range(COMP):
+                        tile = comp * COLS + x * BY + y
+                        basis_ref[tile, start:stop, :] = early_basis[tile, start:stop, :]
+    powers_part(False, blocks, first_state, mine, basis_ref)
+    lane = lane_index()
     order = (POWERS + 1) * RHS
     total = jnp.zeros((order, order), jnp.float32)
     for tile in range(0, COMP * COLS, 2):
@@ -338,29 +383,34 @@
     gram_ref[...] = packed
 
 
-def powers(*parts):
-    count = GRID * GRID
+def early_powers(*blocks):
+    basis = (COMP * COLS, (POWERS + 1) * RHS, LANES)
     return pl.pallas_call(
-        powers_kernel,
+        early_kernel,
+        out_shape=[
+            jax.ShapeDtypeStruct(shape, jnp.float32) for shape in state_shapes(EARLY) + [basis]
+        ],
+        in_specs=[VMEM] * 5,
+        out_specs=[VMEM] * 11,
+        compiler_params=pltpu.CompilerParams(vmem_limit_bytes=20 * 2**20),
+        cost_estimate=pl.CostEstimate(flops=5_000_000, bytes_accessed=8_000_000, transcendentals=0),
+    )(*blocks)
+
+
+def late_powers(low, high, state):
+    basis = (COMP * COLS, (POWERS + 1) * RHS, LANES)
+    return pl.pallas_call(
+        late_kernel,
         out_shape=(
-            jax.ShapeDtypeStruct((COMP * COLS, (POWERS + 1) * RHS, LANES), jnp.float32),
+            jax.ShapeDtypeStruct(basis, jnp.float32),
             jax.ShapeDtypeStruct((RHS, LANES), jnp.float32),
         ),
-        in_specs=[VMEM] * 7,
+        in_specs=[VMEM] * 13,
         out_specs=(VMEM,) * 2,
-        scratch_shapes=[
-            pltpu.VMEM((2, count * COMP, RHS, LANES), jnp.float32),
-            pltpu.VMEM((2, count * COMP, RHS, LANES), jnp.float32),
-            pltpu.VMEM((count, 24, LANES), jnp.float32),
-            pltpu.VMEM((count, 24, LANES), jnp.float32),
-            pltpu.VMEM((count * 6, RHS, LANES), jnp.float32),
-            pltpu.VMEM((count * 6, RHS, LANES), jnp.float32),
-            pltpu.VMEM((count, RHS, LANES), jnp.float32),
-            pltpu.VMEM((count, RHS, LANES), jnp.float32),
-            pltpu.VMEM(((POWERS + 1) * RHS, LANES), jnp.float32),
-        ],
-        compiler_params=pltpu.CompilerParams(vmem_limit_bytes=48 * 2**20),
-    )(*parts)
+        scratch_shapes=[pltpu.VMEM(shape, jnp.float32) for shape in state_shapes(len(PLACES))]
+        + [pltpu.VMEM(((POWERS + 1) * RHS, LANES), jnp.float32)],
+        compiler_params=pltpu.CompilerParams(vmem_limit_bytes=36 * 2**20),
+    )(low, high, *state)
 
 
 def finish_kernel(gram_ref, basis_ref, out_ref, factor_ref, square, upper):
@@ -497,7 +547,8 @@
     front, back = moved(own, "gy", 1), moved(own, "gy", -1)
     down, up = corners(left, right)
     low_corner, high_corner = moved(up, "gy", 1), moved(down, "gy", -1)
-    basis, gram = powers(own, left, right, front, back, low_corner, high_corner)
+    state = early_powers(own, left, right, front, back)
+    basis, gram = late_powers(low_corner, high_corner, state)
     gram = jnp.sum(gathered(gram, ("gy", "gz")), axis=0)
     correction, factor = finish(gathered(gram, "gx"), basis)
     return correction.reshape(residuals.shape), factor

time: 87.6 us -> 85.6 us (0.977)
  blocking collectives: 49.9 us -> 47.8 us
  starting transfers between devices: 19.9 us -> 21.2 us
  waiting for transfers between devices: 5.79 us -> 4.88 us
    all_to_all x2, blocking collectives: 40.3 us -> 38.2 us  [gathered(): lax.all_to_all(jnp.broadcast_to(tile[None], (count,) + tile.shape), axes,...]
    ppermute x6, starting transfers between devices: 19.9 us -> 21.2 us  [moved(): return lax.ppermute(block, axis, pairs)]
    ppermute x6, waiting for transfers between devices: 5.79 us -> 4.88 us  [moved(): return lax.ppermute(block, axis, pairs)]
    pallas_call x1 -> x2, Pallas kernels: 5.6 us -> 5.35 us  [the longest x1 3.35 us: late_powers(): pl.pallas_call(late_kernel, out_shape=(jax.ShapeDtypeStruct(basis, jnp.fl...]
  transfers between devices with their start and end apart: 6 -> 6, of which waited for: 3 -> 2; matrix products, arithmetic and copies ran while one was open for 0% -> 0% of each run, Pallas kernels for 0% -> 2%
where the time goes in v4:
time: 85.6 us; the launch traced here: 85.2 us
  blocking collectives  47.8 us (56%)
  starting transfers between devices  21.2 us (25%)
  Pallas kernels  9.3 us (11%)
  waiting for transfers between devices  4.88 us (6%)
  other arithmetic  1.2 us (1%)
    all_to_all x2, blocking collectives, gathered(): lax.all_to_all(jnp.broadcast_to(tile[None], (count,) + tile.shape), axes,...  38.2 us
    ppermute x6, starting transfers between devices, moved(): return lax.ppermute(block, axis, pairs)  21.2 us
    all_to_all x1, blocking collectives, vertical(): return lax.all_to_all(sent, 'gz', 0, 0)  9.55 us
    ppermute x6, waiting for transfers between devices, moved(): return lax.ppermute(block, axis, pairs)  4.88 us
    pallas_call x1, Pallas kernels, finish(): pl.pallas_call(finish_kernel, out_shape=(jax.ShapeDtypeStruct((RHS * COMP...  3.62 us
    pallas_call x1, Pallas kernels, late_powers(): pl.pallas_call(late_kernel, out_shape=(jax.ShapeDtypeStruct(basis, jnp.fl...  3.35 us
    pallas_call x1, Pallas kernels, early_powers(): pl.pallas_call(early_kernel, out_shape=[jax.ShapeDtypeStruct(shape, jnp.f...  2.01 us
  transfers between devices with their start and end apart: 6, of which 2 were waited for; matrix products, arithmetic and copies ran while one was open for 0% of the time, Pallas kernels for 2%

profile of v4, /device:TPU:1, one launch (start us, length us, event | category | flops | bytes accessed | tf_op | source)
XLA Modules:
  0.0 85.2 jit_solution(13851350677521501232)
XLA Ops:
  0.6 1.1 %pad_maximum_fusion.raw_ref = f32[784,128]{1,0:T(8,128)S(1)} fusion(f32[16,128]{1,0:T(8,128)} %bitcast.6, f32[256,128]{1,0:T(8,128)} %bitcast.5, f32[512,128]{1,0:T(8,128)} %bitcast.4), kind=kLoop, calls=%fused_computation | loop fusion | flops 200704 | bytes 802816 | tf_op jit(solution)/shard_map/concatenate | solution.py:94
  1.7 0.3 shard_map.50
  2.0 0.1 select_select_fusion
  2.1 9.6 %all_to_all.15 = f32[4,56,128]{2,1,0:T(8,128)S(1)} all-to-all(f32[4,56,128]{2,1,0:T(8,128)S(1)} %select_select_fusion), channel_id=1, replica_groups=mesh['gx'=16,'gy'=8,'gz'=4] {'gz'}, dimensions={0} | all-to-all | bytes 229376 | tf_op jit(solution)/shard_map/all_to_all | solution.py:534
  11.7 0.1 fusion
  11.7 3.6 %collective-permute-start = (f32[776,128]{1,0:T(8,128)S(1)}, f32[776,128]{1,0:T(8,128)S(1)}, u32[]{:S(2)}, u32[]{:S(2)}) collective-permute-start(f32[776,128]{1,0:T(8,128)S(1)} %get-tuple-element.43), channel_id=1, source_target_pairs={{0,32},{32,64},{64,96},{96,128},{128,160},{160,192},{192,224},{224... | collective-permute-start | bytes 1191944 | tf_op jit(solution)/shard_map/ppermute | solution.py:527
  15.3 1.3 %collective-permute-start.1 = (f32[776,128]{1,0:T(8,128)S(1)}, f32[776,128]{1,0:T(8,128)S(1)}, u32[]{:S(2)}, u32[]{:S(2)}) collective-permute-start(f32[776,128]{1,0:T(8,128)S(1)} %get-tuple-element.42), channel_id=1, source_target_pairs={{32,0},{64,32},{96,64},{128,96},{160,128},{192,160},{224,192},{256... | collective-permute-start | bytes 1191944 | tf_op jit(solution)/shard_map/ppermute | solution.py:527
  16.6 5.4 %collective-permute-start.4 = (f32[840,128]{1,0:T(8,128)S(1)}, f32[840,128]{1,0:T(8,128)S(1)}, u32[]{:S(2)}, u32[]{:S(2)}) collective-permute-start(f32[840,128]{1,0:T(8,128)S(1)} %constant_dynamic-update-slice_fusion.refs_0_), channel_id=1, source_target_pairs={{0,4},{4,8},{8,12},{12,16},{16,20},{20,24},{24,28},{1,5},{5,9},{9,... | collective-permute-start | bytes 1290248 | tf_op jit(solution)/shard_map/ppermute | solution.py:527
  22.0 1.9 %collective-permute-start.5 = (f32[840,128]{1,0:T(8,128)S(1)}, f32[840,128]{1,0:T(8,128)S(1)}, u32[]{:S(2)}, u32[]{:S(2)}) collective-permute-start(f32[840,128]{1,0:T(8,128)S(1)} %constant_dynamic-update-slice_fusion.refs_0_), channel_id=1, source_target_pairs={{4,0},{8,4},{12,8},{16,12},{20,16},{24,20},{28,24},{5,1},{9,5},{13... | collective-permute-start | bytes 1290248 | tf_op jit(solution)/shard_map/ppermute | solution.py:527
  23.9 0.0 collective-permute-done.left_ref.refs_1_
  23.9 0.9 %collective-permute-done.1.right_ref.refs_2_ = f32[776,128]{1,0:T(8,128)S(1)} collective-permute-done((f32[776,128]{1,0:T(8,128)S(1)}, f32[776,128]{1,0:T(8,128)S(1)}, u32[]{:S(2)}, u32[]{:S(2)}) %collective-permute-start.1) | collective-permute-done | bytes 397344 | tf_op jit(solution)/shard_map/ppermute | solution.py:527
  24.9 7.1 %collective-permute-start.2 = (f32[552,128]{1,0:T(8,128)S(1)}, f32[552,128]{1,0:T(8,128)S(1)}, u32[]{:S(2)}, u32[]{:S(2)}) collective-permute-start(f32[552,128]{1,0:T(8,128)S(1)} %get-tuple-element.25), channel_id=1, source_target_pairs={{0,4},{4,8},{8,12},{12,16},{16,20},{20,24},{24,28},{1,5},{5,9},{9,... | collective-permute-start | bytes 847880 | tf_op jit(solution)/shard_map/ppermute | solution.py:527
  32.0 1.9 %collective-permute-start.3 = (f32[552,128]{1,0:T(8,128)S(1)}, f32[552,128]{1,0:T(8,128)S(1)}, u32[]{:S(2)}, u32[]{:S(2)}) collective-permute-start(f32[552,128]{1,0:T(8,128)S(1)} %get-tuple-element.26), channel_id=1, source_target_pairs={{4,0},{8,4},{12,8},{16,12},{20,16},{24,20},{28,24},{5,1},{9,5},{13... | collective-permute-start | bytes 847880 | tf_op jit(solution)/shard_map/ppermute | solution.py:527
  34.0 0.0 collective-permute-done.4.refs_3_
  34.0 0.0 collective-permute-done.5.refs_4_
  34.0 2.0 %shard_map.52 = (f32[320,8,128]{2,1,0:T(8,128)S(1)}, f32[320,8,128]{2,1,0:T(8,128)S(1)}, f32[320,8,128]{2,1,0:T(8,128)S(1)}, f32[320,8,128]{2,1,0:T(8,128)S(1)},...) custom-call(f32[840,128]{1,0:T(8,128)S(1)} %constant_dynamic-update-, ...), custom_call_target="tpu_custom_call" | custom-call | flops 5000000 | bytes 8000000 | tf_op jit(solution)/shard_map/pallas_call | solution.py:388
  36.0 0.0 collective-permute-done.2.refs_0_
  36.0 3.9 %collective-permute-done.3.refs_1_ = f32[552,128]{1,0:T(8,128)S(1)} collective-permute-done((f32[552,128]{1,0:T(8,128)S(1)}, f32[552,128]{1,0:T(8,128)S(1)}, u32[]{:S(2)}, u32[]{:S(2)}) %collective-permute-start.3) | collective-permute-done | bytes 282656 | tf_op jit(solution)/shard_map/ppermute | solution.py:527
  40.0 3.3 %shard_map.53 = (f32[64,40,128]{2,1,0:T(8,128)S(1)}, f32[8,128]{1,0:T(8,128)S(1)}) custom-call(f32[552,128]{1,0:T(8,128)S(1)} %collective-permute-done.2.refs_0_, f32[552,128]{1,0:T(8,128)S(1)} %collective-permute-done.3.refs_1_, f32[320,8,128]{2,1,0:T(8,128)S(1)} %get-tuple-element.27.refs_2_, f32[320,8,128]{2,1,0:T(8,128)S(1)} %get-tuple-element.28.refs_3_, ...), custom_call_target="tpu_custom_call" | custom-call | tf_op jit(solution)/shard_map/pallas_call | solution.py:402
  43.3 12.3 %all_to_all.16 = f32[32,8,128]{2,1,0:T(8,128)S(1)} all-to-all(f32[32,8,128]{2,1,0:T(8,128)S(1)} %broadcast_in_dim.56), channel_id=1, replica_groups=mesh['gx'=16,'gy'=8,'gz'=4] {'gy','gz'}, dimensions={0} | all-to-all | bytes 262144 | tf_op jit(solution)/shard_map/all_to_all | solution.py:539
  55.6 26.0 %all_to_all.17.gram_ref = f32[16,8,128]{2,1,0:T(8,128)S(1)} all-to-all(f32[16,8,128]{2,1,0:T(8,128)S(1)} %broadcast_in_dim.57), channel_id=1, replica_groups=mesh['gx'=16,'gy'=8,'gz'=4] {'gx'}, dimensions={0} | all-to-all | bytes 131072 | tf_op jit(solution)/shard_map/all_to_all | solution.py:539
  81.6 3.6 %shard_map.54 = (f32[512,128]{1,0:T(8,128)}, f32[40,40]{1,0:T(8,128)}) custom-call(f32[16,8,128]{2,1,0:T(8,128)S(1)} %all_to_all.17.gram_ref, f32[64,40,128]{2,1,0:T(8,128)S(1)} %get-tuple-element.39.basis_ref), custom_call_target="tpu_custom_call" | custom-call | tf_op jit(solution)/shard_map/pallas_call | solution.py:508
  (7 shorter events, 0.1 us)
Async XLA Ops:
  11.7 12.2 %collective-permute-start = (f32[776,128]{1,0:T(8,128)S(1)}, f32[776,128]{1,0:T(8,128)S(1)}, u32[]{:S(2)}, u32[]{:S(2)}) collective-permute-start(f32[776,128]{1,0:T(8,128)S(1)} %get-tuple-element.43), channel_id=1, source_target_pairs={{0,32},{32,64},{64,96},{96,128},{128,160},{160,192},{192,224},{224... | collective-permute-start | bytes 1191944 | tf_op jit(solution)/shard_map/ppermute | solution.py:527
  15.3 9.6 %collective-permute-start.1 = (f32[776,128]{1,0:T(8,128)S(1)}, f32[776,128]{1,0:T(8,128)S(1)}, u32[]{:S(2)}, u32[]{:S(2)}) collective-permute-start(f32[776,128]{1,0:T(8,128)S(1)} %get-tuple-element.42), channel_id=1, source_target_pairs={{32,0},{64,32},{96,64},{128,96},{160,128},{192,160},{224,192},{256... | collective-permute-start | bytes 1191944 | tf_op jit(solution)/shard_map/ppermute | solution.py:527
  16.6 17.4 %collective-permute-start.4 = (f32[840,128]{1,0:T(8,128)S(1)}, f32[840,128]{1,0:T(8,128)S(1)}, u32[]{:S(2)}, u32[]{:S(2)}) collective-permute-start(f32[840,128]{1,0:T(8,128)S(1)} %constant_dynamic-update-slice_fusion.refs_0_), channel_id=1, source_target_pairs={{0,4},{4,8},{8,12},{12,16},{16,20},{20,24},{24,28},{1,5},{5,9},{9,... | collective-permute-start | bytes 1290248 | tf_op jit(solution)/shard_map/ppermute | solution.py:527
  22.0 12.0 %collective-permute-start.5 = (f32[840,128]{1,0:T(8,128)S(1)}, f32[840,128]{1,0:T(8,128)S(1)}, u32[]{:S(2)}, u32[]{:S(2)}) collective-permute-start(f32[840,128]{1,0:T(8,128)S(1)} %constant_dynamic-update-slice_fusion.refs_0_), channel_id=1, source_target_pairs={{4,0},{8,4},{12,8},{16,12},{20,16},{24,20},{28,24},{5,1},{9,5},{13... | collective-permute-start | bytes 1290248 | tf_op jit(solution)/shard_map/ppermute | solution.py:527
  24.9 11.1 %collective-permute-start.2 = (f32[552,128]{1,0:T(8,128)S(1)}, f32[552,128]{1,0:T(8,128)S(1)}, u32[]{:S(2)}, u32[]{:S(2)}) collective-permute-start(f32[552,128]{1,0:T(8,128)S(1)} %get-tuple-element.25), channel_id=1, source_target_pairs={{0,4},{4,8},{8,12},{12,16},{16,20},{20,24},{24,28},{1,5},{5,9},{9,... | collective-permute-start | bytes 847880 | tf_op jit(solution)/shard_map/ppermute | solution.py:527
  32.0 7.9 %collective-permute-start.3 = (f32[552,128]{1,0:T(8,128)S(1)}, f32[552,128]{1,0:T(8,128)S(1)}, u32[]{:S(2)}, u32[]{:S(2)}) collective-permute-start(f32[552,128]{1,0:T(8,128)S(1)} %get-tuple-element.26), channel_id=1, source_target_pairs={{4,0},{8,4},{12,8},{16,12},{20,16},{24,20},{28,24},{5,1},{9,5},{13... | collective-permute-start | bytes 847880 | tf_op jit(solution)/shard_map/ppermute | solution.py:527

commit v5 on v4

--- a/solution.py
+++ b/solution.py
@@ -521,10 +521,14 @@
     )(gram, basis)
 
 
-def moved(block, axis, step):
+def swapped(first, second, axis):
     count = lax.axis_size(axis)
-    pairs = [(i, i + step) for i in range(count) if 0 <= i + step < count]
-    return lax.ppermute(block, axis, pairs)
+    odd = lax.axis_index(axis) % 2 == 1
+    inner = [(i, i ^ 1) for i in range(count)]
+    outer = [(i, ((i + 1) ^ 1) - 1) for i in range(1, count - 1)]
+    one = lax.ppermute(first(odd), axis, inner)
+    two = lax.ppermute(second(odd), axis, outer)
+    return jnp.where(odd, one, two), jnp.where(odd, two, one)
 
 
 def vertical(low, high):
@@ -543,10 +547,16 @@
     block, low, high = pack(residuals, shear_rate, coupling)
     ghosts = jnp.sum(vertical(low, high), axis=0)
     own = lax.dynamic_update_slice(block, ghosts, (GHOST_AT, 0))
-    left, right = moved(own[LAYER:], "gx", 1), moved(own[:SIDE_ROWS], "gx", -1)
-    front, back = moved(own, "gy", 1), moved(own, "gy", -1)
+    left, right = swapped(
+        lambda odd: jnp.where(odd, own[:SIDE_ROWS], own[LAYER:]),
+        lambda odd: jnp.where(odd, own[LAYER:], own[:SIDE_ROWS]),
+        "gx",
+    )
+    front, back = swapped(lambda odd: own, lambda odd: own, "gy")
     down, up = corners(left, right)
-    low_corner, high_corner = moved(up, "gy", 1), moved(down, "gy", -1)
+    low_corner, high_corner = swapped(
+        lambda odd: jnp.where(odd, down, up), lambda odd: jnp.where(odd, up, down), "gy"
+    )
     state = early_powers(own, left, right, front, back)
     basis, gram = late_powers(low_corner, high_corner, state)
     gram = jnp.sum(gathered(gram, ("gy", "gz")), axis=0)

time: 85.6 us -> 86.3 us (level)
  blocking collectives: 47.8 us -> 40.2 us
  waiting for transfers between devices: 4.88 us -> 8.62 us
  starting transfers between devices: 21.2 us -> 24.8 us
  other arithmetic: 1.2 us -> 2.09 us
    all_to_all x1 -> x0, blocking collectives: 9.55 us -> none  [vertical(): return lax.all_to_all(sent, 'gz', 0, 0)]
    all_to_all x0 -> x1, starting transfers between devices: none -> 5.01 us  [vertical(): return lax.all_to_all(sent, 'gz', 0, 0)]
    all_to_all x0 -> x1, waiting for transfers between devices: none -> 4.74 us  [vertical(): return lax.all_to_all(sent, 'gz', 0, 0)]
    all_to_all x2, blocking collectives: 38.2 us -> 40.2 us  [gathered(): lax.all_to_all(jnp.broadcast_to(tile[None], (count,) + tile.shape), axes,...]
    ppermute x6, starting transfers between devices: 21.2 us -> 19.8 us  [the longest x3 15.3 us: swapped(): one = lax.ppermute(first(odd), axis, inner)]
    ppermute x6, waiting for transfers between devices: 4.88 us -> 3.88 us  [the longest x3 3.88 us: swapped(): two = lax.ppermute(second(odd), axis, outer)]
  transfers between devices with their start and end apart: 6 -> 7, of which waited for: 2 -> 3; matrix products, arithmetic and copies ran while one was open for 0% -> 0% of each run, Pallas kernels for 2% -> 2%
where the time goes in v5:
time: 86.3 us; the launch traced here: 85.8 us
  blocking collectives  40.2 us (47%)
  starting transfers between devices  24.8 us (29%)
  Pallas kernels  9.32 us (11%)
  waiting for transfers between devices  8.62 us (10%)
  other arithmetic  2.09 us (2%)
    all_to_all x2, blocking collectives, gathered(): lax.all_to_all(jnp.broadcast_to(tile[None], (count,) + tile.shape), axes,...  40.2 us
    ppermute x3, starting transfers between devices, swapped(): one = lax.ppermute(first(odd), axis, inner)  15.3 us
    all_to_all x1, starting transfers between devices, vertical(): return lax.all_to_all(sent, 'gz', 0, 0)  5.01 us
    all_to_all x1, waiting for transfers between devices, vertical(): return lax.all_to_all(sent, 'gz', 0, 0)  4.74 us
    ppermute x3, starting transfers between devices, swapped(): two = lax.ppermute(second(odd), axis, outer)  4.53 us
    ppermute x3, waiting for transfers between devices, swapped(): two = lax.ppermute(second(odd), axis, outer)  3.88 us
    pallas_call x1, Pallas kernels, finish(): pl.pallas_call(finish_kernel, out_shape=(jax.ShapeDtypeStruct((RHS * COMP...  3.62 us
    pallas_call x1, Pallas kernels, late_powers(): pl.pallas_call(late_kernel, out_shape=(jax.ShapeDtypeStruct(basis, jnp.fl...  3.35 us
  transfers between devices with their start and end apart: 7, of which 3 were waited for; matrix products, arithmetic and copies ran while one was open for 0% of the time, Pallas kernels for 2%

profile of v5, /device:TPU:1, one launch (start us, length us, event | category | flops | bytes accessed | tf_op | source)
XLA Modules:
  0.0 85.8 jit_solution(628755214663127979)
XLA Ops:
  0.6 1.1 %pad_maximum_fusion.raw_ref = f32[784,128]{1,0:T(8,128)S(1)} fusion(f32[16,128]{1,0:T(8,128)} %bitcast.6, f32[256,128]{1,0:T(8,128)} %bitcast.5, f32[512,128]{1,0:T(8,128)} %bitcast.4), kind=kLoop, calls=%fused_computation | loop fusion | flops 200704 | bytes 802816 | tf_op jit(solution)/shard_map/concatenate | solution.py:94
  1.7 0.3 shard_map.50
  2.0 0.7 select_select_fusion
  2.7 5.0 %all-to-all-start = ((f32[4,56,128]{2,1,0:T(8,128)}), f32[4,56,128]{2,1,0:T(8,128)S(1)}, u32[]{:S(2)}, u32[]{:S(2)}) async-start(f32[4,56,128]{2,1,0:T(8,128)} %select_select_fusion), calls=%async_computation | async-start | bytes 229376 | tf_op jit(solution)/shard_map/all_to_all | solution.py:538
  7.7 4.7 %all-to-all-done = f32[4,56,128]{2,1,0:T(8,128)S(1)} async-done(((f32[4,56,128]{2,1,0:T(8,128)}), f32[4,56,128]{2,1,0:T(8,128)S(1)}, u32[]{:S(2)}, u32[]{:S(2)}) %all-to-all-start) | async-done | bytes 114720 | tf_op jit(solution)/shard_map/all_to_all | solution.py:538
  12.5 0.1 slice_select_fusion
  12.6 3.5 %collective-permute-start = (f32[776,128]{1,0:T(8,128)S(1)}, f32[776,128]{1,0:T(8,128)S(1)}, u32[]{:S(2)}, u32[]{:S(2)}) collective-permute-start(f32[776,128]{1,0:T(8,128)S(1)} %get-tuple-element.51), channel_id=1, source_target_pairs={{0,32},{32,0},{64,96},{96,64},{128,160},{160,128},{192,224},{224,1... | collective-permute-start | bytes 1191944 | tf_op jit(solution)/shard_map/ppermute | solution.py:529
  16.1 0.7 collective-permute-start.1
  16.8 6.6 %collective-permute-start.4 = (f32[840,128]{1,0:T(8,128)S(1)}, f32[840,128]{1,0:T(8,128)S(1)}, u32[]{:S(2)}, u32[]{:S(2)}) collective-permute-start(f32[840,128]{1,0:T(8,128)S(1)} %constant_dynamic-update-slice_fusion.refs_0_), channel_id=1, source_target_pairs={{0,4},{4,0},{8,12},{12,8},{16,20},{20,16},{24,28},{28,24},{1,5},{5... | collective-permute-start | bytes 1290248 | tf_op jit(solution)/shard_map/ppermute | solution.py:529
  23.4 1.9 %collective-permute-start.5 = (f32[840,128]{1,0:T(8,128)S(1)}, f32[840,128]{1,0:T(8,128)S(1)}, u32[]{:S(2)}, u32[]{:S(2)}) collective-permute-start(f32[840,128]{1,0:T(8,128)S(1)} %constant_dynamic-update-slice_fusion.refs_0_), channel_id=1, source_target_pairs={{4,8},{8,4},{12,16},{16,12},{20,24},{24,20},{5,9},{9,5},{13,17},{1... | collective-permute-start | bytes 1290248 | tf_op jit(solution)/shard_map/ppermute | solution.py:530
  25.4 0.0 collective-permute-done
  25.4 0.0 collective-permute-done.1
  25.4 0.1 broadcast_select_fusion.2
  25.4 0.1 shard_map.51
  25.5 5.1 %collective-permute-start.2 = (f32[552,128]{1,0:T(8,128)S(1)}, f32[552,128]{1,0:T(8,128)S(1)}, u32[]{:S(2)}, u32[]{:S(2)}) collective-permute-start(f32[552,128]{1,0:T(8,128)S(1)} %get-tuple-element.49), channel_id=1, source_target_pairs={{0,4},{4,0},{8,12},{12,8},{16,20},{20,16},{24,28},{28,24},{1,5},{5... | collective-permute-start | bytes 847880 | tf_op jit(solution)/shard_map/ppermute | solution.py:529
  30.7 1.9 %collective-permute-start.3 = (f32[552,128]{1,0:T(8,128)S(1)}, f32[552,128]{1,0:T(8,128)S(1)}, u32[]{:S(2)}, u32[]{:S(2)}) collective-permute-start(f32[552,128]{1,0:T(8,128)S(1)} %get-tuple-element.48), channel_id=1, source_target_pairs={{4,8},{8,4},{12,16},{16,12},{20,24},{24,20},{5,9},{9,5},{13,17},{1... | collective-permute-start | bytes 847880 | tf_op jit(solution)/shard_map/ppermute | solution.py:530
  32.6 0.0 collective-permute-done.4
  32.6 0.3 collective-permute-done.5
  32.9 0.1 broadcast_select_fusion
  33.0 2.0 %shard_map.52 = (f32[320,8,128]{2,1,0:T(8,128)S(1)}, f32[320,8,128]{2,1,0:T(8,128)S(1)}, f32[320,8,128]{2,1,0:T(8,128)S(1)}, f32[320,8,128]{2,1,0:T(8,128)S(1)},...) custom-call(f32[840,128]{1,0:T(8,128)S(1)} %constant_dynamic-update-, ...), custom_call_target="tpu_custom_call" | custom-call | flops 5000000 | bytes 8000000 | tf_op jit(solution)/shard_map/pallas_call | solution.py:388
  35.0 0.0 collective-permute-done.2
  35.0 3.6 %collective-permute-done.3 = f32[552,128]{1,0:T(8,128)S(1)} collective-permute-done((f32[552,128]{1,0:T(8,128)S(1)}, f32[552,128]{1,0:T(8,128)S(1)}, u32[]{:S(2)}, u32[]{:S(2)}) %collective-permute-start.3) | collective-permute-done | bytes 282656 | tf_op jit(solution)/shard_map/ppermute | solution.py:530
  38.6 3.3 %shard_map.53 = (f32[64,40,128]{2,1,0:T(8,128)S(1)}, f32[8,128]{1,0:T(8,128)S(1)}) custom-call(f32[552,128]{1,0:T(8,128)S(1)} %get-tuple-element.47.refs_0_, f32[552,128]{1,0:T(8,128)S(1)} %get-tuple-element.46.refs_1_, f32[320,8,128]{2,1,0:T(8,128)S(1)} %get-tuple-element.27.refs_2_, f32[320,8,128]{2,1,0:T(8,128)S(1)} %get-tuple-element.28.refs_3_, ...), custom_call_target="tpu_custom_call" | custom-call | tf_op jit(solution)/shard_map/pallas_call | solution.py:402
  42.0 10.2 %all_to_all.15 = f32[32,8,128]{2,1,0:T(8,128)S(1)} all-to-all(f32[32,8,128]{2,1,0:T(8,128)S(1)} %broadcast_in_dim.56), channel_id=1, replica_groups=mesh['gx'=16,'gy'=8,'gz'=4] {'gy','gz'}, dimensions={0} | all-to-all | bytes 262144 | tf_op jit(solution)/shard_map/all_to_all | solution.py:543
  52.3 30.0 %all_to_all.16.gram_ref = f32[16,8,128]{2,1,0:T(8,128)S(1)} all-to-all(f32[16,8,128]{2,1,0:T(8,128)S(1)} %broadcast_in_dim.57), channel_id=1, replica_groups=mesh['gx'=16,'gy'=8,'gz'=4] {'gx'}, dimensions={0} | all-to-all | bytes 131072 | tf_op jit(solution)/shard_map/all_to_all | solution.py:543
  82.2 3.6 %shard_map.54 = (f32[512,128]{1,0:T(8,128)}, f32[40,40]{1,0:T(8,128)}) custom-call(f32[16,8,128]{2,1,0:T(8,128)S(1)} %all_to_all.16.gram_ref, f32[64,40,128]{2,1,0:T(8,128)S(1)} %get-tuple-element.39.basis_ref), custom_call_target="tpu_custom_call" | custom-call | tf_op jit(solution)/shard_map/pallas_call | solution.py:508
  (8 shorter events, 0.2 us)
Async XLA Ops:
  2.7 9.8 %all-to-all-start = ((f32[4,56,128]{2,1,0:T(8,128)}), f32[4,56,128]{2,1,0:T(8,128)S(1)}, u32[]{:S(2)}, u32[]{:S(2)}) async-start(f32[4,56,128]{2,1,0:T(8,128)} %select_select_fusion), calls=%async_computation | async-start | bytes 229376 | tf_op jit(solution)/shard_map/all_to_all | solution.py:538
  12.6 12.8 %collective-permute-start = (f32[776,128]{1,0:T(8,128)S(1)}, f32[776,128]{1,0:T(8,128)S(1)}, u32[]{:S(2)}, u32[]{:S(2)}) collective-permute-start(f32[776,128]{1,0:T(8,128)S(1)} %get-tuple-element.51), channel_id=1, source_target_pairs={{0,32},{32,0},{64,96},{96,64},{128,160},{160,128},{192,224},{224,1... | collective-permute-start | bytes 1191944 | tf_op jit(solution)/shard_map/ppermute | solution.py:529
  16.1 9.2 %collective-permute-start.1 = (f32[776,128]{1,0:T(8,128)S(1)}, f32[776,128]{1,0:T(8,128)S(1)}, u32[]{:S(2)}, u32[]{:S(2)}) collective-permute-start(f32[776,128]{1,0:T(8,128)S(1)} %get-tuple-element.50), channel_id=1, source_target_pairs={{32,64},{64,32},{96,128},{128,96},{160,192},{192,160},{224,256},{2... | collective-permute-start | bytes 1191944 | tf_op jit(solution)/shard_map/ppermute | solution.py:530
  16.8 15.8 %collective-permute-start.4 = (f32[840,128]{1,0:T(8,128)S(1)}, f32[840,128]{1,0:T(8,128)S(1)}, u32[]{:S(2)}, u32[]{:S(2)}) collective-permute-start(f32[840,128]{1,0:T(8,128)S(1)} %constant_dynamic-update-slice_fusion.refs_0_), channel_id=1, source_target_pairs={{0,4},{4,0},{8,12},{12,8},{16,20},{20,16},{24,28},{28,24},{1,5},{5... | collective-permute-start | bytes 1290248 | tf_op jit(solution)/shard_map/ppermute | solution.py:529
  23.4 9.5 %collective-permute-start.5 = (f32[840,128]{1,0:T(8,128)S(1)}, f32[840,128]{1,0:T(8,128)S(1)}, u32[]{:S(2)}, u32[]{:S(2)}) collective-permute-start(f32[840,128]{1,0:T(8,128)S(1)} %constant_dynamic-update-slice_fusion.refs_0_), channel_id=1, source_target_pairs={{4,8},{8,4},{12,16},{16,12},{20,24},{24,20},{5,9},{9,5},{13,17},{1... | collective-permute-start | bytes 1290248 | tf_op jit(solution)/shard_map/ppermute | solution.py:530
  25.5 9.5 %collective-permute-start.2 = (f32[552,128]{1,0:T(8,128)S(1)}, f32[552,128]{1,0:T(8,128)S(1)}, u32[]{:S(2)}, u32[]{:S(2)}) collective-permute-start(f32[552,128]{1,0:T(8,128)S(1)} %get-tuple-element.49), channel_id=1, source_target_pairs={{0,4},{4,0},{8,12},{12,8},{16,20},{20,16},{24,28},{28,24},{1,5},{5... | collective-permute-start | bytes 847880 | tf_op jit(solution)/shard_map/ppermute | solution.py:529
  30.7 7.9 %collective-permute-start.3 = (f32[552,128]{1,0:T(8,128)S(1)}, f32[552,128]{1,0:T(8,128)S(1)}, u32[]{:S(2)}, u32[]{:S(2)}) collective-permute-start(f32[552,128]{1,0:T(8,128)S(1)} %get-tuple-element.48), channel_id=1, source_target_pairs={{4,8},{8,4},{12,16},{16,12},{20,24},{24,20},{5,9},{9,5},{13,17},{1... | collective-permute-start | bytes 847880 | tf_op jit(solution)/shard_map/ppermute | solution.py:530

commit v6 on v4

--- a/solution.py
+++ b/solution.py
@@ -527,11 +527,22 @@
     return lax.ppermute(block, axis, pairs)
 
 
+def swapped(to_low, to_high, axis, even):
+    count = lax.axis_size(axis)
+    inner = [(i, i ^ 1) for i in range(count)]
+    outer = [(i, ((i + 1) ^ 1) - 1) for i in range(1, count - 1)]
+    two = lax.ppermute(jnp.where(even, to_low, to_high), axis, outer)
+    one = lax.ppermute(jnp.where(even, to_high, to_low), axis, inner)
+    return jnp.where(even, two, one), jnp.where(even, one, two)
+
+
 def vertical(low, high):
     count, place = lax.axis_size("gz"), lax.axis_index("gz")
     index = jnp.arange(count)[:, None, None]
     sent = jnp.where(index == place + 1, high[None], jnp.where(index == place - 1, low[None], 0.0))
-    return lax.all_to_all(sent, "gz", 0, 0)
+    even = [lax.axis_index(axis) % 2 == 0 for axis in ("gx", "gy")]
+    sent, even = lax.optimization_barrier((sent, even))
+    return lax.all_to_all(sent, "gz", 0, 0), even
 
 
 def gathered(tile, axes):
@@ -541,12 +552,12 @@
 
 def local(residuals, shear_rate, coupling):
     block, low, high = pack(residuals, shear_rate, coupling)
-    ghosts = jnp.sum(vertical(low, high), axis=0)
-    own = lax.dynamic_update_slice(block, ghosts, (GHOST_AT, 0))
-    left, right = moved(own[LAYER:], "gx", 1), moved(own[:SIDE_ROWS], "gx", -1)
+    received, (even_x, even_y) = vertical(low, high)
+    own = lax.dynamic_update_slice(block, jnp.sum(received, axis=0), (GHOST_AT, 0))
+    left, right = swapped(own[:SIDE_ROWS], own[LAYER:], "gx", even_x)
     front, back = moved(own, "gy", 1), moved(own, "gy", -1)
     down, up = corners(left, right)
-    low_corner, high_corner = moved(up, "gy", 1), moved(down, "gy", -1)
+    low_corner, high_corner = swapped(down, up, "gy", even_y)
     state = early_powers(own, left, right, front, back)
     basis, gram = late_powers(low_corner, high_corner, state)
     gram = jnp.sum(gathered(gram, ("gy", "gz")), axis=0)

time: 85.6 us -> 81.8 us (0.956)
  waiting for transfers between devices: 4.88 us -> 0.87 us
  blocking collectives: 47.8 us -> 46.8 us
  starting transfers between devices: 21.2 us -> 22.1 us
    ppermute x0 -> x4, starting transfers between devices: none -> 14.5 us  [the longest x2 8.33 us: swapped(): one = lax.ppermute(jnp.where(even, to_high, to_low), axis, inner)]
    ppermute x6 -> x2, starting transfers between devices: 21.2 us -> 7.59 us  [moved(): return lax.ppermute(block, axis, pairs)]
    ppermute x6 -> x2, waiting for transfers between devices: 4.88 us -> 0.01 us  [moved(): return lax.ppermute(block, axis, pairs)]
    all_to_all x2, blocking collectives: 38.2 us -> 37.2 us  [gathered(): lax.all_to_all(jnp.broadcast_to(tile[None], (count,) + tile.shape), axes,...]
    ppermute x0 -> x4, waiting for transfers between devices: none -> 0.86 us  [the longest x2 0.86 us: swapped(): two = lax.ppermute(jnp.where(even, to_low, to_high), axis, outer)]
  transfers between devices with their start and end apart: 6 -> 6, of which waited for: 2 -> 1; matrix products, arithmetic and copies ran while one was open for 0% -> 0% of each run, Pallas kernels for 2% -> 3%
where the time goes in v6:
time: 81.8 us; the launch traced here: 81.4 us
  blocking collectives  46.8 us (57%)
  starting transfers between devices  22.1 us (27%)
  Pallas kernels  9.44 us (12%)
  other arithmetic  1.39 us (2%)
  waiting for transfers between devices  0.87 us (1%)
  between operations  0.82 us (1%)
    all_to_all x2, blocking collectives, gathered(): lax.all_to_all(jnp.broadcast_to(tile[None], (count,) + tile.shape), axes,...  37.2 us
    all_to_all x1, blocking collectives, vertical(): return (lax.all_to_all(sent, 'gz', 0, 0), even)  9.55 us
    ppermute x2, starting transfers between devices, swapped(): one = lax.ppermute(jnp.where(even, to_high, to_low), axis, inner)  8.33 us
    ppermute x2, starting transfers between devices, moved(): return lax.ppermute(block, axis, pairs)  7.59 us
    ppermute x2, starting transfers between devices, swapped(): two = lax.ppermute(jnp.where(even, to_low, to_high), axis, outer)  6.2 us
    pallas_call x1, Pallas kernels, finish(): pl.pallas_call(finish_kernel, out_shape=(jax.ShapeDtypeStruct((RHS * COMP...  3.62 us
    pallas_call x1, Pallas kernels, late_powers(): pl.pallas_call(late_kernel, out_shape=(jax.ShapeDtypeStruct(basis, jnp.fl...  3.42 us
    pallas_call x1, Pallas kernels, early_powers(): pl.pallas_call(early_kernel, out_shape=[jax.ShapeDtypeStruct(shape, jnp.f...  2.07 us
  transfers between devices with their start and end apart: 6, of which 1 were waited for; matrix products, arithmetic and copies ran while one was open for 0% of the time, Pallas kernels for 3%

profile of v6, /device:TPU:1, one launch (start us, length us, event | category | flops | bytes accessed | tf_op | source)
XLA Modules:
  0.0 81.4 jit_solution(8214481347969633092)
XLA Ops:
  0.7 1.1 %pad_maximum_fusion.raw_ref = f32[784,128]{1,0:T(8,128)S(1)} fusion(f32[16,128]{1,0:T(8,128)} %bitcast.6, f32[256,128]{1,0:T(8,128)} %bitcast.5, f32[512,128]{1,0:T(8,128)} %bitcast.4), kind=kLoop, calls=%fused_computation | loop fusion | flops 200704 | bytes 802816 | tf_op jit(solution)/shard_map/concatenate | solution.py:94
  1.7 0.3 shard_map.50
  2.0 0.1 select_select_fusion
  2.1 9.6 %all_to_all.15 = f32[4,56,128]{2,1,0:T(8,128)S(1)} all-to-all(f32[4,56,128]{2,1,0:T(8,128)S(1)} %select_select_fusion), channel_id=1, replica_groups=mesh['gx'=16,'gy'=8,'gz'=4] {'gz'}, dimensions={0} | all-to-all | bytes 229376 | tf_op jit(solution)/shard_map/all_to_all | solution.py:545
  11.7 0.1 slice_select_fusion
  11.8 0.7 collective-permute-start
  12.4 6.4 %collective-permute-start.1 = (f32[776,128]{1,0:T(8,128)S(1)}, f32[776,128]{1,0:T(8,128)S(1)}, u32[]{:S(2)}, u32[]{:S(2)}) collective-permute-start(f32[776,128]{1,0:T(8,128)S(1)} %get-tuple-element.54), channel_id=1, source_target_pairs={{0,32},{32,0},{64,96},{96,64},{128,160},{160,128},{192,224},{224,1... | collective-permute-start | bytes 1191944 | tf_op jit(solution)/shard_map/ppermute | solution.py:535
  18.9 5.7 %collective-permute-start.4 = (f32[840,128]{1,0:T(8,128)S(1)}, f32[840,128]{1,0:T(8,128)S(1)}, u32[]{:S(2)}, u32[]{:S(2)}) collective-permute-start(f32[840,128]{1,0:T(8,128)S(1)} %constant_dynamic-update-slice_fusion.refs_0_), channel_id=1, source_target_pairs={{0,4},{4,8},{8,12},{12,16},{16,20},{20,24},{24,28},{1,5},{5,9},{9,... | collective-permute-start | bytes 1290248 | tf_op jit(solution)/shard_map/ppermute | solution.py:527
  24.5 1.9 %collective-permute-start.5 = (f32[840,128]{1,0:T(8,128)S(1)}, f32[840,128]{1,0:T(8,128)S(1)}, u32[]{:S(2)}, u32[]{:S(2)}) collective-permute-start(f32[840,128]{1,0:T(8,128)S(1)} %constant_dynamic-update-slice_fusion.refs_0_), channel_id=1, source_target_pairs={{4,0},{8,4},{12,8},{16,12},{20,16},{24,20},{28,24},{5,1},{9,5},{13... | collective-permute-start | bytes 1290248 | tf_op jit(solution)/shard_map/ppermute | solution.py:527
  26.5 0.0 collective-permute-done
  26.5 0.0 collective-permute-done.1
  26.5 0.1 broadcast_select_fusion
  26.6 0.1 shard_map.51
  26.7 5.5 %collective-permute-start.2 = (f32[552,128]{1,0:T(8,128)S(1)}, f32[552,128]{1,0:T(8,128)S(1)}, u32[]{:S(2)}, u32[]{:S(2)}) collective-permute-start(f32[552,128]{1,0:T(8,128)S(1)} %get-tuple-element.53), channel_id=1, source_target_pairs={{4,8},{8,4},{12,16},{16,12},{20,24},{24,20},{5,9},{9,5},{13,17},{1... | collective-permute-start | bytes 847880 | tf_op jit(solution)/shard_map/ppermute | solution.py:534
  32.2 1.9 %collective-permute-start.3 = (f32[552,128]{1,0:T(8,128)S(1)}, f32[552,128]{1,0:T(8,128)S(1)}, u32[]{:S(2)}, u32[]{:S(2)}) collective-permute-start(f32[552,128]{1,0:T(8,128)S(1)} %get-tuple-element.52), channel_id=1, source_target_pairs={{0,4},{4,0},{8,12},{12,8},{16,20},{20,16},{24,28},{28,24},{1,5},{5... | collective-permute-start | bytes 847880 | tf_op jit(solution)/shard_map/ppermute | solution.py:535
  34.1 0.0 collective-permute-done.4.refs_3_
  34.1 0.0 collective-permute-done.5.refs_4_
  34.1 2.1 %shard_map.52 = (f32[320,8,128]{2,1,0:T(8,128)S(1)}, f32[320,8,128]{2,1,0:T(8,128)S(1)}, f32[320,8,128]{2,1,0:T(8,128)S(1)}, f32[320,8,128]{2,1,0:T(8,128)S(1)},...) custom-call(f32[840,128]{1,0:T(8,128)S(1)} %constant_dynamic-update-, ...), custom_call_target="tpu_custom_call" | custom-call | flops 5000000 | bytes 8000000 | tf_op jit(solution)/shard_map/pallas_call | solution.py:388
  36.2 0.9 %collective-permute-done.2 = f32[552,128]{1,0:T(8,128)S(1)} collective-permute-done((f32[552,128]{1,0:T(8,128)S(1)}, f32[552,128]{1,0:T(8,128)S(1)}, u32[]{:S(2)}, u32[]{:S(2)}) %collective-permute-start.2) | collective-permute-done | bytes 282656 | tf_op jit(solution)/shard_map/ppermute | solution.py:534
  37.1 0.0 collective-permute-done.3
  37.1 3.4 %shard_map.53 = (f32[64,40,128]{2,1,0:T(8,128)S(1)}, f32[8,128]{1,0:T(8,128)S(1)}) custom-call(f32[552,128]{1,0:T(8,128)S(1)} %get-tuple-element.51.refs_0_, f32[552,128]{1,0:T(8,128)S(1)} %get-tuple-element.50.refs_1_, f32[320,8,128]{2,1,0:T(8,128)S(1)} %get-tuple-element.33.refs_2_, f32[320,8,128]{2,1,0:T(8,128)S(1)} %get-tuple-element.34.refs_3_, ...), custom_call_target="tpu_custom_call" | custom-call | tf_op jit(solution)/shard_map/pallas_call | solution.py:402
  40.5 12.5 %all_to_all.16 = f32[32,8,128]{2,1,0:T(8,128)S(1)} all-to-all(f32[32,8,128]{2,1,0:T(8,128)S(1)} %broadcast_in_dim.56), channel_id=1, replica_groups=mesh['gx'=16,'gy'=8,'gz'=4] {'gy','gz'}, dimensions={0} | all-to-all | bytes 262144 | tf_op jit(solution)/shard_map/all_to_all | solution.py:550
  53.0 24.8 %all_to_all.17.gram_ref = f32[16,8,128]{2,1,0:T(8,128)S(1)} all-to-all(f32[16,8,128]{2,1,0:T(8,128)S(1)} %broadcast_in_dim.57), channel_id=1, replica_groups=mesh['gx'=16,'gy'=8,'gz'=4] {'gx'}, dimensions={0} | all-to-all | bytes 131072 | tf_op jit(solution)/shard_map/all_to_all | solution.py:550
  77.8 3.6 %shard_map.54 = (f32[512,128]{1,0:T(8,128)}, f32[40,40]{1,0:T(8,128)}) custom-call(f32[16,8,128]{2,1,0:T(8,128)S(1)} %all_to_all.17.gram_ref, f32[64,40,128]{2,1,0:T(8,128)S(1)} %get-tuple-element.45.basis_ref), custom_call_target="tpu_custom_call" | custom-call | tf_op jit(solution)/shard_map/pallas_call | solution.py:508
  (8 shorter events, 0.2 us)
Async XLA Ops:
  11.8 14.7 %collective-permute-start = (f32[776,128]{1,0:T(8,128)S(1)}, f32[776,128]{1,0:T(8,128)S(1)}, u32[]{:S(2)}, u32[]{:S(2)}) collective-permute-start(f32[776,128]{1,0:T(8,128)S(1)} %get-tuple-element.55), channel_id=1, source_target_pairs={{32,64},{64,32},{96,128},{128,96},{160,192},{192,160},{224,256},{2... | collective-permute-start | bytes 1191944 | tf_op jit(solution)/shard_map/ppermute | solution.py:534
  12.4 14.0 %collective-permute-start.1 = (f32[776,128]{1,0:T(8,128)S(1)}, f32[776,128]{1,0:T(8,128)S(1)}, u32[]{:S(2)}, u32[]{:S(2)}) collective-permute-start(f32[776,128]{1,0:T(8,128)S(1)} %get-tuple-element.54), channel_id=1, source_target_pairs={{0,32},{32,0},{64,96},{96,64},{128,160},{160,128},{192,224},{224,1... | collective-permute-start | bytes 1191944 | tf_op jit(solution)/shard_map/ppermute | solution.py:535
  18.9 15.2 %collective-permute-start.4 = (f32[840,128]{1,0:T(8,128)S(1)}, f32[840,128]{1,0:T(8,128)S(1)}, u32[]{:S(2)}, u32[]{:S(2)}) collective-permute-start(f32[840,128]{1,0:T(8,128)S(1)} %constant_dynamic-update-slice_fusion.refs_0_), channel_id=1, source_target_pairs={{0,4},{4,8},{8,12},{12,16},{16,20},{20,24},{24,28},{1,5},{5,9},{9,... | collective-permute-start | bytes 1290248 | tf_op jit(solution)/shard_map/ppermute | solution.py:527
  24.5 9.6 %collective-permute-start.5 = (f32[840,128]{1,0:T(8,128)S(1)}, f32[840,128]{1,0:T(8,128)S(1)}, u32[]{:S(2)}, u32[]{:S(2)}) collective-permute-start(f32[840,128]{1,0:T(8,128)S(1)} %constant_dynamic-update-slice_fusion.refs_0_), channel_id=1, source_target_pairs={{4,0},{8,4},{12,8},{16,12},{20,16},{24,20},{28,24},{5,1},{9,5},{13... | collective-permute-start | bytes 1290248 | tf_op jit(solution)/shard_map/ppermute | solution.py:527
  26.7 10.4 %collective-permute-start.2 = (f32[552,128]{1,0:T(8,128)S(1)}, f32[552,128]{1,0:T(8,128)S(1)}, u32[]{:S(2)}, u32[]{:S(2)}) collective-permute-start(f32[552,128]{1,0:T(8,128)S(1)} %get-tuple-element.53), channel_id=1, source_target_pairs={{4,8},{8,4},{12,16},{16,12},{20,24},{24,20},{5,9},{9,5},{13,17},{1... | collective-permute-start | bytes 847880 | tf_op jit(solution)/shard_map/ppermute | solution.py:534
  32.2 4.9 %collective-permute-start.3 = (f32[552,128]{1,0:T(8,128)S(1)}, f32[552,128]{1,0:T(8,128)S(1)}, u32[]{:S(2)}, u32[]{:S(2)}) collective-permute-start(f32[552,128]{1,0:T(8,128)S(1)} %get-tuple-element.52), channel_id=1, source_target_pairs={{0,4},{4,0},{8,12},{12,8},{16,20},{20,16},{24,28},{28,24},{1,5},{5... | collective-permute-start | bytes 847880 | tf_op jit(solution)/shard_map/ppermute | solution.py:535

commit v7 on v6

--- a/solution.py
+++ b/solution.py
@@ -533,16 +533,11 @@
     outer = [(i, ((i + 1) ^ 1) - 1) for i in range(1, count - 1)]
     two = lax.ppermute(jnp.where(even, to_low, to_high), axis, outer)
     one = lax.ppermute(jnp.where(even, to_high, to_low), axis, inner)
+    return two, one
+
+
+def sorted_pair(two, one, even):
     return jnp.where(even, two, one), jnp.where(even, one, two)
-
-
-def vertical(low, high):
-    count, place = lax.axis_size("gz"), lax.axis_index("gz")
-    index = jnp.arange(count)[:, None, None]
-    sent = jnp.where(index == place + 1, high[None], jnp.where(index == place - 1, low[None], 0.0))
-    even = [lax.axis_index(axis) % 2 == 0 for axis in ("gx", "gy")]
-    sent, even = lax.optimization_barrier((sent, even))
-    return lax.all_to_all(sent, "gz", 0, 0), even
 
 
 def gathered(tile, axes):
@@ -552,12 +547,13 @@
 
 def local(residuals, shear_rate, coupling):
     block, low, high = pack(residuals, shear_rate, coupling)
-    received, (even_x, even_y) = vertical(low, high)
-    own = lax.dynamic_update_slice(block, jnp.sum(received, axis=0), (GHOST_AT, 0))
-    left, right = swapped(own[:SIDE_ROWS], own[LAYER:], "gx", even_x)
+    even_x, even_y, even_z = (lax.axis_index(axis) % 2 == 0 for axis in ("gx", "gy", "gz"))
+    two, one = swapped(low, high, "gz", even_z)
+    own = lax.dynamic_update_slice(block, two + one, (GHOST_AT, 0))
+    left, right = sorted_pair(*swapped(own[:SIDE_ROWS], own[LAYER:], "gx", even_x), even_x)
     front, back = moved(own, "gy", 1), moved(own, "gy", -1)
     down, up = corners(left, right)
-    low_corner, high_corner = swapped(down, up, "gy", even_y)
+    low_corner, high_corner = sorted_pair(*swapped(down, up, "gy", even_y), even_y)
     state = early_powers(own, left, right, front, back)
     basis, gram = late_powers(low_corner, high_corner, state)
     gram = jnp.sum(gathered(gram, ("gy", "gz")), axis=0)

time: 81.8 us -> 81.7 us (level)
  blocking collectives: 46.8 us -> 38.5 us
  starting transfers between devices: 22.1 us -> 29.3 us
  waiting for transfers between devices: 0.87 us -> 1.87 us
    all_to_all x1 -> x0, blocking collectives: 9.55 us -> none  [vertical(): return (lax.all_to_all(sent, 'gz', 0, 0), even)]
    ppermute x2 -> x3, starting transfers between devices: 8.33 us -> 14.9 us  [swapped(): one = lax.ppermute(jnp.where(even, to_high, to_low), axis, inner)]
    all_to_all x2, blocking collectives: 37.2 us -> 38.5 us  [gathered(): lax.all_to_all(jnp.broadcast_to(tile[None], (count,) + tile.shape), axes,...]
    ppermute x2 -> x3, waiting for transfers between devices: 0.01 us -> 1.27 us  [swapped(): one = lax.ppermute(jnp.where(even, to_high, to_low), axis, inner)]
    ppermute x2 -> x3, starting transfers between devices: 6.2 us -> 7.1 us  [swapped(): two = lax.ppermute(jnp.where(even, to_low, to_high), axis, outer)]
  transfers between devices with their start and end apart: 6 -> 8, of which waited for: 1 -> 2; matrix products, arithmetic and copies ran while one was open for 0% -> 0% of each run, Pallas kernels for 3% -> 3%
where the time goes in v7:
time: 81.7 us; the launch traced here: 81.3 us
  blocking collectives  38.5 us (47%)
  starting transfers between devices  29.3 us (36%)
  Pallas kernels  9.44 us (12%)
  waiting for transfers between devices  1.87 us (2%)
  other arithmetic  1.3 us (2%)
  between operations  0.82 us (1%)
    all_to_all x2, blocking collectives, gathered(): lax.all_to_all(jnp.broadcast_to(tile[None], (count,) + tile.shape), axes,...  38.5 us
    ppermute x3, starting transfers between devices, swapped(): one = lax.ppermute(jnp.where(even, to_high, to_low), axis, inner)  14.9 us
    ppermute x2, starting transfers between devices, moved(): return lax.ppermute(block, axis, pairs)  7.31 us
    ppermute x3, starting transfers between devices, swapped(): two = lax.ppermute(jnp.where(even, to_low, to_high), axis, outer)  7.1 us
    pallas_call x1, Pallas kernels, finish(): pl.pallas_call(finish_kernel, out_shape=(jax.ShapeDtypeStruct((RHS * COMP...  3.62 us
    pallas_call x1, Pallas kernels, late_powers(): pl.pallas_call(late_kernel, out_shape=(jax.ShapeDtypeStruct(basis, jnp.fl...  3.42 us
    pallas_call x1, Pallas kernels, early_powers(): pl.pallas_call(early_kernel, out_shape=[jax.ShapeDtypeStruct(shape, jnp.f...  2.07 us
  transfers between devices with their start and end apart: 8, of which 2 were waited for; matrix products, arithmetic and copies ran while one was open for 0% of the time, Pallas kernels for 3%

profile of v7, /device:TPU:1, one launch (start us, length us, event | category | flops | bytes accessed | tf_op | source)
XLA Modules:
  0.0 81.3 jit_solution(6498318395780793828)
XLA Ops:
  0.6 1.1 %pad_maximum_fusion.raw_ref = f32[784,128]{1,0:T(8,128)S(1)} fusion(f32[16,128]{1,0:T(8,128)} %bitcast.6, f32[256,128]{1,0:T(8,128)} %bitcast.5, f32[512,128]{1,0:T(8,128)} %bitcast.4), kind=kLoop, calls=%fused_computation | loop fusion | flops 200704 | bytes 802816 | tf_op jit(solution)/shard_map/concatenate | solution.py:94
  1.7 0.3 shard_map.50
  2.0 0.7 collective-permute-start
  2.7 6.6 %collective-permute-start.1 = (f32[56,128]{1,0:T(8,128)S(1)}, f32[56,128]{1,0:T(8,128)S(1)}, u32[]{:S(2)}, u32[]{:S(2)}) collective-permute-start(f32[56,128]{1,0:T(8,128)S(1)} %get-tuple-element.50), channel_id=1, source_target_pairs={{0,1},{1,0},{2,3},{3,2},{4,5},{5,4},{6,7},{7,6},{8,9},{9,8},{10,11... | collective-permute-start | bytes 86024 | tf_op jit(solution)/shard_map/ppermute | solution.py:535
  9.3 0.0 collective-permute-done
  9.3 1.2 %collective-permute-done.1 = f32[56,128]{1,0:T(8,128)S(1)} collective-permute-done((f32[56,128]{1,0:T(8,128)S(1)}, f32[56,128]{1,0:T(8,128)S(1)}, u32[]{:S(2)}, u32[]{:S(2)}) %collective-permute-start.1) | collective-permute-done | bytes 28704 | tf_op jit(solution)/shard_map/ppermute | solution.py:535
  10.5 0.1 slice_select_fusion
  10.6 0.7 collective-permute-start.2
  11.3 6.4 %collective-permute-start.3 = (f32[776,128]{1,0:T(8,128)S(1)}, f32[776,128]{1,0:T(8,128)S(1)}, u32[]{:S(2)}, u32[]{:S(2)}) collective-permute-start(f32[776,128]{1,0:T(8,128)S(1)} %get-tuple-element.48), channel_id=1, source_target_pairs={{0,32},{32,0},{64,96},{96,64},{128,160},{160,128},{192,224},{224,1... | collective-permute-start | bytes 1191944 | tf_op jit(solution)/shard_map/ppermute | solution.py:535
  17.7 5.4 %collective-permute-start.6 = (f32[840,128]{1,0:T(8,128)S(1)}, f32[840,128]{1,0:T(8,128)S(1)}, u32[]{:S(2)}, u32[]{:S(2)}) collective-permute-start(f32[840,128]{1,0:T(8,128)S(1)} %add_dynamic-update-slice_fusion.refs_0_), channel_id=1, source_target_pairs={{0,4},{4,8},{8,12},{12,16},{16,20},{20,24},{24,28},{1,5},{5,9},{9,... | collective-permute-start | bytes 1290248 | tf_op jit(solution)/shard_map/ppermute | solution.py:527
  23.1 1.9 %collective-permute-start.7 = (f32[840,128]{1,0:T(8,128)S(1)}, f32[840,128]{1,0:T(8,128)S(1)}, u32[]{:S(2)}, u32[]{:S(2)}) collective-permute-start(f32[840,128]{1,0:T(8,128)S(1)} %add_dynamic-update-slice_fusion.refs_0_), channel_id=1, source_target_pairs={{4,0},{8,4},{12,8},{16,12},{20,16},{24,20},{28,24},{5,1},{9,5},{13... | collective-permute-start | bytes 1290248 | tf_op jit(solution)/shard_map/ppermute | solution.py:527
  25.0 0.0 collective-permute-done.2
  25.0 0.0 collective-permute-done.3
  25.1 0.1 broadcast_select_fusion
  25.1 0.1 shard_map.51
  25.2 5.8 %collective-permute-start.4 = (f32[552,128]{1,0:T(8,128)S(1)}, f32[552,128]{1,0:T(8,128)S(1)}, u32[]{:S(2)}, u32[]{:S(2)}) collective-permute-start(f32[552,128]{1,0:T(8,128)S(1)} %get-tuple-element.47), channel_id=1, source_target_pairs={{4,8},{8,4},{12,16},{16,12},{20,24},{24,20},{5,9},{9,5},{13,17},{1... | collective-permute-start | bytes 847880 | tf_op jit(solution)/shard_map/ppermute | solution.py:534
  31.0 1.9 %collective-permute-start.5 = (f32[552,128]{1,0:T(8,128)S(1)}, f32[552,128]{1,0:T(8,128)S(1)}, u32[]{:S(2)}, u32[]{:S(2)}) collective-permute-start(f32[552,128]{1,0:T(8,128)S(1)} %get-tuple-element.46), channel_id=1, source_target_pairs={{0,4},{4,0},{8,12},{12,8},{16,20},{20,16},{24,28},{28,24},{1,5},{5... | collective-permute-start | bytes 847880 | tf_op jit(solution)/shard_map/ppermute | solution.py:535
  32.9 0.0 collective-permute-done.6.refs_3_
  32.9 0.0 collective-permute-done.7.refs_4_
  32.9 2.1 %shard_map.52 = (f32[320,8,128]{2,1,0:T(8,128)S(1)}, f32[320,8,128]{2,1,0:T(8,128)S(1)}, f32[320,8,128]{2,1,0:T(8,128)S(1)}, f32[320,8,128]{2,1,0:T(8,128)S(1)},...) custom-call(f32[840,128]{1,0:T(8,128)S(1)} %add_dynamic-update-slice, ...), custom_call_target="tpu_custom_call" | custom-call | flops 5000000 | bytes 8000000 | tf_op jit(solution)/shard_map/pallas_call | solution.py:388
  35.0 0.6 collective-permute-done.4
  35.6 0.0 collective-permute-done.5
  35.7 3.4 %shard_map.53 = (f32[64,40,128]{2,1,0:T(8,128)S(1)}, f32[8,128]{1,0:T(8,128)S(1)}) custom-call(f32[552,128]{1,0:T(8,128)S(1)} %get-tuple-element.45.refs_0_, f32[552,128]{1,0:T(8,128)S(1)} %get-tuple-element.44.refs_1_, f32[320,8,128]{2,1,0:T(8,128)S(1)} %get-tuple-element.27.refs_2_, f32[320,8,128]{2,1,0:T(8,128)S(1)} %get-tuple-element.28.refs_3_, ...), custom_call_target="tpu_custom_call" | custom-call | tf_op jit(solution)/shard_map/pallas_call | solution.py:402
  39.1 13.8 %all_to_all.10 = f32[32,8,128]{2,1,0:T(8,128)S(1)} all-to-all(f32[32,8,128]{2,1,0:T(8,128)S(1)} %broadcast_in_dim.4), channel_id=1, replica_groups=mesh['gx'=16,'gy'=8,'gz'=4] {'gy','gz'}, dimensions={0} | all-to-all | bytes 262144 | tf_op jit(solution)/shard_map/all_to_all | solution.py:545
  52.9 24.8 %all_to_all.11.gram_ref = f32[16,8,128]{2,1,0:T(8,128)S(1)} all-to-all(f32[16,8,128]{2,1,0:T(8,128)S(1)} %broadcast_in_dim.5), channel_id=1, replica_groups=mesh['gx'=16,'gy'=8,'gz'=4] {'gx'}, dimensions={0} | all-to-all | bytes 131072 | tf_op jit(solution)/shard_map/all_to_all | solution.py:545
  77.7 3.6 %shard_map.54 = (f32[512,128]{1,0:T(8,128)}, f32[40,40]{1,0:T(8,128)}) custom-call(f32[16,8,128]{2,1,0:T(8,128)S(1)} %all_to_all.11.gram_ref, f32[64,40,128]{2,1,0:T(8,128)S(1)} %get-tuple-element.39.basis_ref), custom_call_target="tpu_custom_call" | custom-call | tf_op jit(solution)/shard_map/pallas_call | solution.py:508
  (7 shorter events, 0.2 us)
Async XLA Ops:
  2.0 7.3 %collective-permute-start = (f32[56,128]{1,0:T(8,128)S(1)}, f32[56,128]{1,0:T(8,128)S(1)}, u32[]{:S(2)}, u32[]{:S(2)}) collective-permute-start(f32[56,128]{1,0:T(8,128)S(1)} %get-tuple-element.51), channel_id=1, source_target_pairs={{1,2},{2,1},{5,6},{6,5},{9,10},{10,9},{13,14},{14,13},{17,18},{18,... | collective-permute-start | bytes 86024 | tf_op jit(solution)/shard_map/ppermute | solution.py:534
  2.7 7.8 %collective-permute-start.1 = (f32[56,128]{1,0:T(8,128)S(1)}, f32[56,128]{1,0:T(8,128)S(1)}, u32[]{:S(2)}, u32[]{:S(2)}) collective-permute-start(f32[56,128]{1,0:T(8,128)S(1)} %get-tuple-element.50), channel_id=1, source_target_pairs={{0,1},{1,0},{2,3},{3,2},{4,5},{5,4},{6,7},{7,6},{8,9},{9,8},{10,11... | collective-permute-start | bytes 86024 | tf_op jit(solution)/shard_map/ppermute | solution.py:535
  10.6 14.4 %collective-permute-start.2 = (f32[776,128]{1,0:T(8,128)S(1)}, f32[776,128]{1,0:T(8,128)S(1)}, u32[]{:S(2)}, u32[]{:S(2)}) collective-permute-start(f32[776,128]{1,0:T(8,128)S(1)} %get-tuple-element.49), channel_id=1, source_target_pairs={{32,64},{64,32},{96,128},{128,96},{160,192},{192,160},{224,256},{2... | collective-permute-start | bytes 1191944 | tf_op jit(solution)/shard_map/ppermute | solution.py:534
  11.3 13.8 %collective-permute-start.3 = (f32[776,128]{1,0:T(8,128)S(1)}, f32[776,128]{1,0:T(8,128)S(1)}, u32[]{:S(2)}, u32[]{:S(2)}) collective-permute-start(f32[776,128]{1,0:T(8,128)S(1)} %get-tuple-element.48), channel_id=1, source_target_pairs={{0,32},{32,0},{64,96},{96,64},{128,160},{160,128},{192,224},{224,1... | collective-permute-start | bytes 1191944 | tf_op jit(solution)/shard_map/ppermute | solution.py:535
  17.7 15.2 %collective-permute-start.6 = (f32[840,128]{1,0:T(8,128)S(1)}, f32[840,128]{1,0:T(8,128)S(1)}, u32[]{:S(2)}, u32[]{:S(2)}) collective-permute-start(f32[840,128]{1,0:T(8,128)S(1)} %add_dynamic-update-slice_fusion.refs_0_), channel_id=1, source_target_pairs={{0,4},{4,8},{8,12},{12,16},{16,20},{20,24},{24,28},{1,5},{5,9},{9,... | collective-permute-start | bytes 1290248 | tf_op jit(solution)/shard_map/ppermute | solution.py:527
  23.1 9.8 %collective-permute-start.7 = (f32[840,128]{1,0:T(8,128)S(1)}, f32[840,128]{1,0:T(8,128)S(1)}, u32[]{:S(2)}, u32[]{:S(2)}) collective-permute-start(f32[840,128]{1,0:T(8,128)S(1)} %add_dynamic-update-slice_fusion.refs_0_), channel_id=1, source_target_pairs={{4,0},{8,4},{12,8},{16,12},{20,16},{24,20},{28,24},{5,1},{9,5},{13... | collective-permute-start | bytes 1290248 | tf_op jit(solution)/shard_map/ppermute | solution.py:527
  25.2 10.4 %collective-permute-start.4 = (f32[552,128]{1,0:T(8,128)S(1)}, f32[552,128]{1,0:T(8,128)S(1)}, u32[]{:S(2)}, u32[]{:S(2)}) collective-permute-start(f32[552,128]{1,0:T(8,128)S(1)} %get-tuple-element.47), channel_id=1, source_target_pairs={{4,8},{8,4},{12,16},{16,12},{20,24},{24,20},{5,9},{9,5},{13,17},{1... | collective-permute-start | bytes 847880 | tf_op jit(solution)/shard_map/ppermute | solution.py:534
  31.0 4.6 %collective-permute-start.5 = (f32[552,128]{1,0:T(8,128)S(1)}, f32[552,128]{1,0:T(8,128)S(1)}, u32[]{:S(2)}, u32[]{:S(2)}) collective-permute-start(f32[552,128]{1,0:T(8,128)S(1)} %get-tuple-element.46), channel_id=1, source_target_pairs={{0,4},{4,0},{8,12},{12,8},{16,20},{20,16},{24,28},{28,24},{1,5},{5... | collective-permute-start | bytes 847880 | tf_op jit(solution)/shard_map/ppermute | solution.py:535

commit v8 on v7

--- a/solution.py
+++ b/solution.py
@@ -19,12 +19,13 @@
 FIELD_ROWS = COMP * COLS * RHS
 LAYER = COMP * COMP * BY
 GHOST_ROWS = COMP * RHS + 24
-GHOST_AT = LAYER
-FIELD_AT = GHOST_AT + GHOST_ROWS
+FIELD_AT = GHOST_ROWS + LAYER
 ETA_AT = FIELD_AT + FIELD_ROWS
 TAIL_AT = ETA_AT + COLS
 BLOCK_ROWS = TAIL_AT + (BX - 1) * LAYER
-SIDE_ROWS = BLOCK_ROWS - LAYER
+SIDE_ROWS = BLOCK_ROWS - LAYER - GHOST_ROWS
+LOW_BASE = -GHOST_ROWS - LAYER
+HIGH_BASE = -GHOST_ROWS
 
 NEAR = [(1, 1), (1, 2), (2, 1)]
 FAR = [(1, 3), (2, 2), (3, 1)]
@@ -37,7 +38,7 @@
 
 
 def couple_at(x):
-    return TAIL_AT + (x - 1) * LAYER if x else 0
+    return TAIL_AT + (x - 1) * LAYER if x else GHOST_ROWS
 
 
 def lane_index():
@@ -51,7 +52,7 @@
     shear = raw_ref[raw_shear : raw_shear + COLS, :]
     eta = -0.5 * (0.2 + (1.0 - jnp.exp(-100.0 * shear)) / shear)
     main_ref[ETA_AT:TAIL_AT, :] = eta
-    main_ref[GHOST_AT:FIELD_AT, :] = jnp.zeros((GHOST_ROWS, LANES), jnp.float32)
+    main_ref[0:GHOST_ROWS, :] = jnp.zeros((GHOST_ROWS, LANES), jnp.float32)
     for entry in range(COMP * COMP):
         for x in range(BX):
             start = raw_couple + entry * COLS + x * BY
@@ -107,12 +108,12 @@
     )(raw)
 
 
-def corner_kernel(left_ref, right_ref, down_ref, up_ref):
+def corner_kernel(left_ref, right_ref, left_ghost, right_ghost, down_ref, up_ref):
     lane = lane_index()
     for out_ref, top in ((down_ref, False), (up_ref, True)):
         for place, (side, a, b) in enumerate(CORNER):
             src = right_ref if side else left_ref
-            base = 0 if side else -LAYER
+            base = HIGH_BASE if side else LOW_BASE
             x = a - 1 if side else BX - a
             y = BY - b if top else b - 1
             col = x * BY + y
@@ -131,21 +132,20 @@
             (16 - len(CORNER), LANES), jnp.float32
         )
         for row in range(0, GHOST_ROWS, 8):
-            right = right_ref[GHOST_AT + row : GHOST_AT + row + 8, :]
-            left = left_ref[GHOST_AT - LAYER + row : GHOST_AT - LAYER + row + 8, :]
+            right, left = right_ghost[row : row + 8, :], left_ghost[row : row + 8, :]
             out_ref[C_GHOST_AT + row : C_GHOST_AT + row + 8, :] = jnp.where(
                 lane < LANES // 2, right, left
             )
 
 
-def corners(left, right):
+def corners(*parts):
     return pl.pallas_call(
         corner_kernel,
         out_shape=(jax.ShapeDtypeStruct((CORNER_ROWS, LANES), jnp.float32),) * 2,
-        in_specs=[VMEM] * 2,
+        in_specs=[VMEM] * 4,
         out_specs=(VMEM,) * 2,
         compiler_params=pltpu.CompilerParams(vmem_limit_bytes=4 * 2**20),
-    )(left, right)
+    )(*parts)
 
 
 def distance(place):
@@ -190,7 +190,7 @@
     def held(kind, x, y, power):
         return first_state[kind] if early or ready(x, y, power) else mine[kind]
 
-    def place_column(src, x, y, field_at, entry_at, stride, eta_at, ghost_at, col):
+    def place_column(src, x, y, field_at, entry_at, stride, eta_at, ghosts, ghost_at, col):
         at = SLOT[x, y]
         for comp in range(COMP):
             mine[MAIN][at * COMP + comp] = src[field_at[comp] : field_at[comp] + RHS, :]
@@ -205,18 +205,19 @@
         shift = (-8 * col - 4) % LANES
         for comp in range(COMP):
             row = ghost_at + comp * RHS
-            mine[GHOST][at * COMP + comp] = pltpu.roll(src[row : row + RHS, :], shift, 1)
+            mine[GHOST][at * COMP + comp] = pltpu.roll(ghosts[row : row + RHS, :], shift, 1)
         for part in range(3):
             row = ghost_at + COMP * RHS + part * 8
             mine[COEF + 1][at, part * 8 : part * 8 + 8, :] = pltpu.roll(
-                src[row : row + 8, :], shift, 1
+                ghosts[row : row + 8, :], shift, 1
             )
 
     if early:
-        own_ref, left_ref, right_ref, front_ref, back_ref = blocks
-        for src, base, off_x, off_y in (
-            (own_ref, 0, 0, 0), (left_ref, -LAYER, -1, 0), (right_ref, 0, 1, 0),
-            (front_ref, 0, 0, -1), (back_ref, 0, 0, 1),
+        own_ref, left_ref, right_ref, front_ref, back_ref, left_ghost, right_ghost = blocks
+        for src, base, ghosts, off_x, off_y in (
+            (own_ref, 0, own_ref, 0, 0), (left_ref, LOW_BASE, left_ghost, -1, 0),
+            (right_ref, HIGH_BASE, right_ghost, 1, 0),
+            (front_ref, 0, front_ref, 0, -1), (back_ref, 0, back_ref, 0, 1),
         ):
             for x in range(BX):
                 for y in range(BY):
@@ -224,7 +225,7 @@
                     place_column(
                         src, POWERS + off_x * BX + x, POWERS + off_y * BY + y,
                         [base + FIELD_AT + (comp * COLS + col) * RHS for comp in range(COMP)],
-                        base + couple_at(x) + y, BY, base + ETA_AT + col, base + GHOST_AT, col,
+                        base + couple_at(x) + y, BY, base + ETA_AT + col, ghosts, 0, col,
                     )
     else:
         low_ref, high_ref = blocks
@@ -235,7 +236,7 @@
                 col = (a - 1 if side else BX - a) * BY + (BY - b if top else b - 1)
                 place_column(
                     src, x, y, [(place * COMP + comp) * RHS for comp in range(COMP)],
-                    C_COUPLE_AT + place * 16, 1, C_ETA_AT + place, C_GHOST_AT, col,
+                    C_COUPLE_AT + place * 16, 1, C_ETA_AT + place, src, C_GHOST_AT, col,
                 )
 
     def shifted(value, other):
@@ -344,7 +345,7 @@
 
 
 def early_kernel(*refs):
-    powers_part(True, refs[:5], refs[5:15], refs[5:15], refs[15])
+    powers_part(True, refs[:7], refs[7:17], refs[7:17], refs[17])
 
 
 def late_kernel(*refs):
@@ -390,7 +391,7 @@
         out_shape=[
             jax.ShapeDtypeStruct(shape, jnp.float32) for shape in state_shapes(EARLY) + [basis]
         ],
-        in_specs=[VMEM] * 5,
+        in_specs=[VMEM] * 7,
         out_specs=[VMEM] * 11,
         compiler_params=pltpu.CompilerParams(vmem_limit_bytes=20 * 2**20),
         cost_estimate=pl.CostEstimate(flops=5_000_000, bytes_accessed=8_000_000, transcendentals=0),
@@ -549,12 +550,15 @@
     block, low, high = pack(residuals, shear_rate, coupling)
     even_x, even_y, even_z = (lax.axis_index(axis) % 2 == 0 for axis in ("gx", "gy", "gz"))
     two, one = swapped(low, high, "gz", even_z)
-    own = lax.dynamic_update_slice(block, two + one, (GHOST_AT, 0))
-    left, right = sorted_pair(*swapped(own[:SIDE_ROWS], own[LAYER:], "gx", even_x), even_x)
+    to_low, to_high = block[GHOST_ROWS : GHOST_ROWS + SIDE_ROWS], block[GHOST_ROWS + LAYER :]
+    left, right = sorted_pair(*swapped(to_low, to_high, "gx", even_x), even_x)
+    ghosts = two + one
+    left_ghost, right_ghost = sorted_pair(*swapped(ghosts, ghosts, "gx", even_x), even_x)
+    own = lax.dynamic_update_slice(block, ghosts, (0, 0))
     front, back = moved(own, "gy", 1), moved(own, "gy", -1)
-    down, up = corners(left, right)
+    down, up = corners(left, right, left_ghost, right_ghost)
     low_corner, high_corner = sorted_pair(*swapped(down, up, "gy", even_y), even_y)
-    state = early_powers(own, left, right, front, back)
+    state = early_powers(own, left, right, front, back, left_ghost, right_ghost)
     basis, gram = late_powers(low_corner, high_corner, state)
     gram = jnp.sum(gathered(gram, ("gy", "gz")), axis=0)
     correction, factor = finish(gathered(gram, "gx"), basis)

time: 81.7 us -> 84 us (1.028)
  starting transfers between devices: 29.3 us -> 35.5 us
  blocking collectives: 38.5 us -> 33.6 us
  waiting for transfers between devices: 1.87 us -> 2.73 us
    ppermute x3 -> x4, starting transfers between devices: 14.9 us -> 22.5 us  [swapped(): one = lax.ppermute(jnp.where(even, to_high, to_low), axis, inner)]
    all_to_all x2, blocking collectives: 38.5 us -> 33.6 us  [gathered(): lax.all_to_all(jnp.broadcast_to(tile[None], (count,) + tile.shape), axes,...]
    ppermute x2, waiting for transfers between devices: 0.01 us -> 1.76 us  [moved(): return lax.ppermute(block, axis, pairs)]
    ppermute x3 -> x4, starting transfers between devices: 7.1 us -> 5.65 us  [swapped(): two = lax.ppermute(jnp.where(even, to_low, to_high), axis, outer)]
    ppermute x3 -> x4, waiting for transfers between devices: 1.27 us -> 0.01 us  [swapped(): one = lax.ppermute(jnp.where(even, to_high, to_low), axis, inner)]
  transfers between devices with their start and end apart: 8 -> 10, of which waited for: 2 -> 2; matrix products, arithmetic and copies ran while one was open for 0% -> 0% of each run, Pallas kernels for 3% -> 3%
where the time goes in v8:
time: 84 us; the launch traced here: 83.5 us
  starting transfers between devices  35.5 us (42%)
  blocking collectives  33.6 us (40%)
  Pallas kernels  9.44 us (11%)
  waiting for transfers between devices  2.73 us (3%)
  other arithmetic  1.34 us (2%)
  between operations  0.88 us (1%)
    all_to_all x2, blocking collectives, gathered(): lax.all_to_all(jnp.broadcast_to(tile[None], (count,) + tile.shape), axes,...  33.6 us
    ppermute x4, starting transfers between devices, swapped(): one = lax.ppermute(jnp.where(even, to_high, to_low), axis, inner)  22.5 us
    ppermute x2, starting transfers between devices, moved(): return lax.ppermute(block, axis, pairs)  7.28 us
    ppermute x4, starting transfers between devices, swapped(): two = lax.ppermute(jnp.where(even, to_low, to_high), axis, outer)  5.65 us
    pallas_call x1, Pallas kernels, finish(): pl.pallas_call(finish_kernel, out_shape=(jax.ShapeDtypeStruct((RHS * COMP...  3.62 us
    pallas_call x1, Pallas kernels, late_powers(): pl.pallas_call(late_kernel, out_shape=(jax.ShapeDtypeStruct(basis, jnp.fl...  3.42 us
    pallas_call x1, Pallas kernels, early_powers(): pl.pallas_call(early_kernel, out_shape=[jax.ShapeDtypeStruct(shape, jnp.f...  2.08 us
    ppermute x2, waiting for transfers between devices, moved(): return lax.ppermute(block, axis, pairs)  1.76 us
  transfers between devices with their start and end apart: 10, of which 2 were waited for; matrix products, arithmetic and copies ran while one was open for 0% of the time, Pallas kernels for 3%

profile of v8, /device:TPU:1, one launch (start us, length us, event | category | flops | bytes accessed | tf_op | source)
XLA Modules:
  0.0 83.5 jit_solution(14191051465190039448)
XLA Ops:
  0.6 1.1 %pad_maximum_fusion.raw_ref = f32[784,128]{1,0:T(8,128)S(1)} fusion(f32[16,128]{1,0:T(8,128)} %bitcast.6, f32[256,128]{1,0:T(8,128)} %bitcast.5, f32[512,128]{1,0:T(8,128)} %bitcast.4), kind=kLoop, calls=%fused_computation | loop fusion | flops 200704 | bytes 802816 | tf_op jit(solution)/shard_map/concatenate | solution.py:95
  1.7 0.3 shard_map.50
  2.0 0.7 collective-permute-start.2
  2.7 6.6 %collective-permute-start.3 = (f32[56,128]{1,0:T(8,128)S(1)}, f32[56,128]{1,0:T(8,128)S(1)}, u32[]{:S(2)}, u32[]{:S(2)}) collective-permute-start(f32[56,128]{1,0:T(8,128)S(1)} %get-tuple-element.54), channel_id=1, source_target_pairs={{0,1},{1,0},{2,3},{3,2},{4,5},{5,4},{6,7},{7,6},{8,9},{9,8},{10,11... | collective-permute-start | bytes 86024 | tf_op jit(solution)/shard_map/ppermute | solution.py:536
  9.3 0.1 slice_select_fusion
  9.3 0.7 collective-permute-start
  10.0 6.4 %collective-permute-start.1 = (f32[720,128]{1,0:T(8,128)S(1)}, f32[720,128]{1,0:T(8,128)S(1)}, u32[]{:S(2)}, u32[]{:S(2)}) collective-permute-start(f32[720,128]{1,0:T(8,128)S(1)} %get-tuple-element.50), channel_id=1, source_target_pairs={{0,32},{32,0},{64,96},{96,64},{128,160},{160,128},{192,224},{224,1... | collective-permute-start | bytes 1105928 | tf_op jit(solution)/shard_map/ppermute | solution.py:536
  16.4 0.0 collective-permute-done.2
  16.5 0.0 collective-permute-done.3
  16.5 0.7 collective-permute-start.4
  17.2 7.6 %collective-permute-start.5 = (f32[56,128]{1,0:T(8,128)S(1)}, f32[56,128]{1,0:T(8,128)S(1)}, u32[]{:S(2)}, u32[]{:S(2)}) collective-permute-start(f32[56,128]{1,0:T(8,128)S(1)} %get-tuple-element.43), channel_id=1, source_target_pairs={{0,32},{32,0},{64,96},{96,64},{128,160},{160,128},{192,224},{224,1... | collective-permute-start | bytes 86024 | tf_op jit(solution)/shard_map/ppermute | solution.py:536
  24.8 5.4 %collective-permute-start.8 = (f32[840,128]{1,0:T(8,128)S(1)}, f32[840,128]{1,0:T(8,128)S(1)}, u32[]{:S(2)}, u32[]{:S(2)}) collective-permute-start(f32[840,128]{1,0:T(8,128)S(1)} %get-tuple-element.42.refs_0_), channel_id=1, source_target_pairs={{0,4},{4,8},{8,12},{12,16},{16,20},{20,24},{24,28},{1,5},{5,9},{9,... | collective-permute-start | bytes 1290248 | tf_op jit(solution)/shard_map/ppermute | solution.py:528
  30.2 0.0 collective-permute-done.4
  30.2 1.9 %collective-permute-start.9 = (f32[840,128]{1,0:T(8,128)S(1)}, f32[840,128]{1,0:T(8,128)S(1)}, u32[]{:S(2)}, u32[]{:S(2)}) collective-permute-start(f32[840,128]{1,0:T(8,128)S(1)} %get-tuple-element.42.refs_0_), channel_id=1, source_target_pairs={{4,0},{8,4},{12,8},{16,12},{20,16},{24,20},{28,24},{5,1},{9,5},{13... | collective-permute-start | bytes 1290248 | tf_op jit(solution)/shard_map/ppermute | solution.py:528
  32.1 0.0 collective-permute-done.5
  32.1 0.0 collective-permute-done
  32.2 0.0 collective-permute-done.1
  32.2 0.1 broadcast_select_fusion
  32.3 3.6 %collective-permute-start.6 = (f32[552,128]{1,0:T(8,128)S(1)}, f32[552,128]{1,0:T(8,128)S(1)}, u32[]{:S(2)}, u32[]{:S(2)}) collective-permute-start(f32[552,128]{1,0:T(8,128)S(1)} %get-tuple-element.49), channel_id=1, source_target_pairs={{4,8},{8,4},{12,16},{16,12},{20,24},{24,20},{5,9},{9,5},{13,17},{1... | collective-permute-start | bytes 847880 | tf_op jit(solution)/shard_map/ppermute | solution.py:535
  36.0 1.9 %collective-permute-start.7 = (f32[552,128]{1,0:T(8,128)S(1)}, f32[552,128]{1,0:T(8,128)S(1)}, u32[]{:S(2)}, u32[]{:S(2)}) collective-permute-start(f32[552,128]{1,0:T(8,128)S(1)} %get-tuple-element.48), channel_id=1, source_target_pairs={{0,4},{4,0},{8,12},{12,8},{16,20},{20,16},{24,28},{28,24},{1,5},{5... | collective-permute-start | bytes 847880 | tf_op jit(solution)/shard_map/ppermute | solution.py:536
  37.9 0.0 collective-permute-done.8.refs_3_
  37.9 1.8 %collective-permute-done.9.refs_4_ = f32[840,128]{1,0:T(8,128)S(1)} collective-permute-done((f32[840,128]{1,0:T(8,128)S(1)}, f32[840,128]{1,0:T(8,128)S(1)}, u32[]{:S(2)}, u32[]{:S(2)}) %collective-permute-start.9) | collective-permute-done | bytes 430112 | tf_op jit(solution)/shard_map/ppermute | solution.py:528
  39.7 2.1 %shard_map.52 = (f32[320,8,128]{2,1,0:T(8,128)S(1)}, f32[320,8,128]{2,1,0:T(8,128)S(1)}, f32[320,8,128]{2,1,0:T(8,128)S(1)}, f32[320,8,128]{2,1,0:T(8,128)S(1)},...) custom-call(f32[840,128]{1,0:T(8,128)S(1)} %get-tuple-element.42.ref, ...), custom_call_target="tpu_custom_call" | custom-call | flops 5000000 | bytes 8000000 | tf_op jit(solution)/shard_map/pallas_call | solution.py:389
  41.8 0.9 %collective-permute-done.6 = f32[552,128]{1,0:T(8,128)S(1)} collective-permute-done((f32[552,128]{1,0:T(8,128)S(1)}, f32[552,128]{1,0:T(8,128)S(1)}, u32[]{:S(2)}, u32[]{:S(2)}) %collective-permute-start.6) | collective-permute-done | bytes 282656 | tf_op jit(solution)/shard_map/ppermute | solution.py:535
  42.7 0.0 collective-permute-done.7
  42.7 0.1 broadcast_select_fusion.2
  42.8 3.4 %shard_map.53 = (f32[64,40,128]{2,1,0:T(8,128)S(1)}, f32[8,128]{1,0:T(8,128)S(1)}) custom-call(f32[552,128]{1,0:T(8,128)S(1)} %get-tuple-element.47.refs_0_, f32[552,128]{1,0:T(8,128)S(1)} %get-tuple-element.46.refs_1_, f32[320,8,128]{2,1,0:T(8,128)S(1)} %get-tuple-element.27.refs_2_, f32[320,8,128]{2,1,0:T(8,128)S(1)} %get-tuple-element.28.refs_3_, ...), custom_call_target="tpu_custom_call" | custom-call | tf_op jit(solution)/shard_map/pallas_call | solution.py:403
  46.2 12.1 %all_to_all.10 = f32[32,8,128]{2,1,0:T(8,128)S(1)} all-to-all(f32[32,8,128]{2,1,0:T(8,128)S(1)} %broadcast_in_dim.4), channel_id=1, replica_groups=mesh['gx'=16,'gy'=8,'gz'=4] {'gy','gz'}, dimensions={0} | all-to-all | bytes 262144 | tf_op jit(solution)/shard_map/all_to_all | solution.py:546
  58.4 21.5 %all_to_all.11.gram_ref = f32[16,8,128]{2,1,0:T(8,128)S(1)} all-to-all(f32[16,8,128]{2,1,0:T(8,128)S(1)} %broadcast_in_dim.5), channel_id=1, replica_groups=mesh['gx'=16,'gy'=8,'gz'=4] {'gx'}, dimensions={0} | all-to-all | bytes 131072 | tf_op jit(solution)/shard_map/all_to_all | solution.py:546
  79.9 3.6 %shard_map.54 = (f32[512,128]{1,0:T(8,128)}, f32[40,40]{1,0:T(8,128)}) custom-call(f32[16,8,128]{2,1,0:T(8,128)S(1)} %all_to_all.11.gram_ref, f32[64,40,128]{2,1,0:T(8,128)S(1)} %get-tuple-element.39.basis_ref), custom_call_target="tpu_custom_call" | custom-call | tf_op jit(solution)/shard_map/pallas_call | solution.py:509
  (8 shorter events, 0.2 us)
Async XLA Ops:
  2.0 14.4 %collective-permute-start.2 = (f32[56,128]{1,0:T(8,128)S(1)}, f32[56,128]{1,0:T(8,128)S(1)}, u32[]{:S(2)}, u32[]{:S(2)}) collective-permute-start(f32[56,128]{1,0:T(8,128)S(1)} %get-tuple-element.55), channel_id=1, source_target_pairs={{1,2},{2,1},{5,6},{6,5},{9,10},{10,9},{13,14},{14,13},{17,18},{18,... | collective-permute-start | bytes 86024 | tf_op jit(solution)/shard_map/ppermute | solution.py:535
  2.7 13.8 %collective-permute-start.3 = (f32[56,128]{1,0:T(8,128)S(1)}, f32[56,128]{1,0:T(8,128)S(1)}, u32[]{:S(2)}, u32[]{:S(2)}) collective-permute-start(f32[56,128]{1,0:T(8,128)S(1)} %get-tuple-element.54), channel_id=1, source_target_pairs={{0,1},{1,0},{2,3},{3,2},{4,5},{5,4},{6,7},{7,6},{8,9},{9,8},{10,11... | collective-permute-start | bytes 86024 | tf_op jit(solution)/shard_map/ppermute | solution.py:536
  9.3 22.8 %collective-permute-start = (f32[720,128]{1,0:T(8,128)S(1)}, f32[720,128]{1,0:T(8,128)S(1)}, u32[]{:S(2)}, u32[]{:S(2)}) collective-permute-start(f32[720,128]{1,0:T(8,128)S(1)} %get-tuple-element.51), channel_id=1, source_target_pairs={{32,64},{64,32},{96,128},{128,96},{160,192},{192,160},{224,256},{2... | collective-permute-start | bytes 1105928 | tf_op jit(solution)/shard_map/ppermute | solution.py:535
  10.0 22.1 %collective-permute-start.1 = (f32[720,128]{1,0:T(8,128)S(1)}, f32[720,128]{1,0:T(8,128)S(1)}, u32[]{:S(2)}, u32[]{:S(2)}) collective-permute-start(f32[720,128]{1,0:T(8,128)S(1)} %get-tuple-element.50), channel_id=1, source_target_pairs={{0,32},{32,0},{64,96},{96,64},{128,160},{160,128},{192,224},{224,1... | collective-permute-start | bytes 1105928 | tf_op jit(solution)/shard_map/ppermute | solution.py:536
  16.5 13.7 %collective-permute-start.4 = (f32[56,128]{1,0:T(8,128)S(1)}, f32[56,128]{1,0:T(8,128)S(1)}, u32[]{:S(2)}, u32[]{:S(2)}) collective-permute-start(f32[56,128]{1,0:T(8,128)S(1)} %get-tuple-element.43), channel_id=1, source_target_pairs={{32,64},{64,32},{96,128},{128,96},{160,192},{192,160},{224,256},{2... | collective-permute-start | bytes 86024 | tf_op jit(solution)/shard_map/ppermute | solution.py:535
  17.2 15.0 %collective-permute-start.5 = (f32[56,128]{1,0:T(8,128)S(1)}, f32[56,128]{1,0:T(8,128)S(1)}, u32[]{:S(2)}, u32[]{:S(2)}) collective-permute-start(f32[56,128]{1,0:T(8,128)S(1)} %get-tuple-element.43), channel_id=1, source_target_pairs={{0,32},{32,0},{64,96},{96,64},{128,160},{160,128},{192,224},{224,1... | collective-permute-start | bytes 86024 | tf_op jit(solution)/shard_map/ppermute | solution.py:536
  24.8 13.1 %collective-permute-start.8 = (f32[840,128]{1,0:T(8,128)S(1)}, f32[840,128]{1,0:T(8,128)S(1)}, u32[]{:S(2)}, u32[]{:S(2)}) collective-permute-start(f32[840,128]{1,0:T(8,128)S(1)} %get-tuple-element.42.refs_0_), channel_id=1, source_target_pairs={{0,4},{4,8},{8,12},{12,16},{16,20},{20,24},{24,28},{1,5},{5,9},{9,... | collective-permute-start | bytes 1290248 | tf_op jit(solution)/shard_map/ppermute | solution.py:528
  30.2 9.5 %collective-permute-start.9 = (f32[840,128]{1,0:T(8,128)S(1)}, f32[840,128]{1,0:T(8,128)S(1)}, u32[]{:S(2)}, u32[]{:S(2)}) collective-permute-start(f32[840,128]{1,0:T(8,128)S(1)} %get-tuple-element.42.refs_0_), channel_id=1, source_target_pairs={{4,0},{8,4},{12,8},{16,12},{20,16},{24,20},{28,24},{5,1},{9,5},{13... | collective-permute-start | bytes 1290248 | tf_op jit(solution)/shard_map/ppermute | solution.py:528
  32.3 10.4 %collective-permute-start.6 = (f32[552,128]{1,0:T(8,128)S(1)}, f32[552,128]{1,0:T(8,128)S(1)}, u32[]{:S(2)}, u32[]{:S(2)}) collective-permute-start(f32[552,128]{1,0:T(8,128)S(1)} %get-tuple-element.49), channel_id=1, source_target_pairs={{4,8},{8,4},{12,16},{16,12},{20,24},{24,20},{5,9},{9,5},{13,17},{1... | collective-permute-start | bytes 847880 | tf_op jit(solution)/shard_map/ppermute | solution.py:535
  36.0 6.7 %collective-permute-start.7 = (f32[552,128]{1,0:T(8,128)S(1)}, f32[552,128]{1,0:T(8,128)S(1)}, u32[]{:S(2)}, u32[]{:S(2)}) collective-permute-start(f32[552,128]{1,0:T(8,128)S(1)} %get-tuple-element.48), channel_id=1, source_target_pairs={{0,4},{4,0},{8,12},{12,8},{16,20},{20,16},{24,28},{28,24},{1,5},{5... | collective-permute-start | bytes 847880 | tf_op jit(solution)/shard_map/ppermute | solution.py:536

commit v9 on v8

--- a/solution.py
+++ b/solution.py
@@ -522,12 +522,6 @@
     )(gram, basis)
 
 
-def moved(block, axis, step):
-    count = lax.axis_size(axis)
-    pairs = [(i, i + step) for i in range(count) if 0 <= i + step < count]
-    return lax.ppermute(block, axis, pairs)
-
-
 def swapped(to_low, to_high, axis, even):
     count = lax.axis_size(axis)
     inner = [(i, i ^ 1) for i in range(count)]
@@ -555,7 +549,7 @@
     ghosts = two + one
     left_ghost, right_ghost = sorted_pair(*swapped(ghosts, ghosts, "gx", even_x), even_x)
     own = lax.dynamic_update_slice(block, ghosts, (0, 0))
-    front, back = moved(own, "gy", 1), moved(own, "gy", -1)
+    front, back = sorted_pair(*swapped(own, own, "gy", even_y), even_y)
     down, up = corners(left, right, left_ghost, right_ghost)
     low_corner, high_corner = sorted_pair(*swapped(down, up, "gy", even_y), even_y)
     state = early_powers(own, left, right, front, back, left_ghost, right_ghost)

time: 84 us -> 81.8 us (0.974)
  waiting for transfers between devices: 2.73 us -> 0.38 us
    ppermute x2 -> x0, starting transfers between devices: 7.28 us -> none  [moved(): return lax.ppermute(block, axis, pairs)]
    ppermute x4 -> x5, starting transfers between devices: 5.65 us -> 10.9 us  [swapped(): two = lax.ppermute(jnp.where(even, to_low, to_high), axis, outer)]
    ppermute x4 -> x5, starting transfers between devices: 22.5 us -> 24.5 us  [swapped(): one = lax.ppermute(jnp.where(even, to_high, to_low), axis, inner)]
    ppermute x2 -> x0, waiting for transfers between devices: 1.76 us -> none  [moved(): return lax.ppermute(block, axis, pairs)]
  transfers between devices with their start and end apart: 10 -> 10, of which waited for: 2 -> 1; matrix products, arithmetic and copies ran while one was open for 0% -> 0% of each run, Pallas kernels for 3% -> 3%
where the time goes in v9:
time: 81.8 us; the launch traced here: 81.3 us
  starting transfers between devices  35.3 us (43%)
  blocking collectives  34 us (42%)
  Pallas kernels  9.32 us (11%)
  other arithmetic  1.37 us (2%)
  between operations  0.9 us (1%)
    all_to_all x2, blocking collectives, gathered(): lax.all_to_all(jnp.broadcast_to(tile[None], (count,) + tile.shape), axes,...  34 us
    ppermute x5, starting transfers between devices, swapped(): one = lax.ppermute(jnp.where(even, to_high, to_low), axis, inner)  24.5 us
    ppermute x5, starting transfers between devices, swapped(): two = lax.ppermute(jnp.where(even, to_low, to_high), axis, outer)  10.9 us
    pallas_call x1, Pallas kernels, finish(): pl.pallas_call(finish_kernel, out_shape=(jax.ShapeDtypeStruct((RHS * COMP...  3.62 us
    pallas_call x1, Pallas kernels, late_powers(): pl.pallas_call(late_kernel, out_shape=(jax.ShapeDtypeStruct(basis, jnp.fl...  3.35 us
    pallas_call x1, Pallas kernels, early_powers(): pl.pallas_call(early_kernel, out_shape=[jax.ShapeDtypeStruct(shape, jnp.f...  2.02 us
  transfers between devices with their start and end apart: 10, of which 1 were waited for; matrix products, arithmetic and copies ran while one was open for 0% of the time, Pallas kernels for 3%

profile of v9, /device:TPU:1, one launch (start us, length us, event | category | flops | bytes accessed | tf_op | source)
XLA Modules:
  0.0 81.3 jit_solution(4915000062645123733)
XLA Ops:
  0.6 1.1 %pad_maximum_fusion.raw_ref = f32[784,128]{1,0:T(8,128)S(1)} fusion(f32[16,128]{1,0:T(8,128)} %bitcast.6, f32[256,128]{1,0:T(8,128)} %bitcast.5, f32[512,128]{1,0:T(8,128)} %bitcast.4), kind=kLoop, calls=%fused_computation | loop fusion | flops 200704 | bytes 802816 | tf_op jit(solution)/shard_map/concatenate | solution.py:95
  1.7 0.3 shard_map.50
  2.0 0.7 collective-permute-start.2
  2.7 6.6 %collective-permute-start.3 = (f32[56,128]{1,0:T(8,128)S(1)}, f32[56,128]{1,0:T(8,128)S(1)}, u32[]{:S(2)}, u32[]{:S(2)}) collective-permute-start(f32[56,128]{1,0:T(8,128)S(1)} %get-tuple-element.56), channel_id=1, source_target_pairs={{0,1},{1,0},{2,3},{3,2},{4,5},{5,4},{6,7},{7,6},{8,9},{9,8},{10,11... | collective-permute-start | bytes 86024 | tf_op jit(solution)/shard_map/ppermute | solution.py:530
  9.3 0.1 slice_select_fusion
  9.3 0.7 collective-permute-start
  10.0 6.4 %collective-permute-start.1 = (f32[720,128]{1,0:T(8,128)S(1)}, f32[720,128]{1,0:T(8,128)S(1)}, u32[]{:S(2)}, u32[]{:S(2)}) collective-permute-start(f32[720,128]{1,0:T(8,128)S(1)} %get-tuple-element.52), channel_id=1, source_target_pairs={{0,32},{32,0},{64,96},{96,64},{128,160},{160,128},{192,224},{224,1... | collective-permute-start | bytes 1105928 | tf_op jit(solution)/shard_map/ppermute | solution.py:530
  16.4 0.0 collective-permute-done.2
  16.5 0.0 collective-permute-done.3
  16.5 0.7 collective-permute-start.4
  17.2 7.6 %collective-permute-start.5 = (f32[56,128]{1,0:T(8,128)S(1)}, f32[56,128]{1,0:T(8,128)S(1)}, u32[]{:S(2)}, u32[]{:S(2)}) collective-permute-start(f32[56,128]{1,0:T(8,128)S(1)} %get-tuple-element.43), channel_id=1, source_target_pairs={{0,32},{32,0},{64,96},{96,64},{128,160},{160,128},{192,224},{224,1... | collective-permute-start | bytes 86024 | tf_op jit(solution)/shard_map/ppermute | solution.py:530
  24.8 5.4 %collective-permute-start.8 = (f32[840,128]{1,0:T(8,128)S(1)}, f32[840,128]{1,0:T(8,128)S(1)}, u32[]{:S(2)}, u32[]{:S(2)}) collective-permute-start(f32[840,128]{1,0:T(8,128)S(1)} %get-tuple-element.42.refs_0_), channel_id=1, source_target_pairs={{4,8},{8,4},{12,16},{16,12},{20,24},{24,20},{5,9},{9,5},{13,17},{1... | collective-permute-start | bytes 1290248 | tf_op jit(solution)/shard_map/ppermute | solution.py:529
  30.2 0.0 collective-permute-done.4
  30.2 1.9 %collective-permute-start.9 = (f32[840,128]{1,0:T(8,128)S(1)}, f32[840,128]{1,0:T(8,128)S(1)}, u32[]{:S(2)}, u32[]{:S(2)}) collective-permute-start(f32[840,128]{1,0:T(8,128)S(1)} %get-tuple-element.42.refs_0_), channel_id=1, source_target_pairs={{0,4},{4,0},{8,12},{12,8},{16,20},{20,16},{24,28},{28,24},{1,5},{5... | collective-permute-start | bytes 1290248 | tf_op jit(solution)/shard_map/ppermute | solution.py:530
  32.1 0.0 collective-permute-done.5
  32.1 0.0 collective-permute-done
  32.2 0.0 collective-permute-done.1
  32.2 0.1 broadcast_select_fusion.2
  32.3 3.5 %collective-permute-start.6 = (f32[552,128]{1,0:T(8,128)S(1)}, f32[552,128]{1,0:T(8,128)S(1)}, u32[]{:S(2)}, u32[]{:S(2)}) collective-permute-start(f32[552,128]{1,0:T(8,128)S(1)} %get-tuple-element.51), channel_id=1, source_target_pairs={{4,8},{8,4},{12,16},{16,12},{20,24},{24,20},{5,9},{9,5},{13,17},{1... | collective-permute-start | bytes 847880 | tf_op jit(solution)/shard_map/ppermute | solution.py:529
  35.8 1.9 %collective-permute-start.7 = (f32[552,128]{1,0:T(8,128)S(1)}, f32[552,128]{1,0:T(8,128)S(1)}, u32[]{:S(2)}, u32[]{:S(2)}) collective-permute-start(f32[552,128]{1,0:T(8,128)S(1)} %get-tuple-element.50), channel_id=1, source_target_pairs={{0,4},{4,0},{8,12},{12,8},{16,20},{20,16},{24,28},{28,24},{1,5},{5... | collective-permute-start | bytes 847880 | tf_op jit(solution)/shard_map/ppermute | solution.py:530
  37.8 0.0 collective-permute-done.8
  37.8 0.0 collective-permute-done.9
  37.8 0.1 broadcast_select_fusion
  37.9 2.0 %shard_map.52 = (f32[320,8,128]{2,1,0:T(8,128)S(1)}, f32[320,8,128]{2,1,0:T(8,128)S(1)}, f32[320,8,128]{2,1,0:T(8,128)S(1)}, f32[320,8,128]{2,1,0:T(8,128)S(1)},...) custom-call(f32[840,128]{1,0:T(8,128)S(1)} %get-tuple-element.42.ref, ...), custom_call_target="tpu_custom_call" | custom-call | flops 5000000 | bytes 8000000 | tf_op jit(solution)/shard_map/pallas_call | solution.py:389
  39.9 0.4 collective-permute-done.6
  40.2 0.0 collective-permute-done.7
  40.3 3.3 %shard_map.53 = (f32[64,40,128]{2,1,0:T(8,128)S(1)}, f32[8,128]{1,0:T(8,128)S(1)}) custom-call(f32[552,128]{1,0:T(8,128)S(1)} %get-tuple-element.49.refs_0_, f32[552,128]{1,0:T(8,128)S(1)} %get-tuple-element.48.refs_1_, f32[320,8,128]{2,1,0:T(8,128)S(1)} %get-tuple-element.27.refs_2_, f32[320,8,128]{2,1,0:T(8,128)S(1)} %get-tuple-element.28.refs_3_, ...), custom_call_target="tpu_custom_call" | custom-call | tf_op jit(solution)/shard_map/pallas_call | solution.py:403
  43.7 12.5 %all_to_all.10 = f32[32,8,128]{2,1,0:T(8,128)S(1)} all-to-all(f32[32,8,128]{2,1,0:T(8,128)S(1)} %broadcast_in_dim.4), channel_id=1, replica_groups=mesh['gx'=16,'gy'=8,'gz'=4] {'gy','gz'}, dimensions={0} | all-to-all | bytes 262144 | tf_op jit(solution)/shard_map/all_to_all | solution.py:540
  56.2 21.5 %all_to_all.11.gram_ref = f32[16,8,128]{2,1,0:T(8,128)S(1)} all-to-all(f32[16,8,128]{2,1,0:T(8,128)S(1)} %broadcast_in_dim.5), channel_id=1, replica_groups=mesh['gx'=16,'gy'=8,'gz'=4] {'gx'}, dimensions={0} | all-to-all | bytes 131072 | tf_op jit(solution)/shard_map/all_to_all | solution.py:540
  77.7 3.6 %shard_map.54 = (f32[512,128]{1,0:T(8,128)}, f32[40,40]{1,0:T(8,128)}) custom-call(f32[16,8,128]{2,1,0:T(8,128)S(1)} %all_to_all.11.gram_ref, f32[64,40,128]{2,1,0:T(8,128)S(1)} %get-tuple-element.39.basis_ref), custom_call_target="tpu_custom_call" | custom-call | tf_op jit(solution)/shard_map/pallas_call | solution.py:509
  (9 shorter events, 0.2 us)
Async XLA Ops:
  2.0 14.4 %collective-permute-start.2 = (f32[56,128]{1,0:T(8,128)S(1)}, f32[56,128]{1,0:T(8,128)S(1)}, u32[]{:S(2)}, u32[]{:S(2)}) collective-permute-start(f32[56,128]{1,0:T(8,128)S(1)} %get-tuple-element.57), channel_id=1, source_target_pairs={{1,2},{2,1},{5,6},{6,5},{9,10},{10,9},{13,14},{14,13},{17,18},{18,... | collective-permute-start | bytes 86024 | tf_op jit(solution)/shard_map/ppermute | solution.py:529
  2.7 13.8 %collective-permute-start.3 = (f32[56,128]{1,0:T(8,128)S(1)}, f32[56,128]{1,0:T(8,128)S(1)}, u32[]{:S(2)}, u32[]{:S(2)}) collective-permute-start(f32[56,128]{1,0:T(8,128)S(1)} %get-tuple-element.56), channel_id=1, source_target_pairs={{0,1},{1,0},{2,3},{3,2},{4,5},{5,4},{6,7},{7,6},{8,9},{9,8},{10,11... | collective-permute-start | bytes 86024 | tf_op jit(solution)/shard_map/ppermute | solution.py:530
  9.3 22.8 %collective-permute-start = (f32[720,128]{1,0:T(8,128)S(1)}, f32[720,128]{1,0:T(8,128)S(1)}, u32[]{:S(2)}, u32[]{:S(2)}) collective-permute-start(f32[720,128]{1,0:T(8,128)S(1)} %get-tuple-element.53), channel_id=1, source_target_pairs={{32,64},{64,32},{96,128},{128,96},{160,192},{192,160},{224,256},{2... | collective-permute-start | bytes 1105928 | tf_op jit(solution)/shard_map/ppermute | solution.py:529
  10.0 22.1 %collective-permute-start.1 = (f32[720,128]{1,0:T(8,128)S(1)}, f32[720,128]{1,0:T(8,128)S(1)}, u32[]{:S(2)}, u32[]{:S(2)}) collective-permute-start(f32[720,128]{1,0:T(8,128)S(1)} %get-tuple-element.52), channel_id=1, source_target_pairs={{0,32},{32,0},{64,96},{96,64},{128,160},{160,128},{192,224},{224,1... | collective-permute-start | bytes 1105928 | tf_op jit(solution)/shard_map/ppermute | solution.py:530
  16.5 13.7 %collective-permute-start.4 = (f32[56,128]{1,0:T(8,128)S(1)}, f32[56,128]{1,0:T(8,128)S(1)}, u32[]{:S(2)}, u32[]{:S(2)}) collective-permute-start(f32[56,128]{1,0:T(8,128)S(1)} %get-tuple-element.43), channel_id=1, source_target_pairs={{32,64},{64,32},{96,128},{128,96},{160,192},{192,160},{224,256},{2... | collective-permute-start | bytes 86024 | tf_op jit(solution)/shard_map/ppermute | solution.py:529
  17.2 15.0 %collective-permute-start.5 = (f32[56,128]{1,0:T(8,128)S(1)}, f32[56,128]{1,0:T(8,128)S(1)}, u32[]{:S(2)}, u32[]{:S(2)}) collective-permute-start(f32[56,128]{1,0:T(8,128)S(1)} %get-tuple-element.43), channel_id=1, source_target_pairs={{0,32},{32,0},{64,96},{96,64},{128,160},{160,128},{192,224},{224,1... | collective-permute-start | bytes 86024 | tf_op jit(solution)/shard_map/ppermute | solution.py:530
  24.8 13.0 %collective-permute-start.8 = (f32[840,128]{1,0:T(8,128)S(1)}, f32[840,128]{1,0:T(8,128)S(1)}, u32[]{:S(2)}, u32[]{:S(2)}) collective-permute-start(f32[840,128]{1,0:T(8,128)S(1)} %get-tuple-element.42.refs_0_), channel_id=1, source_target_pairs={{4,8},{8,4},{12,16},{16,12},{20,24},{24,20},{5,9},{9,5},{13,17},{1... | collective-permute-start | bytes 1290248 | tf_op jit(solution)/shard_map/ppermute | solution.py:529
  30.2 7.6 %collective-permute-start.9 = (f32[840,128]{1,0:T(8,128)S(1)}, f32[840,128]{1,0:T(8,128)S(1)}, u32[]{:S(2)}, u32[]{:S(2)}) collective-permute-start(f32[840,128]{1,0:T(8,128)S(1)} %get-tuple-element.42.refs_0_), channel_id=1, source_target_pairs={{0,4},{4,0},{8,12},{12,8},{16,20},{20,16},{24,28},{28,24},{1,5},{5... | collective-permute-start | bytes 1290248 | tf_op jit(solution)/shard_map/ppermute | solution.py:530
  32.3 7.9 %collective-permute-start.6 = (f32[552,128]{1,0:T(8,128)S(1)}, f32[552,128]{1,0:T(8,128)S(1)}, u32[]{:S(2)}, u32[]{:S(2)}) collective-permute-start(f32[552,128]{1,0:T(8,128)S(1)} %get-tuple-element.51), channel_id=1, source_target_pairs={{4,8},{8,4},{12,16},{16,12},{20,24},{24,20},{5,9},{9,5},{13,17},{1... | collective-permute-start | bytes 847880 | tf_op jit(solution)/shard_map/ppermute | solution.py:529
  35.8 4.4 %collective-permute-start.7 = (f32[552,128]{1,0:T(8,128)S(1)}, f32[552,128]{1,0:T(8,128)S(1)}, u32[]{:S(2)}, u32[]{:S(2)}) collective-permute-start(f32[552,128]{1,0:T(8,128)S(1)} %get-tuple-element.50), channel_id=1, source_target_pairs={{0,4},{4,0},{8,12},{12,8},{16,20},{20,16},{24,28},{28,24},{1,5},{5... | collective-permute-start | bytes 847880 | tf_op jit(solution)/shard_map/ppermute | solution.py:530
